TPU v7x, 32 devices: a whole 2x2x4 slice. The times are simulated.
32 devices in a mesh: tm: 8 (over y, x, core), space: 4 (over z).
Axes of the slice: x: 2, y: 2, z: 4, core: 2. Of those that a mesh axis runs over, the one named last changes fastest.
Arguments:
- frames_in: bfloat16 [64, 32, 64, 256], P('tm', 'space'), may hold values from -6 to 6
- cotangent: bfloat16 [64, 32, 64, 256], P('tm', 'space'), may hold values from -6 to 6
- spatial: bfloat16 [3, 3, 256, 256], replicated, may hold values from -0.125 to 0.125
- temporal: bfloat16 [3, 256, 256], replicated, may hold values from -0.375 to 0.375
- norm_gain: float32 [256], replicated, may hold values from 0.5 to 2
- norm_shift: float32 [256], replicated, may hold values from -3 to 3
- clip_frames: int32 [2], replicated, may hold values from 8 to 48, as said below
- dilation: int32 [2], replicated, may hold values from 1 to 8, as said below
Outputs:
- out_frames: bfloat16 [64, 32, 64, 256], P('tm', 'space')
- in_grad: bfloat16 [64, 32, 64, 256], P('tm', 'space')
- spatial_grad: float32 [3, 3, 256, 256], replicated
- temporal_grad: float32 [3, 256, 256], replicated
Inputs may be any that keep to these rules, and one draw needn't show every extreme that they name: `clip_frames`: the two clips are packed in order from slot 0 and fill at least 56 and at most 64 slots together; one of them has exactly 48 frames. One of the two clips has dilation 8.
All inputs are finite; a program needn't handle non-finite values.
Results may differ from a plain program's by a relative error of at most 0.0055.
Values may be sent and summed in bfloat16 or wider, within the bound.
No kernel may reach another device: no remote copies, remote signals or barrier semaphores. Data moves between devices by JAX's collectives and lax.ppermute only.
A program may use at most 128 MiB of HBM per device.

v0:
```python
import jax
import jax.numpy as jnp
from jax import lax
from jax.sharding import PartitionSpec as P

GROUPS = 32
DMAX = 8


NORM_EPS = 1e-05


def extended(x, sides, width):
    for axis, dim in sides:
        size, length = (lax.axis_size(axis), x.shape[dim])
        up = [(i, (i + 1) % size) for i in range(size - 1)]
        down = [(j, i) for i, j in up]
        last = lax.slice_in_dim(x, length - width, length, axis=dim)
        initial = lax.slice_in_dim(x, 0, width, axis=dim)
        before = lax.ppermute(last, axis, up)
        after = lax.ppermute(initial, axis, down)
        x = jnp.concatenate([before, x, after], axis=dim)
    return x


def slot_tables(frame_ids, clip_frames):
    filled = clip_frames[0] + clip_frames[1]
    usable = (frame_ids >= 0) & (frame_ids < filled)
    clip_ids = (frame_ids >= clip_frames[0]).astype(jnp.int32)
    return (usable, clip_ids)


def shifted_pieces(source, first_frame, out_first, frame_count, clip_frames, dilation, direction):
    frame_ids = out_first + jnp.arange(frame_count, dtype=jnp.int32)
    usable, clip_ids = slot_tables(frame_ids, clip_frames)
    results = []
    for tap_index in range(3):
        combined = jnp.zeros((frame_count,) + source.shape[1:], source.dtype)
        for which_clip in range(2):
            offset_val = direction * (tap_index - 1) * dilation[which_clip]
            target_ok, target_clip = slot_tables(frame_ids + offset_val, clip_frames)
            keep_mask = usable & target_ok & (clip_ids == which_clip) & (target_clip == which_clip)
            start_row = out_first + offset_val - first_frame
            shifted = lax.dynamic_slice_in_dim(source, start_row, frame_count, 0)
            combined = jnp.where(keep_mask[:, None, None], shifted, combined)
        results.append(combined)
    return results


def time_forward(act_src, first_frame, out_first, frame_count, clip_frames, dilation, temporal):
    pieces = shifted_pieces(act_src, first_frame, out_first, frame_count, clip_frames, dilation, 1)
    summed = jnp.zeros(pieces[0].shape, jnp.float32)
    for tap_index in range(3):
        summed = summed + jnp.dot(
            pieces[tap_index], temporal[tap_index], preferred_element_type=jnp.float32
        )
    return summed.astype(jnp.bfloat16)


def time_backward(
    act_src, grad_src, first_frame, out_first, frame_count, clip_frames, dilation, temporal
):
    pieces_act = shifted_pieces(
        act_src, first_frame, out_first, frame_count, clip_frames, dilation, 1
    )
    pieces_grad = shifted_pieces(
        grad_src, first_frame, out_first, frame_count, clip_frames, dilation, -1
    )
    channels = grad_src.shape[-1]
    own_grad = lax.dynamic_slice_in_dim(grad_src, out_first - first_frame, frame_count, 0)
    flat_grad = own_grad.reshape(-1, channels)
    back_sum = jnp.zeros(pieces_grad[0].shape, jnp.float32)
    weight_terms = []
    for tap_index in range(3):
        back_sum = back_sum + lax.dot_general(
            pieces_grad[tap_index],
            temporal[tap_index],
            (((2,), (1,)), ((), ())),
            preferred_element_type=jnp.float32,
        )
        weight_terms.append(
            lax.dot_general(
                pieces_act[tap_index].reshape(-1, channels),
                flat_grad,
                (((0,), (0,)), ((), ())),
                preferred_element_type=jnp.float32,
            )
        )
    return (back_sum.astype(jnp.bfloat16), jnp.stack(weight_terms))


def widen(padded):
    return jnp.pad(padded, ((0, 0), (0, 0), (1, 1), (0, 0)))


def spatial_forward(padded, spatial):
    row_count = padded.shape[1] - 2
    col_count = padded.shape[2]
    wide = widen(padded)
    summed = jnp.zeros((padded.shape[0], row_count, col_count, spatial.shape[3]), jnp.float32)
    for offset_row in range(3):
        for offset_col in range(3):
            window = wide[
                :, offset_row : offset_row + row_count, offset_col : offset_col + col_count, :
            ]
            summed = summed + jnp.dot(
                window, spatial[offset_row, offset_col], preferred_element_type=jnp.float32
            )
    return summed


def spatial_backward(padded, spatial):
    row_count = padded.shape[1] - 2
    col_count = padded.shape[2]
    wide = widen(padded)
    summed = jnp.zeros((padded.shape[0], row_count, col_count, spatial.shape[2]), jnp.float32)
    for offset_row in range(3):
        for offset_col in range(3):
            window = wide[
                :,
                2 - offset_row : 2 - offset_row + row_count,
                2 - offset_col : 2 - offset_col + col_count,
                :,
            ]
            summed = summed + lax.dot_general(
                window,
                spatial[offset_row, offset_col],
                (((3,), (1,)), ((), ())),
                preferred_element_type=jnp.float32,
            )
    return summed


def weight_grad(padded, grad_conv):
    row_count = padded.shape[1] - 2
    col_count = padded.shape[2]
    channels = grad_conv.shape[-1]
    wide = widen(padded)
    flat_grad = grad_conv.reshape(-1, channels)
    outer_rows = []
    for offset_row in range(3):
        inner_cols = []
        for offset_col in range(3):
            window = wide[
                :, offset_row : offset_row + row_count, offset_col : offset_col + col_count, :
            ]
            inner_cols.append(
                lax.dot_general(
                    window.reshape(-1, window.shape[-1]),
                    flat_grad,
                    (((0,), (0,)), ((), ())),
                    preferred_element_type=jnp.float32,
                )
            )
        outer_rows.append(jnp.stack(inner_cols))
    return jnp.stack(outer_rows)


def group_fold(values):
    return values.reshape(values.shape[0], GROUPS, -1).sum(axis=2)


def spread_groups(values, group_size):
    return jnp.repeat(values, group_size, axis=-1)[:, None, None, :]


def normalize(conv_out, sum_first, sum_second, norm_gain, norm_shift, entries):
    group_size = conv_out.shape[-1] // GROUPS
    mean_val = sum_first / entries
    variance = sum_second / entries - mean_val * mean_val
    inv_std = lax.rsqrt(variance + NORM_EPS)
    inv_wide = spread_groups(inv_std, group_size)
    normed = (conv_out - spread_groups(mean_val, group_size)) * inv_wide
    shaped = normed * norm_gain + norm_shift
    return (normed, shaped, inv_wide)


def gradient_normed(grad_act, shaped, norm_gain):
    sigmoid_val = jax.nn.sigmoid(shaped)
    return (
        grad_act.astype(jnp.float32)
        * sigmoid_val
        * (1.0 + shaped * (1.0 - sigmoid_val))
        * norm_gain
    )


def norm_backward(grad_normed, normed, inv_wide, mean_first, mean_second):
    group_size = grad_normed.shape[-1] // GROUPS
    result = inv_wide * (
        grad_normed
        - spread_groups(mean_first, group_size)
        - normed * spread_groups(mean_second, group_size)
    )
    return result.astype(jnp.bfloat16)


def per_device(
    frames_in, cotangent, spatial, temporal, norm_gain, norm_shift, clip_frames, dilation
):
    slot_local, row_count, col_count, channels = frames_in.shape
    pixels = row_count * col_count
    entries = row_count * lax.axis_size("space") * col_count * (channels // GROUPS)
    tm_index = lax.axis_index("tm")
    padded = extended(frames_in, (("space", 1),), 1)
    conv_out = spatial_forward(padded, spatial)
    sum_first, sum_second = lax.psum(
        (
            group_fold(jnp.sum(conv_out, axis=(1, 2))),
            group_fold(jnp.sum(conv_out * conv_out, axis=(1, 2))),
        ),
        "space",
    )
    normed, shaped, inv_wide = normalize(
        conv_out, sum_first, sum_second, norm_gain, norm_shift, entries
    )
    frame_ids = tm_index * slot_local + jnp.arange(slot_local, dtype=jnp.int32)
    usable, clip_ids = slot_tables(frame_ids, clip_frames)
    activation = jnp.where(usable[:, None, None, None], jax.nn.silu(shaped), 0.0).astype(
        jnp.bfloat16
    )
    activation = activation.reshape(slot_local, pixels, channels)
    grad_rows = cotangent.reshape(slot_local, pixels, channels)
    pad_spec = ((DMAX, DMAX), (0, 0), (0, 0))
    act_tiles = lax.all_to_all(activation, "tm", split_axis=1, concat_axis=0, tiled=True)
    act_src = jnp.pad(act_tiles, pad_spec)
    frame_total = act_tiles.shape[0]
    out_tiles = time_forward(act_src, -DMAX, 0, frame_total, clip_frames, dilation, temporal)
    temporal_out = lax.all_to_all(out_tiles, "tm", split_axis=0, concat_axis=1, tiled=True)
    grad_tiles = lax.all_to_all(grad_rows, "tm", split_axis=1, concat_axis=0, tiled=True)
    back_tiles, temporal_part = time_backward(
        act_src,
        jnp.pad(grad_tiles, pad_spec),
        -DMAX,
        0,
        frame_total,
        clip_frames,
        dilation,
        temporal,
    )
    grad_act = lax.all_to_all(back_tiles, "tm", split_axis=0, concat_axis=1, tiled=True)
    out_frames = (
        frames_in.astype(jnp.float32) + temporal_out.reshape(frames_in.shape).astype(jnp.float32)
    ).astype(jnp.bfloat16)
    grad_normed = gradient_normed(grad_act.reshape(frames_in.shape), shaped, norm_gain)
    mean_first, mean_second = lax.psum(
        (
            group_fold(jnp.sum(grad_normed, axis=(1, 2))),
            group_fold(jnp.sum(grad_normed * normed, axis=(1, 2))),
        ),
        "space",
    )
    grad_conv = norm_backward(
        grad_normed, normed, inv_wide, mean_first / entries, mean_second / entries
    )
    conv_pad = extended(grad_conv, (("space", 1),), 1)
    in_grad = (cotangent.astype(jnp.float32) + spatial_backward(conv_pad, spatial)).astype(
        jnp.bfloat16
    )
    spatial_part = weight_grad(padded, grad_conv)
    spatial_grad, temporal_grad = lax.psum((spatial_part, temporal_part), ("tm", "space"))
    return (out_frames, in_grad, spatial_grad, temporal_grad)


def solution(mesh):
    placed = (
        P("tm", "space", None, None),
        P("tm", "space", None, None),
        P(),
        P(),
        P(),
        P(),
        P(),
        P(),
    )
    return jax.shard_map(
        per_device,
        mesh=mesh,
        in_specs=placed,
        out_specs=(P("tm", "space", None, None), P("tm", "space", None, None), P(), P()),
        check_vma=False,
    )
```

profile of v0, /device:TPU:0, one launch (start us, length us, event | category | flops | bytes accessed | tf_op | source)
XLA Modules:
  0.0 369.5 jit_solution(1602154628930145497)
XLA Ops:
  7.2 1.1 fusion.164
  8.2 4.9 %collective-permute-start = (bf16[8,1,64,256]{3,2,1,0:T(8,128)(2,1)S(1)}, bf16[8,1,64,256]{3,2,1,0:T(8,128)(2,1)S(1)}, u32[]{:S(2)}, u32[]{:S(2)}) collective-permute-start(bf16[8,1,64,256]{3,2,1,0:T(8,128)(2,1)S(1)} %get-tuple-element.22), channel_id=1, source_target_pairs={{0,1},{1,2},{2,3},{4,5},{5,6},{6,7},{8,9},{9,10},{10,11},{12,13},{... | collective-permute-start | bytes 786440 | tf_op jit(solution)/shard_map/ppermute | solution.py:20
  13.2 1.3 collective-permute-start.1
  14.5 4.2 %copy.23 = bf16[8,8,64,256]{3,0,2,1:T(8,128)(2,1)} copy(bf16[8,8,64,256]{3,2,1,0:T(8,128)(2,1)} %param.9) | data formatting | bytes 4194304 | tf_op args[1]
  18.7 4.5 %all-to-all-start.2 = ((bf16[8,512,256]{2,0,1:T(8,128)(2,1)}), bf16[8,512,256]{2,0,1:T(8,128)(2,1)}, u32[]{:S(2)}, u32[]{:S(2)}) async-start(bf16[8,512,256]{2,0,1:T(8,128)(2,1)} %bitcast.241), calls=%async_computation.2 | async-start | bytes 4194304 | tf_op jit(solution)/shard_map/all_to_all | solution.py:230
  28.1 1.9 compare_and_fusion
  32.6 3.8 %fusion.106 = f32[8,8,64,256]{3,2,1,0:T(8,128)} fusion(bf16[8,8,64,256]{3,2,1,0:T(8,128)(2,1)S(1)} %copy-done.2, bf16[3,3,256,256]{3,2,1,0:T(8,128)(2,1)} %param.10), kind=kOutput, calls=%fused_computation.123 | convolution fusion | flops 536870912 | bytes 6422528 | tf_op jit(solution)/shard_map/dot_general | solution.py:106
  36.4 1.6 select_maximum_fusion.2
  38.0 2.8 fusion.54
  41.4 3.1 fusion.58
  44.5 2.8 fusion.62
  47.2 2.8 fusion.66
  50.0 2.8 fusion.98
  52.8 2.7 fusion.113
  55.5 2.1 copy.25
  57.6 2.9 select_select_fusion
  62.1 2.4 add_convert_fusion.1
  64.5 14.6 %all-to-all-start.3 = ((bf16[64,64,256]{2,1,0:T(8,128)(2,1)}), bf16[64,64,256]{2,1,0:T(8,128)(2,1)}, u32[]{:S(2)}, u32[]{:S(2)}) async-start(bf16[64,64,256]{2,1,0:T(8,128)(2,1)} %add_convert_fusion.1), calls=%async_computation.3 | async-start | bytes 4194304 | tf_op jit(solution)/shard_map/all_to_all | solution.py:241
  79.1 1.8 fusion.70
  81.3 11.5 %fusion.161 = (f32[8,256]{1,0:T(8,128)S(1)}, f32[8,256]{1,0:T(8,128)S(1)}, f32[8,8,64,256]{3,2,1,0:T(8,128)}) fusion(bf16[3,3,256,256]{3,2,1,0:T(8,128)(2,1)} %param.10, bf16[8,10,66,256]{3,2,1,0:T(8,128)(2,1)S(1)} %select_maximum_fusion.2, f32[8,8,64,256]{3,2,1,0:T(8,128)} %fusion.98, f32[8,8,64,256]{3,2,1,0:T(8,128)} %fusion.54, ...), kind=kOutput, calls=%fused_computation.202 | convolution fusion | flops 548401152 | bytes 39993344 | tf_op jit(solution)/shard_map/dot_general | solution.py:106
  93.8 1.0 reduce_sum.75
  94.8 13.2 %all-reduce.6 = (f32[8,32]{1,0:T(8,128)S(1)}, f32[8,32]{1,0:T(8,128)S(1)}) all-reduce(f32[8,32]{1,0:T(8,128)S(1)} %reduce_sum.75, f32[8,32]{1,0:T(8,128)S(1)} %reduce_sum.73), channel_id=1, replica_groups=mesh['tm'=8,'space'=4] {'space'}, use_global_device_ids=true, to_apply=%region_5.6 | all-reduce | flops 512 | bytes 4096 | tf_op jit(solution)/shard_map/psum | solution.py:207
  108.5 2.3 bitcast_convert_fusion
  111.3 4.4 %fusion.160 = (f32[8,256]{1,0:T(8,128)S(1)}, f32[8,256]{1,0:T(8,128)S(1)}, f32[8,8,64,256]{3,2,1,0:T(8,128)}, bf16[8,8,64,256]{3,2,1,0:T(8,128)(2,1)}) fusion(f32[8,256]{1,0:T(8,128)S(1)} %mul.79, f32[8,8,64,256]{3,2,1,0:T(8,128)S(1)} %copy-done.5, f32[8,256]{1,0:T(8,128)S(1)} %sub.49, f32[256]{0:T(256)S(1)} %copy-done.33, f32[256]{0:T(256)S(1)} %copy-done.34, ...), kind=kLoop, calls=%fused_computation.201 | loop fusion | flops 19918848 | bytes 14714888 | tf_op jit(solution)/shard_map/reduce_sum | solution.py:248
  116.1 10.4 %all-reduce.5 = (f32[8,32]{1,0:T(8,128)S(1)}, f32[8,32]{1,0:T(8,128)S(1)}) all-reduce(f32[8,32]{1,0:T(8,128)S(1)} %reduce_sum.79, f32[8,32]{1,0:T(8,128)S(1)} %reduce_sum.77), channel_id=1, replica_groups=mesh['tm'=8,'space'=4] {'space'}, use_global_device_ids=true, to_apply=%region_11.12 | all-reduce | flops 512 | bytes 4096 | tf_op jit(solution)/shard_map/psum | solution.py:246
  127.0 4.8 %multiply_convert_fusion = bf16[8,8,64,256]{3,2,1,0:T(8,128)(2,1)S(1)} fusion(f32[8,8,64,256]{3,2,1,0:T(8,128)} %get-tuple-element.14, f32[8,8,64,256]{3,2,1,0:T(8,128)} %get-tuple-element.30, f32[8,256]{1,0:T(8,128)S(1)} %mul.91, f32[8,256]{1,0:T(8,128)S(1)} %sub.58, f32[8,256]{1,0:T(8,128)S(1)} %mul.79, f32[8,256]{1,0:T(8,128)S(1)} %sub.49), kind=kLoop, calls=%fused_computation.9 | loop fusion | flops 7340032 | bytes 10518528 | tf_op jit(solution)/shard_map/convert_element_type | solution.py:195
  131.8 1.4 convolution_bitcast_fusion.1
  133.3 1.5 fusion.72
  134.8 1.5 fusion.75
  136.3 1.5 fusion.78
  137.7 1.5 fusion.81
  139.3 1.7 convolution_bitcast_fusion.4
  141.0 1.5 convolution_bitcast_fusion
  142.5 1.5 fusion.84
  143.9 1.5 fusion.87
  145.5 3.8 %fusion.104 = f32[8,8,64,256]{3,2,1,0:T(8,128)} fusion(bf16[8,8,64,256]{3,2,1,0:T(8,128)(2,1)S(1)} %multiply_convert_fusion, bf16[3,3,256,256]{3,2,1,0:T(8,128)(2,1)} %param.10), kind=kOutput, calls=%fused_computation.121 | convolution fusion | flops 536870912 | bytes 6422528 | tf_op jit(solution)/shard_map/dot_general | solution.py:125
  149.3 2.5 copy.19
  151.8 4.5 %all-to-all-start = ((bf16[8,512,256]{2,0,1:T(8,128)(2,1)}), bf16[8,512,256]{2,0,1:T(8,128)(2,1)}, u32[]{:S(2)}, u32[]{:S(2)}) async-start(bf16[8,512,256]{2,0,1:T(8,128)(2,1)} %copy.19), calls=%async_computation | async-start | bytes 4194304 | tf_op jit(solution)/shard_map/all_to_all | solution.py:225
  156.4 1.4 collective-permute-start.3
  157.8 4.7 %collective-permute-start.2 = (bf16[8,1,64,256]{3,2,1,0:T(8,128)(2,1)S(1)}, bf16[8,1,64,256]{3,2,1,0:T(8,128)(2,1)S(1)}, u32[]{:S(2)}, u32[]{:S(2)}) collective-permute-start(bf16[8,1,64,256]{3,2,1,0:T(8,128)(2,1)S(1)} %get-tuple-element.17), channel_id=1, source_target_pairs={{0,1},{1,2},{2,3},{4,5},{5,6},{6,7},{8,9},{9,10},{10,11},{12,13},{... | collective-permute-start | bytes 786440 | tf_op jit(solution)/shard_map/ppermute | solution.py:20
  162.8 1.6 pad_maximum_fusion
  164.4 2.6 collective-permute-done.3
  167.0 1.2 collective-permute-done.2
  168.1 1.6 select_maximum_fusion
  169.7 2.7 fusion.30
  172.4 2.8 fusion.5
  175.2 2.7 fusion.9
  178.0 2.7 fusion.32
  180.7 2.8 fusion.34
  183.5 2.7 fusion.36
  186.2 2.7 fusion.38
  188.9 2.1 copy.21
  191.1 2.1 select_select_fusion.1
  193.2 1.4 fusion.15
  194.6 4.5 %fusion.90 = f32[1,256,256]{2,1,0:T(8,128)} fusion(bf16[8,8,64,256]{3,2,1,0:T(8,128)(2,1)S(1)} %select_select_fusion.1, bf16[8,8,64,256]{3,0,2,1:T(8,128)(2,1)} %bitcast.45), kind=kOutput, calls=%fused_computation.100 | convolution fusion | flops 536870912 | bytes 4456448 | tf_op jit(solution)/shard_map/dot_general | solution.py:82
  200.6 2.0 add_convert_fusion.2
  202.6 4.3 %all-to-all-start.1 = ((bf16[64,64,256]{2,1,0:T(8,128)(2,1)}), bf16[64,64,256]{2,1,0:T(8,128)(2,1)}, u32[]{:S(2)}, u32[]{:S(2)}) async-start(bf16[64,64,256]{2,1,0:T(8,128)(2,1)} %add_convert_fusion.2), calls=%async_computation.1 | async-start | bytes 4194304 | tf_op jit(solution)/shard_map/all_to_all | solution.py:229
  207.3 3.1 convolution_bitcast_fusion.2
  211.7 0.9 pad_maximum_fusion.1
  212.6 14.1 %add_convert_fusion = bf16[8,8,64,256]{3,2,1,0:T(8,128)(2,1)} fusion(f32[8,8,64,256]{3,2,1,0:T(8,128)} %fusion.9, f32[8,8,64,256]{3,2,1,0:T(8,128)} %fusion.30, f32[8,8,64,256]{3,2,1,0:T(8,128)} %fusion.32, f32[8,8,64,256]{3,2,1,0:T(8,128)} %fusion.104, f32[8,8,64,256]{3,2,1,0:T(8,128)} %fusion.34, f32[8,8,64,256]{3,2,1,0:T(8,128)} %fusion.36, ...), kind=kOutput, calls=%fused_computation.8 | convolution fusion | flops 548405248 | bytes 39976960 | tf_op jit(solution)/shard_map/dot_general | solution.py:125
  226.7 11.2 %all-to-all-done.1 = bf16[64,64,256]{2,1,0:T(8,128)(2,1)} async-done(((bf16[64,64,256]{2,1,0:T(8,128)(2,1)}), bf16[64,64,256]{2,1,0:T(8,128)(2,1)}, u32[]{:S(2)}, u32[]{:S(2)}) %all-to-all-start.1) | async-done | bytes 2097184 | tf_op jit(solution)/shard_map/all_to_all | solution.py:229
  237.9 4.5 %fusion.3 = bf16[8,8,64,256]{3,2,1,0:T(8,128)(2,1)} fusion(bf16[8,8,64,256]{3,2,1,0:T(8,128)(2,1)} %param.8, bf16[8,8,64,256]{3,2,1,0:T(8,128)(2,1)} %bitcast.109), kind=kLoop, calls=%fused_computation.7 | loop fusion | flops 4194304 | bytes 6291456 | tf_op jit(solution)/shard_map/convert_element_type | solution.py:244
  242.4 115.6 %all-reduce.9.cloned.1.call-done = (f32[3,3,256,256]{3,2,1,0:T(8,128)}, f32[3,256,256]{2,1,0:T(8,128)}) async-done(((f32[3,3,256,256]{3,2,1,0:T(8,128)}, f32[3,256,256]{2,1,0:T(8,128)}), (f32[3,3,256,256]{3,2,1,0:T(8,128)}, f32[3,256,256]{2,1,0:T(8,128)})) %all-reduce.9.cloned.1.call-update) | async-done | bytes 3145744 | tf_op jit(solution)/shard_map/psum | solution.py:261
  358.0 3.3 copy.65
  (113 shorter events, 11.9 us)
Async XLA Ops:
  8.2 28.1 %collective-permute-start = (bf16[8,1,64,256]{3,2,1,0:T(8,128)(2,1)S(1)}, bf16[8,1,64,256]{3,2,1,0:T(8,128)(2,1)S(1)}, u32[]{:S(2)}, u32[]{:S(2)}) collective-permute-start(bf16[8,1,64,256]{3,2,1,0:T(8,128)(2,1)S(1)} %get-tuple-element.22), channel_id=1, source_target_pairs={{0,1},{1,2},{2,3},{4,5},{5,6},{6,7},{8,9},{9,10},{10,11},{12,13},{... | collective-permute-start | bytes 786440 | tf_op jit(solution)/shard_map/ppermute | solution.py:20
  13.2 23.2 %collective-permute-start.1 = (bf16[8,1,64,256]{3,2,1,0:T(8,128)(2,1)S(1)}, bf16[8,1,64,256]{3,2,1,0:T(8,128)(2,1)S(1)}, u32[]{:S(2)}, u32[]{:S(2)}) collective-permute-start(bf16[8,1,64,256]{3,2,1,0:T(8,128)(2,1)S(1)} %get-tuple-element.23), channel_id=1, source_target_pairs={{1,0},{2,1},{3,2},{5,4},{6,5},{7,6},{9,8},{10,9},{11,10},{13,12},{... | collective-permute-start | bytes 786440 | tf_op jit(solution)/shard_map/ppermute | solution.py:21
  18.7 4.5 %copy-start.31 = (s32[2]{0:T(128)S(1)}, s32[2]{0:T(128)}, u32[]{:S(2)}) copy-start(s32[2]{0:T(128)} %param.15) | copy-start | bytes 28
  18.7 7.7 %copy-start.32 = (s32[2]{0:T(128)S(1)}, s32[2]{0:T(128)}, u32[]{:S(2)}) copy-start(s32[2]{0:T(128)} %param.14) | copy-start | bytes 28
  18.7 13.9 %copy-start.2 = (bf16[8,8,64,256]{3,2,1,0:T(8,128)(2,1)S(1)}, bf16[8,8,64,256]{3,2,1,0:T(8,128)(2,1)}, u32[]{:S(2)}) copy-start(bf16[8,8,64,256]{3,2,1,0:T(8,128)(2,1)} %param.8) | copy-start | bytes 6291460
  18.7 36.8 %all-to-all-start.2 = ((bf16[8,512,256]{2,0,1:T(8,128)(2,1)}), bf16[8,512,256]{2,0,1:T(8,128)(2,1)}, u32[]{:S(2)}, u32[]{:S(2)}) async-start(bf16[8,512,256]{2,0,1:T(8,128)(2,1)} %bitcast.241), calls=%async_computation.2 | async-start | bytes 4194304 | tf_op jit(solution)/shard_map/all_to_all | solution.py:230
  32.5 3.9 %copy-start.3 = (bf16[8,8,64,256]{3,2,1,0:T(8,128)(2,1)S(1)}, bf16[8,8,64,256]{3,2,1,0:T(8,128)(2,1)}, u32[]{:S(2)}) copy-start(bf16[8,8,64,256]{3,2,1,0:T(8,128)(2,1)} %param.8) | copy-start | bytes 6291460
  36.4 1.6 copy-start.15
  41.3 11.5 %copy-start.17 = (bf16[8,9,64,256]{3,2,1,0:T(8,128)(2,1)}, bf16[8,9,64,256]{3,2,1,0:T(8,128)(2,1)S(1)}, u32[]{:S(2)}) copy-start(bf16[8,9,64,256]{3,2,1,0:T(8,128)(2,1)S(1)} %get-tuple-element.20) | copy-start | bytes 7077892
  41.4 8.7 %copy-start.7 = (bf16[8,9,64,256]{3,2,1,0:T(8,128)(2,1)}, bf16[8,9,64,256]{3,2,1,0:T(8,128)(2,1)S(1)}, u32[]{:S(2)}) copy-start(bf16[8,9,64,256]{3,2,1,0:T(8,128)(2,1)S(1)} %constant_dynamic-update-slice_fusion.2) | copy-start | bytes 7077892
  57.6 4.4 %copy-start.13 = (bf16[8,8,64,256]{3,2,0,1:T(8,128)(2,1)}, bf16[8,8,64,256]{3,2,0,1:T(8,128)(2,1)S(1)}, u32[]{:S(2)}) copy-start(bf16[8,8,64,256]{3,2,0,1:T(8,128)(2,1)S(1)} %copy.25) | copy-start | bytes 6291460
  57.6 2.9 copy-start.19
  64.5 44.0 %all-to-all-start.3 = ((bf16[64,64,256]{2,1,0:T(8,128)(2,1)}), bf16[64,64,256]{2,1,0:T(8,128)(2,1)}, u32[]{:S(2)}, u32[]{:S(2)}) async-start(bf16[64,64,256]{2,1,0:T(8,128)(2,1)} %add_convert_fusion.1), calls=%async_computation.3 | async-start | bytes 4194304 | tf_op jit(solution)/shard_map/all_to_all | solution.py:241
  79.0 2.3 copy-start.6
  108.4 2.3 copy-start.33
  108.4 2.3 copy-start.34
  108.5 2.8 copy-start.5
  127.0 4.9 %copy-start.18 = (bf16[8,9,64,256]{3,2,1,0:T(8,128)(2,1)S(1)}, bf16[8,9,64,256]{3,2,1,0:T(8,128)(2,1)}, u32[]{:S(2)}) copy-start(bf16[8,9,64,256]{3,2,1,0:T(8,128)(2,1)} %copy-done.17) | copy-start | bytes 7077892
  131.8 13.6 %copy-start = (bf16[8,8,64,256]{3,2,1,0:T(8,128)(2,1)}, bf16[8,8,64,256]{3,2,1,0:T(8,128)(2,1)S(1)}, u32[]{:S(2)}) copy-start(bf16[8,8,64,256]{3,2,1,0:T(8,128)(2,1)S(1)} %multiply_convert_fusion) | copy-start | bytes 6291460
  137.7 1.6 copy-start.4
  139.3 1.7 copy-start.8
  145.4 3.8 %copy-start.9 = (bf16[8,8,64,256]{3,2,1,0:T(8,128)(2,1)S(1)}, bf16[8,8,64,256]{3,2,1,0:T(8,128)(2,1)}, u32[]{:S(2)}) copy-start(bf16[8,8,64,256]{3,2,1,0:T(8,128)(2,1)} %get-tuple-element.15) | copy-start | bytes 6291460
  151.8 10.8 %copy-start.22 = (f32[1,256,256]{2,1,0:T(8,128)S(1)}, f32[1,256,256]{2,1,0:T(8,128)}, u32[]{:S(2)}) copy-start(f32[1,256,256]{2,1,0:T(8,128)} %convolution_bitcast_fusion.1) | copy-start | bytes 786436
  151.8 10.8 %copy-start.28 = (f32[1,256,256]{2,1,0:T(8,128)S(1)}, f32[1,256,256]{2,1,0:T(8,128)}, u32[]{:S(2)}) copy-start(f32[1,256,256]{2,1,0:T(8,128)} %fusion.72) | copy-start | bytes 786436
  151.8 10.8 %copy-start.29 = (f32[1,256,256]{2,1,0:T(8,128)S(1)}, f32[1,256,256]{2,1,0:T(8,128)}, u32[]{:S(2)}) copy-start(f32[1,256,256]{2,1,0:T(8,128)} %fusion.75) | copy-start | bytes 786436
  151.8 10.8 %copy-start.23 = (f32[1,256,256]{2,1,0:T(8,128)S(1)}, f32[1,256,256]{2,1,0:T(8,128)}, u32[]{:S(2)}) copy-start(f32[1,256,256]{2,1,0:T(8,128)} %fusion.78) | copy-start | bytes 786436
  151.8 10.8 %copy-start.24 = (f32[1,256,256]{2,1,0:T(8,128)S(1)}, f32[1,256,256]{2,1,0:T(8,128)}, u32[]{:S(2)}) copy-start(f32[1,256,256]{2,1,0:T(8,128)} %fusion.81) | copy-start | bytes 786436
  151.8 10.8 %copy-start.25 = (f32[1,256,256]{2,1,0:T(8,128)S(1)}, f32[1,256,256]{2,1,0:T(8,128)}, u32[]{:S(2)}) copy-start(f32[1,256,256]{2,1,0:T(8,128)} %convolution_bitcast_fusion.4) | copy-start | bytes 786436
  151.8 37.1 %all-to-all-start = ((bf16[8,512,256]{2,0,1:T(8,128)(2,1)}), bf16[8,512,256]{2,0,1:T(8,128)(2,1)}, u32[]{:S(2)}, u32[]{:S(2)}) async-start(bf16[8,512,256]{2,0,1:T(8,128)(2,1)} %copy.19), calls=%async_computation | async-start | bytes 4194304 | tf_op jit(solution)/shard_map/all_to_all | solution.py:225
  156.3 6.4 %copy-start.21 = (f32[1,256,256]{2,1,0:T(8,128)S(1)}, f32[1,256,256]{2,1,0:T(8,128)}, u32[]{:S(2)}) copy-start(f32[1,256,256]{2,1,0:T(8,128)} %convolution_bitcast_fusion) | copy-start | bytes 786436
  156.3 6.4 %copy-start.26 = (f32[1,256,256]{2,1,0:T(8,128)S(1)}, f32[1,256,256]{2,1,0:T(8,128)}, u32[]{:S(2)}) copy-start(f32[1,256,256]{2,1,0:T(8,128)} %fusion.84) | copy-start | bytes 786436
  156.3 6.4 %copy-start.27 = (f32[1,256,256]{2,1,0:T(8,128)S(1)}, f32[1,256,256]{2,1,0:T(8,128)}, u32[]{:S(2)}) copy-start(f32[1,256,256]{2,1,0:T(8,128)} %fusion.87) | copy-start | bytes 786436
  156.4 10.6 %collective-permute-start.3 = (bf16[8,1,64,256]{3,2,1,0:T(8,128)(2,1)S(1)}, bf16[8,1,64,256]{3,2,1,0:T(8,128)(2,1)S(1)}, u32[]{:S(2)}, u32[]{:S(2)}) collective-permute-start(bf16[8,1,64,256]{3,2,1,0:T(8,128)(2,1)S(1)} %get-tuple-element.16), channel_id=1, source_target_pairs={{1,0},{2,1},{3,2},{5,4},{6,5},{7,6},{9,8},{10,9},{11,10},{13,12},{... | collective-permute-start | bytes 786440 | tf_op jit(solution)/shard_map/ppermute | solution.py:21
  157.8 10.3 %collective-permute-start.2 = (bf16[8,1,64,256]{3,2,1,0:T(8,128)(2,1)S(1)}, bf16[8,1,64,256]{3,2,1,0:T(8,128)(2,1)S(1)}, u32[]{:S(2)}, u32[]{:S(2)}) collective-permute-start(bf16[8,1,64,256]{3,2,1,0:T(8,128)(2,1)S(1)} %get-tuple-element.17), channel_id=1, source_target_pairs={{0,1},{1,2},{2,3},{4,5},{5,6},{6,7},{8,9},{9,10},{10,11},{12,13},{... | collective-permute-start | bytes 786440 | tf_op jit(solution)/shard_map/ppermute | solution.py:20
  162.8 5.3 %copy-start.1 = (bf16[8,8,64,256]{3,2,1,0:T(8,128)(2,1)S(1)}, bf16[8,8,64,256]{3,2,1,0:T(8,128)(2,1)}, u32[]{:S(2)}) copy-start(bf16[8,8,64,256]{3,2,1,0:T(8,128)(2,1)} %copy-done) | copy-start | bytes 6291460
  164.4 5.3 %copy-start.16 = (bf16[3,3,256,256]{3,2,1,0:T(8,128)(2,1)S(1)}, bf16[3,3,256,256]{3,2,1,0:T(8,128)(2,1)}, u32[]{:S(2)}) copy-start(bf16[3,3,256,256]{3,2,1,0:T(8,128)(2,1)} %param.10) | copy-start | bytes 3538948
  194.6 4.6 %copy-start.10 = (bf16[64,64,256]{2,1,0:T(8,128)(2,1)}, bf16[64,64,256]{2,1,0:T(8,128)(2,1)S(1)}, u32[]{:S(2)}) copy-start(bf16[64,64,256]{2,1,0:T(8,128)(2,1)S(1)} %get-tuple-element.19) | copy-start | bytes 6291460
  194.6 6.0 %copy-start.12 = (bf16[64,64,256]{2,1,0:T(8,128)(2,1)}, bf16[64,64,256]{2,1,0:T(8,128)(2,1)S(1)}, u32[]{:S(2)}) copy-start(bf16[64,64,256]{2,1,0:T(8,128)(2,1)S(1)} %get-tuple-element.18) | copy-start | bytes 6291460
  202.6 35.3 %all-to-all-start.1 = ((bf16[64,64,256]{2,1,0:T(8,128)(2,1)}), bf16[64,64,256]{2,1,0:T(8,128)(2,1)}, u32[]{:S(2)}, u32[]{:S(2)}) async-start(bf16[64,64,256]{2,1,0:T(8,128)(2,1)} %add_convert_fusion.2), calls=%async_computation.1 | async-start | bytes 4194304 | tf_op jit(solution)/shard_map/all_to_all | solution.py:229
  206.9 151.1 %all-reduce.9.cloned.1.call-start = ((), (), s32[]{:S(2)}) async-start(), calls=%async_computation.4 | async-start | bytes 6291456 | tf_op jit(solution)/shard_map/psum | solution.py:261
  207.2 3.1 copy-start.11
  207.3 3.5 copy-start.14
  210.7 0.9 copy-start.30
  358.0 3.3 copy-start.20
Sparse Core Ops, SparseCore 0:
  214.0 143.9 all-reduce.8
where the time goes:
time: 373 us; the launch traced here: 369 us
  waiting for transfers between devices  131 us (35%)
  matrix products  100 us (27%)
  starting transfers between devices  40.6 us (11%)
  other arithmetic  32.5 us (9%)
  blocking collectives  23.6 us (6%)
  local copies, waits for them, and re-layouts  21.6 us (6%)
  between operations  20.4 us (5%)
    psum x1, waiting for transfers between devices, per_device(): lax.psum((spatial_part, temporal_part), ('tm', 'space'))  116 us
    dot_general x9, matrix products, spatial_backward(): lax.dot_general(window, spatial[offset_row, offset_col], (((3,), (1,)), (...  37.1 us
    dot_general x9, matrix products, spatial_forward(): jnp.dot(window, spatial[offset_row, offset_col], preferred_element_type=j...  34 us
    all_to_all x1, starting transfers between devices, per_device(): lax.all_to_all(back_tiles, 'tm', split_axis=0, concat_axis=1, tiled=True)  14.6 us
    dot_general x9, matrix products, weight_grad(): lax.dot_general(window.reshape(-1, window.shape[-1]), flat_grad, (((0,),...  13.4 us
    psum x1, blocking collectives, per_device(): lax.psum((group_fold(jnp.sum(conv_out, axis=(1, 2))), group_fold(jnp.sum(...  13.2 us
    all_to_all x1, waiting for transfers between devices, per_device(): lax.all_to_all(out_tiles, 'tm', split_axis=0, concat_axis=1, tiled=True)  11.2 us
    psum x1, blocking collectives, per_device(): lax.psum((group_fold(jnp.sum(grad_normed, axis=(1, 2))), group_fold(jnp.s...  10.4 us
  transfers between devices with their start and end apart: 9, of which 4 were waited for; matrix products, arithmetic and copies ran while one was open for 25% of the time, Pallas kernels for 0%

commit v1 on v0

v1 whole, which is shorter than its diff:
```python
import functools

import jax
import jax.numpy as jnp
from jax import lax
from jax.experimental import pallas as pl
from jax.experimental.pallas import tpu as pltpu
from jax.sharding import PartitionSpec as P

GROUPS = 32
NORM_EPS = 1e-05
BF16 = jnp.bfloat16
F32 = jnp.float32
VMEM_LIMIT = 48 * 2**20


def params():
    return pltpu.CompilerParams(
        vmem_limit_bytes=VMEM_LIMIT, dimension_semantics=("arbitrary",)
    )


def cost(flops, moved, exps=0):
    return pl.CostEstimate(flops=int(flops), bytes_accessed=int(moved), transcendentals=int(exps))


def dot(a, b):
    return jnp.dot(a, b, preferred_element_type=F32)


def dot_rows(a, b):
    return lax.dot_general(a, b, (((0,), (0,)), ((), ())), preferred_element_type=F32)


def group_total(row, group_size):
    channels = row.shape[-1]
    lane = lax.broadcasted_iota(jnp.int32, row.shape, 1)
    step = 1
    while step < group_size:
        up = pltpu.roll(row, channels - step, axis=1)
        down = pltpu.roll(row, step, axis=1)
        row = row + jnp.where((lane & step) == 0, up, down)
        step *= 2
    return row


def frame_stats(part_refs, entries, group_size):
    total = part_refs[0][0]
    for ref in part_refs[1:]:
        total = total + ref[0]
    return group_total(total, group_size) / entries


def mean_and_inv(part_refs, entries, group_size):
    both = frame_stats(part_refs, entries, group_size)
    mean = both[0:1]
    inv = lax.rsqrt(both[1:2] - mean * mean + NORM_EPS)
    return mean, inv


def column_sums(first, second, out_ref):
    out_ref[0, 0:1, :] = jnp.sum(first, axis=0, keepdims=True)
    out_ref[0, 1:2, :] = jnp.sum(second, axis=0, keepdims=True)


def with_halo(above_ref, mid, below_ref):
    width, channels = above_ref.shape[-2:]
    return jnp.concatenate(
        [above_ref[...].reshape(width, channels), mid, below_ref[...].reshape(width, channels)],
        axis=0,
    )


def from_left(y, width):
    col = lax.broadcasted_iota(jnp.int32, y.shape, 0) & (width - 1)
    return jnp.where(col == 0, 0.0, pltpu.roll(y, 1, axis=0))


def from_right(y, width):
    col = lax.broadcasted_iota(jnp.int32, y.shape, 0) & (width - 1)
    return jnp.where(col == width - 1, 0.0, pltpu.roll(y, y.shape[0] - 1, axis=0))


def conv_kernel(x_ref, above_ref, below_ref, w_ref, out_ref, sums_ref):
    _, rows, width, channels = x_ref.shape
    pixels = rows * width
    padded = with_halo(above_ref, x_ref[...].reshape(pixels, channels), below_ref)
    lhs = jnp.concatenate([padded[i * width : i * width + pixels] for i in range(3)], axis=1)
    y = [dot(lhs, w_ref[:, j].reshape(3 * channels, channels)) for j in range(3)]
    out = y[1] + from_left(y[0], width) + from_right(y[2], width)
    out_ref[0] = out
    column_sums(out, out * out, sums_ref)


def act_kernel(n, entries, group_size, info_ref, *refs):
    parts, (conv_ref, gain_ref, shift_ref, act_ref) = refs[:n], refs[n:]
    mean, inv = mean_and_inv(parts, entries, group_size)
    shaped = (conv_ref[0] - mean) * inv * gain_ref[...] + shift_ref[...]
    used = info_ref[pl.program_id(0), 6] > 0
    act_ref[0] = jnp.where(used, shaped * jax.nn.sigmoid(shaped), 0.0).astype(BF16)


def gather_taps(info_ref, own_up, nxt, mid, own_dn, prv, cat_ref, up_slot):
    frame = pl.program_id(0)
    channels = mid.shape[-1]
    dn_slot = 2 - up_slot

    def put(slot, ref):
        cat_ref[:, slot * channels : (slot + 1) * channels] = ref[0]

    def clear(slot):
        cat_ref[:, slot * channels : (slot + 1) * channels] = jnp.zeros(
            (cat_ref.shape[0], channels), cat_ref.dtype
        )

    for slot, which, own, other in ((up_slot, info_ref[frame, 2], own_up, nxt), (dn_slot, info_ref[frame, 5], own_dn, prv)):
        pl.when(which == 1)(functools.partial(put, slot, own))
        pl.when(which == 2)(functools.partial(put, slot, other))
        pl.when(which == 0)(functools.partial(clear, slot))
    used = info_ref[frame, 6]
    pl.when(used == 1)(functools.partial(put, 1, mid))
    pl.when(used == 0)(functools.partial(clear, 1))


def grad_act_kernel(
    n, entries, group_size, info_ref, own_up, nxt, mid, own_dn, prv, tw_ref, conv_ref, gain_ref, shift_ref, *rest
):
    parts, (gn_ref, sums_ref, cat_ref) = rest[:n], rest[n:]
    gather_taps(info_ref, own_up, nxt, mid, own_dn, prv, cat_ref, 0)
    grad_act = dot(cat_ref[...], tw_ref[...]).astype(BF16).astype(F32)
    mean, inv = mean_and_inv(parts, entries, group_size)
    normed = (conv_ref[0] - mean) * inv
    shaped = normed * gain_ref[...] + shift_ref[...]
    sig = jax.nn.sigmoid(shaped)
    gn = grad_act * sig * (1.0 + shaped * (1.0 - sig)) * gain_ref[...]
    gn_ref[0] = gn
    column_sums(gn, gn * normed, sums_ref)


def temporal_grad_kernel(info_ref, own_up, nxt, mid, own_dn, prv, act_ref, out_ref, cat_ref):
    channels = act_ref.shape[-1]
    gather_taps(info_ref, own_up, nxt, mid, own_dn, prv, cat_ref, 0)
    part = dot_rows(act_ref[0], cat_ref[...])

    @pl.when(pl.program_id(0) == 0)
    def _():
        out_ref[...] = jnp.zeros_like(out_ref)

    for k in range(3):
        out_ref[k] += part[:, k * channels : (k + 1) * channels]


def weight_grad_kernel(
    n, entries, group_size, x_ref, above_ref, below_ref, conv_ref, gn_ref, *refs
):
    parts, grad_parts, (g_ref, first_ref, last_ref, out_ref) = refs[:n], refs[n : 2 * n], refs[2 * n :]
    _, rows, width, channels = x_ref.shape
    pixels = rows * width
    mean, inv = mean_and_inv(parts, entries, group_size)
    means = frame_stats(grad_parts, entries, group_size)
    normed = (conv_ref[0] - mean) * inv
    grad = (inv * (gn_ref[0] - means[0:1] - normed * means[1:2])).astype(BF16)
    g_ref[0] = grad
    first_ref[0] = grad[:width]
    last_ref[0] = grad[pixels - width :]
    wide = grad.astype(F32)
    moved = jnp.concatenate(
        [from_right(wide, width).astype(BF16), grad, from_left(wide, width).astype(BF16)], axis=1
    )
    padded = with_halo(above_ref, x_ref[...].reshape(pixels, channels), below_ref)

    @pl.when(pl.program_id(0) == 0)
    def _():
        out_ref[...] = jnp.zeros_like(out_ref)

    for i in range(3):
        part = dot_rows(padded[i * width : i * width + pixels], moved)
        for j in range(3):
            out_ref[i, j] += part[:, j * channels : (j + 1) * channels]


def conv_back_kernel(g_ref, above_ref, below_ref, cot_ref, w_ref, out_ref):
    _, rows, width, channels = cot_ref.shape
    pixels = rows * width
    padded = with_halo(above_ref, g_ref[0], below_ref)
    lhs = jnp.concatenate([padded[(2 - i) * width : (2 - i) * width + pixels] for i in range(3)], axis=1)
    z = [dot(lhs, w_ref[j]) for j in range(3)]
    out = z[1] + from_right(z[0], width) + from_left(z[2], width)
    out = out + cot_ref[...].reshape(pixels, channels).astype(F32)
    out_ref[...] = out.astype(BF16).reshape(out_ref.shape)


def out_kernel(info_ref, own_up, nxt, mid, own_dn, prv, tw_ref, x_ref, out_ref, cat_ref):
    gather_taps(info_ref, own_up, nxt, mid, own_dn, prv, cat_ref, 2)
    _, rows, width, channels = x_ref.shape
    temporal_out = dot(cat_ref[...], tw_ref[...]).astype(BF16).astype(F32)
    out = x_ref[...].reshape(rows * width, channels).astype(F32) + temporal_out
    out_ref[...] = out.astype(BF16).reshape(out_ref.shape)


def neighbours(axis, low, high):
    size = lax.axis_size(axis)
    up = [(i, i + 1) for i in range(size - 1)]
    down = [(j, i) for i, j in up]
    return lax.ppermute(high, axis, up), lax.ppermute(low, axis, down)


def spread_parts(part, axis):
    size = lax.axis_size(axis)
    return [part] + [
        lax.ppermute(part, axis, [(i, (i + s) % size) for i in range(size)]) for s in range(1, size)
    ]


def halve(x, axis, bit):
    size = lax.axis_size(axis)
    mine = (lax.axis_index(axis) >> bit) & 1
    half = x.shape[0] // 2
    send = lax.dynamic_slice_in_dim(x, (1 - mine) * half, half, 0).astype(BF16)
    keep = lax.dynamic_slice_in_dim(x, mine * half, half, 0)
    got = lax.ppermute(send, axis, [(i, i ^ (1 << bit)) for i in range(size)])
    return keep + got.astype(F32)


def double(x, axis, bit):
    size = lax.axis_size(axis)
    mine = (lax.axis_index(axis) >> bit) & 1
    got = lax.ppermute(x, axis, [(i, i ^ (1 << bit)) for i in range(size)])
    return jnp.concatenate([jnp.where(mine == 1, got, x), jnp.where(mine == 1, x, got)], axis=0)


def sum_everywhere(x):
    bits = [("tm", b) for b in range(1, lax.axis_size("tm").bit_length() - 1)]
    deep = [("space", b) for b in range(lax.axis_size("space").bit_length() - 1)]
    x = halve(x, "tm", 0)
    half = x.shape[0] // 2
    orders = [bits + deep, bits[::-1] + deep]
    pieces = [x[:half], x[half:]]
    for step in range(len(orders[0])):
        pieces = [halve(p, *order[step]) for p, order in zip(pieces, orders)]
    pieces = [p.astype(BF16) for p in pieces]
    for step in range(len(orders[0]) - 1, -1, -1):
        pieces = [double(p, *order[step]) for p, order in zip(pieces, orders)]
    return double(jnp.concatenate(pieces, axis=0), "tm", 0)


def slot_info(frames, clip_frames, dilation):
    first = lax.axis_index("tm") * frames
    local = jnp.arange(frames, dtype=jnp.int32)
    ids = first + local
    filled = clip_frames[0] + clip_frames[1]

    def clip_of(f):
        return (f >= clip_frames[0]).astype(jnp.int32)

    used = (ids >= 0) & (ids < filled)
    d = jnp.where(clip_of(ids) == 0, dilation[0], dilation[1])

    def live(g):
        return used & (g >= 0) & (g < filled) & (clip_of(g) == clip_of(ids))

    up, dn = local + d, local - d
    up_which = jnp.where(live(ids + d), jnp.where(up < frames, 1, 2), 0)
    dn_which = jnp.where(live(ids - d), jnp.where(dn >= 0, 1, 2), 0)
    last = frames - 1
    columns = [
        jnp.clip(up, 0, last),
        jnp.clip(up - frames, 0, last),
        up_which,
        jnp.clip(dn, 0, last),
        jnp.clip(dn + frames, 0, last),
        dn_which,
        used.astype(jnp.int32),
    ]
    return jnp.stack(columns, axis=1).astype(jnp.int32)


def per_device(frames_in, cotangent, spatial, temporal, norm_gain, norm_shift, clip_frames, dilation):
    frames, rows, width, channels = frames_in.shape
    pixels = rows * width
    n = lax.axis_size("space")
    group_size = channels // GROUPS
    entries = float(rows * n * width * group_size)
    gain, shift = norm_gain[None], norm_shift[None]
    info = slot_info(frames, clip_frames, dilation)
    big = frames * pixels * channels

    x_spec = pl.BlockSpec((1, rows, width, channels), lambda f, *_: (f, 0, 0, 0))
    edge_spec = pl.BlockSpec((1, 1, width, channels), lambda f, *_: (f, 0, 0, 0))
    row_spec = pl.BlockSpec((1, width, channels), lambda f, *_: (f, 0, 0))
    px_spec = pl.BlockSpec((1, pixels, channels), lambda f, *_: (f, 0, 0))
    sum_spec = pl.BlockSpec((1, 2, channels), lambda f, *_: (f, 0, 0))
    chan_spec = pl.BlockSpec((1, channels), lambda f, *_: (0, 0))

    def whole(*dims):
        return pl.BlockSpec(dims, lambda f, *_: (0,) * len(dims))

    def picked(column):
        return pl.BlockSpec((1, pixels, channels), lambda f, info: (info[f, column], 0, 0))

    taps = [picked(0), picked(1), px_spec, picked(3), picked(4)]
    cat = pltpu.VMEM((pixels, 3 * channels), BF16)
    shape = jax.ShapeDtypeStruct

    above, below = neighbours("space", frames_in[:, :1], frames_in[:, rows - 1 :])
    cot = cotangent.reshape(frames, pixels, channels)
    cot_prev, cot_next = neighbours("tm", cot, cot)

    conv_out, sums = pl.pallas_call(
        conv_kernel,
        grid=(frames,),
        in_specs=[x_spec, edge_spec, edge_spec, whole(3, 3, channels, channels)],
        out_specs=[px_spec, sum_spec],
        out_shape=[shape((frames, pixels, channels), F32), shape((frames, 2, channels), F32)],
        compiler_params=params(),
        cost_estimate=cost(18 * big * channels, 6 * big),
        name="conv_forward",
    )(frames_in, above, below, spatial)
    parts = spread_parts(sums, "space")

    act = pl.pallas_call(
        functools.partial(act_kernel, n, entries, group_size),
        grid_spec=pltpu.PrefetchScalarGridSpec(
            num_scalar_prefetch=1,
            grid=(frames,),
            in_specs=[sum_spec] * n + [px_spec, chan_spec, chan_spec],
            out_specs=px_spec,
        ),
        out_shape=shape((frames, pixels, channels), BF16),
        compiler_params=params(),
        cost_estimate=cost(10 * big, 6 * big, 2 * big),
        name="activation",
    )(info, *parts, conv_out, gain, shift)
    act_prev, act_next = neighbours("tm", act, act)

    grad_normed, grad_sums = pl.pallas_call(
        functools.partial(grad_act_kernel, n, entries, group_size),
        grid_spec=pltpu.PrefetchScalarGridSpec(
            num_scalar_prefetch=1,
            grid=(frames,),
            in_specs=taps + [whole(3 * channels, channels), px_spec, chan_spec, chan_spec] + [sum_spec] * n,
            out_specs=[px_spec, sum_spec],
            scratch_shapes=[cat],
        ),
        out_shape=[shape((frames, pixels, channels), F32), shape((frames, 2, channels), F32)],
        compiler_params=params(),
        cost_estimate=cost(6 * big * channels, 16 * big, 2 * big),
        name="grad_activation",
    )(
        info, cot, cot_next, cot, cot, cot_prev,
        temporal.transpose(0, 2, 1).reshape(3 * channels, channels), conv_out, gain, shift, *parts,
    )
    grad_parts = spread_parts(grad_sums, "space")

    temporal_part = pl.pallas_call(
        temporal_grad_kernel,
        grid_spec=pltpu.PrefetchScalarGridSpec(
            num_scalar_prefetch=1,
            grid=(frames,),
            in_specs=taps + [px_spec],
            out_specs=whole(3, channels, channels),
            scratch_shapes=[cat],
        ),
        out_shape=shape((3, channels, channels), F32),
        compiler_params=params(),
        cost_estimate=cost(6 * big * channels, 8 * big),
        name="temporal_grad",
    )(info, cot, cot_next, cot, cot, cot_prev, act)

    grad_conv, first_rows, last_rows, spatial_part = pl.pallas_call(
        functools.partial(weight_grad_kernel, n, entries, group_size),
        grid=(frames,),
        in_specs=[x_spec, edge_spec, edge_spec, px_spec, px_spec] + [sum_spec] * (2 * n),
        out_specs=[px_spec, row_spec, row_spec, whole(3, 3, channels, channels)],
        out_shape=[
            shape((frames, pixels, channels), BF16),
            shape((frames, width, channels), BF16),
            shape((frames, width, channels), BF16),
            shape((3, 3, channels, channels), F32),
        ],
        compiler_params=params(),
        cost_estimate=cost(18 * big * channels, 12 * big),
        name="weight_grad",
    )(frames_in, above, below, conv_out, grad_normed, *parts, *grad_parts)

    grad_above, grad_below = neighbours("space", first_rows, last_rows)
    back_weights = spatial.transpose(1, 0, 3, 2).reshape(3, 3 * channels, channels)
    in_grad = pl.pallas_call(
        conv_back_kernel,
        grid=(frames,),
        in_specs=[px_spec, row_spec, row_spec, x_spec, whole(3, 3 * channels, channels)],
        out_specs=x_spec,
        out_shape=shape(frames_in.shape, BF16),
        compiler_params=params(),
        cost_estimate=cost(18 * big * channels, 6 * big),
        name="conv_backward",
    )(grad_conv, grad_above, grad_below, cotangent, back_weights)

    out_frames = pl.pallas_call(
        out_kernel,
        grid_spec=pltpu.PrefetchScalarGridSpec(
            num_scalar_prefetch=1,
            grid=(frames,),
            in_specs=taps + [whole(3 * channels, channels), x_spec],
            out_specs=x_spec,
            scratch_shapes=[cat],
        ),
        out_shape=shape(frames_in.shape, BF16),
        compiler_params=params(),
        cost_estimate=cost(6 * big * channels, 10 * big),
        name="temporal_forward",
    )(info, act, act_next, act, act, act_prev, temporal.reshape(3 * channels, channels), frames_in)

    stacked = jnp.concatenate([spatial_part.reshape(-1, channels), temporal_part.reshape(-1, channels)], axis=0)
    total = sum_everywhere(stacked).astype(F32)
    split = 9 * channels
    spatial_grad = total[:split].reshape(spatial.shape)
    temporal_grad = total[split:].reshape(temporal.shape)
    return (out_frames, in_grad, spatial_grad, temporal_grad)


def solution(mesh):
    tiles = P("tm", "space", None, None)
    return jax.shard_map(
        per_device,
        mesh=mesh,
        in_specs=(tiles, tiles, P(), P(), P(), P(), P(), P()),
        out_specs=(tiles, tiles, P(), P()),
        check_vma=False,
    )
```

time: 373 us -> 222 us (0.60)
  matrix products: 100 us -> 0 us
  Pallas kernels: 0 us -> 62.4 us
  waiting for transfers between devices: 131 us -> 71.8 us
  blocking collectives: 23.6 us -> 0 us
  between operations: 20.4 us -> 2.57 us
  other arithmetic: 32.5 us -> 16.3 us
  starting transfers between devices: 40.6 us -> 52.4 us
  local copies, waits for them, and re-layouts: 21.6 us -> 15.6 us
    psum x1 -> x0, waiting for transfers between devices: 116 us -> none  [per_device(): lax.psum((spatial_part, temporal_part), ('tm', 'space'))]
    dot_general x36 -> x0, matrix products: 100 us -> none  [the longest x9 37.1 us: spatial_backward(): lax.dot_general(window, spatial[offset_row, offset_col], (((3,), (1,)), (...]
    ppermute x4 -> x32, waiting for transfers between devices: 3.74 us -> 71.8 us  [the longest x9 54 us: halve(): got = lax.ppermute(send, axis, [(i, i ^ 1 << bit) for i in range(size)])]
    pallas_call x0 -> x7, Pallas kernels: none -> 62.4 us  [the longest x1 14.5 us: per_device(): pl.pallas_call(functools.partial(weight_grad_kernel, n, entries, group_si...]
    ppermute x4 -> x32, starting transfers between devices: 12.4 us -> 52.4 us  [the longest x8 20.9 us: neighbours(): return (lax.ppermute(high, axis, up), lax.ppermute(low, axis, down))]
    all_to_all x4 -> x0, starting transfers between devices: 27.9 us -> none  [the longest x1 14.6 us: per_device(): lax.all_to_all(back_tiles, 'tm', split_axis=0, concat_axis=1, tiled=True)]
    psum x2 -> x0, blocking collectives: 23.6 us -> none  [the longest x1 13.2 us: per_device(): lax.psum((group_fold(jnp.sum(conv_out, axis=(1, 2))), group_fold(jnp.sum(...]
    all_to_all x4 -> x0, waiting for transfers between devices: 11.2 us -> none  [the longest x1 11.2 us: per_device(): lax.all_to_all(out_tiles, 'tm', split_axis=0, concat_axis=1, tiled=True)]
  transfers between devices with their start and end apart: 9 -> 32, of which waited for: 4 -> 17; matrix products, arithmetic and copies ran while one was open for 25% -> 7% of each run, Pallas kernels for 0% -> 17%
where the time goes in v1:
time: 222 us; the launch traced here: 221 us
  waiting for transfers between devices  71.8 us (32%)
  Pallas kernels  62.4 us (28%)
  starting transfers between devices  52.4 us (24%)
  other arithmetic  16.3 us (7%)
  local copies, waits for them, and re-layouts  15.6 us (7%)
  between operations  2.57 us (1%)
    ppermute x9, waiting for transfers between devices, halve(): got = lax.ppermute(send, axis, [(i, i ^ 1 << bit) for i in range(size)])  54 us
    ppermute x8, starting transfers between devices, neighbours(): return (lax.ppermute(high, axis, up), lax.ppermute(low, axis, down))  20.9 us
    ppermute x9, starting transfers between devices, halve(): got = lax.ppermute(send, axis, [(i, i ^ 1 << bit) for i in range(size)])  18.1 us
    pallas_call x1, Pallas kernels, per_device(): pl.pallas_call(functools.partial(weight_grad_kernel, n, entries, group_si...  14.5 us
    ppermute x9, waiting for transfers between devices, double(): got = lax.ppermute(x, axis, [(i, i ^ 1 << bit) for i in range(size)])  14.1 us
    pallas_call x1, Pallas kernels, per_device(): pl.pallas_call(functools.partial(grad_act_kernel, n, entries, group_size)...  9.93 us
    pallas_call x1, Pallas kernels, per_device(): pl.pallas_call(out_kernel, grid_spec=pltpu.PrefetchScalarGridSpec(num_sca...  8.54 us
    pallas_call x1, Pallas kernels, per_device(): pl.pallas_call(temporal_grad_kernel, grid_spec=pltpu.PrefetchScalarGridSp...  7.9 us
  transfers between devices with their start and end apart: 32, of which 17 were waited for; matrix products, arithmetic and copies ran while one was open for 7% of the time, Pallas kernels for 17%

profile of v1, /device:TPU:0, one launch (start us, length us, event | category | flops | bytes accessed | tf_op | source)
XLA Modules:
  0.0 221.1 jit_solution(14010268493353875267)
XLA Ops:
  0.6 3.8 %collective-permute-start.8 = (bf16[8,512,256]{2,1,0:T(8,128)(2,1)}, bf16[8,512,256]{2,1,0:T(8,128)(2,1)}, u32[]{:S(2)}, u32[]{:S(2)}) collective-permute-start(bf16[8,512,256]{2,1,0:T(8,128)(2,1)} %bitcast.16), channel_id=1, source_target_pairs={{0,4},{4,8},{8,12},{12,16},{16,20},{20,24},{24,28},{1,5},{5,9},{9,... | collective-permute-start | bytes 6291464 | tf_op jit(solution)/shard_map/ppermute | solution.py:205
  4.5 1.3 collective-permute-start.7
  5.7 1.1 fusion.25
  6.8 1.3 collective-permute-start.1
  8.1 5.0 %collective-permute-start = (bf16[8,1,64,256]{3,2,1,0:T(8,128)(2,1)S(1)}, bf16[8,1,64,256]{3,2,1,0:T(8,128)(2,1)S(1)}, u32[]{:S(2)}, u32[]{:S(2)}) collective-permute-start(bf16[8,1,64,256]{3,2,1,0:T(8,128)(2,1)S(1)} %get-tuple-element.21), channel_id=1, source_target_pairs={{0,1},{1,2},{2,3},{4,5},{5,6},{6,7},{8,9},{9,10},{10,11},{12,13},{... | collective-permute-start | bytes 786440 | tf_op jit(solution)/shard_map/ppermute | solution.py:205
  13.1 1.3 fusion.27
  15.7 1.3 fusion.28
  17.0 1.9 fusion.5
  19.0 2.0 select_select_fusion
  21.0 2.0 add_clamp_fusion.1
  23.0 1.7 copy-done.3
  24.6 1.3 copy-done.6
  25.9 7.2 %conv_forward.1 = (f32[8,512,256]{2,1,0:T(8,128)}, f32[8,2,256]{2,1,0:T(2,128)S(1)}) custom-call(bf16[8,8,64,256]{3,2,1,0:T(8,128)(2,1)S(1)} %copy-done.3, bf16[8,1,64,256]{3,2,1,0:T(8,128)(2,1)S(1)} %collective-permute-done.above_ref, bf16[8,1,64,256]{3,2,1,0:T(8,128)(2,1)S(1)} %collective-permute-done.1.below_ref, bf16[3,3,256,256]{3,2,1,0:T(8,128)(2,1)S(1)} %copy-done.6), custom_call_target="tpu_custom_call" | custom-call | flops 4831838208 | bytes 6291456 | tf_op jit(solution)/shard_map/conv_forward/pallas_call | solution.py:309
  33.2 1.8 collective-permute-start.4
  35.0 1.6 collective-permute-start.3
  36.6 1.6 collective-permute-start.2
  38.5 1.2 collective-permute-done.3.refs_2_.rest_2_
  39.7 2.5 %collective-permute-done.2.refs_1_.rest_1_ = f32[8,2,256]{2,1,0:T(2,128)S(1)} collective-permute-done((f32[8,2,256]{2,1,0:T(2,128)S(1)}, f32[8,2,256]{2,1,0:T(2,128)S(1)}, u32[]{:S(2)}, u32[]{:S(2)}) %collective-permute-start.2) | collective-permute-done | bytes 16416 | tf_op jit(solution)/shard_map/ppermute | solution.py:211
  42.2 7.2 %activation.1.own_up.mid.own_dn.act_ref = bf16[8,512,256]{2,1,0:T(8,128)(2,1)S(1)} custom-call(s32[8,7]{1,0:T(8,128)S(1)} %stack.2.info_ref, f32[8,2,256]{2,1,0:T(2,128)S(1)} %get-tuple-element.12.refs_0_.rest_0_, f32[8,2,256]{2,1,0:T(2,128)S(1)} %collective-permute-done.2.refs_1_.rest_1_, f32[8,2,256]{2,1,0:T(2,128)S(1)} %collective-permute-done.3.refs_2_.rest_2_, ...), custom_call_target="tpu_custom_call" | custom-call | flops 10485760 | bytes 6291456 | tf_op jit(solution)/shard_map/activation/pallas_call | solution.py:321
  49.4 1.3 copy-done.1
  50.7 9.9 %grad_activation.1 = (f32[8,512,256]{2,1,0:T(8,128)}, f32[8,2,256]{2,1,0:T(2,128)S(1)}) custom-call(s32[8,7]{1,0:T(8,128)S(1)} %stack.2.info_ref, bf16[8,512,256]{2,1,0:T(8,128)(2,1)S(1)} %bitcast.18, bf16[8,512,256]{2,1,0:T(8,128)(2,1)} %collective-permute-done.7.nxt, bf16[8,512,256]{2,1,0:T(8,128)(2,1)S(1)} %bitcast.19, bf16[8,512,256]{2,1,0:T(8,128)(2,1)S(1)} %bitcast.20, ...), custom_call_target="tpu_custom_call" | custom-call | flops 1610612736 | bytes 16777216 | tf_op jit(solution)/shard_map/grad_activation/pallas_call | solution.py:336
  60.9 1.1 collective-permute-start.10
  62.0 0.8 collective-permute-start.9
  62.7 7.9 %temporal_grad.1 = f32[3,256,256]{2,1,0:T(8,128)S(1)} custom-call(s32[8,7]{1,0:T(8,128)S(1)} %stack.2.info_ref, bf16[8,512,256]{2,1,0:T(8,128)(2,1)S(1)} %bitcast.21, bf16[8,512,256]{2,1,0:T(8,128)(2,1)} %collective-permute-done.7.nxt, bf16[8,512,256]{2,1,0:T(8,128)(2,1)S(1)} %bitcast.22, bf16[8,512,256]{2,1,0:T(8,128)(2,1)S(1)} %bitcast.23, ...), custom_call_target="tpu_custom_call" | custom-call | flops 1610612736 | bytes 8388608 | tf_op jit(solution)/shard_map/temporal_grad/pallas_call | solution.py:355
  70.7 14.5 %weight_grad.1 = (bf16[8,512,256]{2,1,0:T(8,128)(2,1)S(1)}, bf16[8,64,256]{2,1,0:T(8,128)(2,1)S(1)}, bf16[8,64,256]{2,1,0:T(8,128)(2,1)S(1)}, f32[3,3,256,256]{3,2,1,0:T(8,128)}) custom-call(bf16[8,8,64,256]{3,2,1,0:T(8,128)(2,1)S(1)} %copy-done.4, bf16[8,1,64,256]{3,2,1,0:T(8,128)(2,1)S(1)} %copy-done.17, bf16[8,1,64,256]{3,2,1,0:T(8,128)(2,1)S(1)} %copy-done.15, ...), custom_call_target="tpu_custom_call" | custom-call | flops 4831838208 | bytes 12582912 | tf_op jit(solution)/shard_map/weight_grad/pallas_call | solution.py:370
  85.2 3.2 %fusion.1 = bf16[1536,256]{1,0:T(8,128)(2,1)} fusion(s32[]{:T(128)S(6)} %select_n.226, f32[2304,256]{1,0:T(8,128)} %bitcast.35, f32[768,256]{1,0:T(8,128)S(1)} %bitcast.24), kind=kLoop, calls=%fused_computation.5 | loop fusion | flops 1572864 | bytes 3932164 | tf_op jit(solution)/shard_map/convert_element_type | solution.py:219
  88.4 5.5 %collective-permute-start.14 = (bf16[1536,256]{1,0:T(8,128)(2,1)}, bf16[1536,256]{1,0:T(8,128)(2,1)}, u32[]{:S(2)}, u32[]{:S(2)}) collective-permute-start(bf16[1536,256]{1,0:T(8,128)(2,1)} %fusion.1), channel_id=1, source_target_pairs={{0,4},{4,0},{8,12},{12,8},{16,20},{20,16},{24,28},{28,24},{1,5},{5... | collective-permute-start | bytes 2359304 | tf_op jit(solution)/shard_map/ppermute | solution.py:221
  94.0 2.3 %collective-permute-done.14 = bf16[1536,256]{1,0:T(8,128)(2,1)} collective-permute-done((bf16[1536,256]{1,0:T(8,128)(2,1)}, bf16[1536,256]{1,0:T(8,128)(2,1)}, u32[]{:S(2)}, u32[]{:S(2)}) %collective-permute-start.14) | collective-permute-done | bytes 786464 | tf_op jit(solution)/shard_map/ppermute | solution.py:221
  96.2 2.1 fusion.3
  98.5 0.9 copy-done.20
  100.4 3.0 %collective-permute-start.6 = (bf16[8,512,256]{2,1,0:T(8,128)(2,1)}, bf16[8,512,256]{2,1,0:T(8,128)(2,1)}, u32[]{:S(2)}, u32[]{:S(2)}) collective-permute-start(bf16[8,512,256]{2,1,0:T(8,128)(2,1)} %copy-done.1), channel_id=1, source_target_pairs={{0,4},{4,8},{8,12},{12,16},{16,20},{20,24},{24,28},{1,5},{5,9},{9,... | collective-permute-start | bytes 6291464 | tf_op jit(solution)/shard_map/ppermute | solution.py:205
  103.5 1.3 collective-permute-start.5
  104.8 2.5 %collective-permute-start.15 = (bf16[384,256]{1,0:T(8,128)(2,1)S(1)}, bf16[384,256]{1,0:T(8,128)(2,1)S(1)}, u32[]{:S(2)}, u32[]{:S(2)}) collective-permute-start(bf16[384,256]{1,0:T(8,128)(2,1)S(1)} %dynamic-slice_convert_fusion.1), channel_id=1, source_target_pairs={{0,8},{4,12},{8,0},{12,4},{16,24},{20,28},{24,16},{28,20},{1,9},{5... | collective-permute-start | bytes 589832 | tf_op jit(solution)/shard_map/ppermute | solution.py:221
  107.2 1.0 convert_add_fusion
  108.3 1.5 collective-permute-start.24
  109.9 46.9 %collective-permute-done.15 = bf16[384,256]{1,0:T(8,128)(2,1)S(1)} collective-permute-done((bf16[384,256]{1,0:T(8,128)(2,1)S(1)}, bf16[384,256]{1,0:T(8,128)(2,1)S(1)}, u32[]{:S(2)}, u32[]{:S(2)}) %collective-permute-start.15) | collective-permute-done | bytes 196640 | tf_op jit(solution)/shard_map/ppermute | solution.py:221
  156.9 0.9 collective-permute-done.24
  157.9 2.5 %collective-permute-start.25 = (bf16[96,256]{1,0:T(8,128)(2,1)S(1)}, bf16[96,256]{1,0:T(8,128)(2,1)S(1)}, u32[]{:S(2)}, u32[]{:S(2)}) collective-permute-start(bf16[96,256]{1,0:T(8,128)(2,1)S(1)} %dynamic-slice_convert_fusion.4), channel_id=1, source_target_pairs={{0,1},{1,0},{2,3},{3,2},{4,5},{5,4},{6,7},{7,6},{8,9},{9,8},{10,11... | collective-permute-start | bytes 147464 | tf_op jit(solution)/shard_map/ppermute | solution.py:221
  160.4 1.1 collective-permute-done.16
  161.6 2.5 %collective-permute-start.17 = (bf16[96,256]{1,0:T(8,128)(2,1)S(1)}, bf16[96,256]{1,0:T(8,128)(2,1)S(1)}, u32[]{:S(2)}, u32[]{:S(2)}) collective-permute-start(bf16[96,256]{1,0:T(8,128)(2,1)S(1)} %dynamic-slice_convert_fusion.5), channel_id=1, source_target_pairs={{0,1},{1,0},{2,3},{3,2},{4,5},{5,4},{6,7},{7,6},{8,9},{9,8},{10,11... | collective-permute-start | bytes 147464 | tf_op jit(solution)/shard_map/ppermute | solution.py:221
  164.2 1.2 collective-permute-start.26
  165.4 0.8 collective-permute-done.17
  166.2 1.8 collective-permute-start.18
  168.0 1.3 collective-permute-done.26
  169.3 0.9 collective-permute-start.27
  171.0 1.9 collective-permute-start.19
  173.0 1.2 collective-permute-done.27
  174.7 1.2 collective-permute-done.19
  175.9 2.3 %collective-permute-start.20 = (bf16[96,256]{1,0:T(8,128)(2,1)S(1)}, bf16[96,256]{1,0:T(8,128)(2,1)S(1)}, u32[]{:S(2)}, u32[]{:S(2)}) collective-permute-start(bf16[96,256]{1,0:T(8,128)(2,1)S(1)} %pad_maximum_fusion.5), channel_id=1, source_target_pairs={{0,1},{1,0},{2,3},{3,2},{4,5},{5,4},{6,7},{7,6},{8,9},{9,8},{10,11... | collective-permute-start | bytes 147464 | tf_op jit(solution)/shard_map/ppermute | solution.py:228
  178.4 1.9 collective-permute-done.20
  180.5 2.5 %collective-permute-done.29 = bf16[192,256]{1,0:T(8,128)(2,1)S(1)} collective-permute-done((bf16[192,256]{1,0:T(8,128)(2,1)S(1)}, bf16[192,256]{1,0:T(8,128)(2,1)S(1)}, u32[]{:S(2)}, u32[]{:S(2)}) %collective-permute-start.29) | collective-permute-done | bytes 98336 | tf_op jit(solution)/shard_map/ppermute | solution.py:228
  183.2 1.8 collective-permute-done.21
  185.3 3.5 %collective-permute-done.30 = bf16[384,256]{1,0:T(8,128)(2,1)S(1)} collective-permute-done((bf16[384,256]{1,0:T(8,128)(2,1)S(1)}, bf16[384,256]{1,0:T(8,128)(2,1)S(1)}, u32[]{:S(2)}, u32[]{:S(2)}) %collective-permute-start.30) | collective-permute-done | bytes 196640 | tf_op jit(solution)/shard_map/ppermute | solution.py:228
  188.9 1.9 collective-permute-done.22
  190.9 1.0 pad_maximum_fusion
  191.9 3.9 %collective-permute-start.12 = (bf16[8,64,256]{2,1,0:T(8,128)(2,1)S(1)}, bf16[8,64,256]{2,1,0:T(8,128)(2,1)S(1)}, u32[]{:S(2)}, u32[]{:S(2)}) collective-permute-start(bf16[8,64,256]{2,1,0:T(8,128)(2,1)S(1)} %copy-done.13), channel_id=1, source_target_pairs={{0,1},{1,2},{2,3},{4,5},{5,6},{6,7},{8,9},{9,10},{10,11},{12,13},{... | collective-permute-start | bytes 786440 | tf_op jit(solution)/shard_map/ppermute | solution.py:205
  195.9 1.3 collective-permute-start.13
  197.2 2.4 %copy.13 = bf16[3,3,256,256]{3,2,1,0:T(8,128)(2,1)} copy(bf16[3,3,256,256]{2,3,0,1:T(8,128)(2,1)} %bitcast.29) | data formatting | bytes 2359296 | tf_op jit(solution)/shard_map/transpose | solution.py:387
  199.6 1.6 copy-done.2
  201.2 8.5 %temporal_forward.1 = bf16[8,8,64,256]{3,2,1,0:T(8,128)(2,1)} custom-call(s32[8,7]{1,0:T(8,128)S(1)} %stack.2.info_ref, bf16[8,512,256]{2,1,0:T(8,128)(2,1)S(1)} %copy-done.2, bf16[8,512,256]{2,1,0:T(8,128)(2,1)} %collective-permute-done.5.nxt, bf16[8,512,256]{2,1,0:T(8,128)(2,1)S(1)} %copy-done.2, bf16[8,512,256]{2,1,0:T(8,128)(2,1)S(1)} %copy-done.2, ...), custom_call_target="tpu_custom_call" | custom-call | flops 1610612736 | bytes 10485760 | tf_op jit(solution)/shard_map/temporal_forward/pallas_call | solution.py:399
  209.8 7.1 %conv_backward.1 = bf16[8,8,64,256]{3,2,1,0:T(8,128)(2,1)} custom-call(bf16[8,512,256]{2,1,0:T(8,128)(2,1)S(1)} %copy-done.19, bf16[8,64,256]{2,1,0:T(8,128)(2,1)S(1)} %collective-permute-done.12.above_ref, bf16[8,64,256]{2,1,0:T(8,128)(2,1)S(1)} %collective-permute-done.13.below_ref, bf16[8,8,64,256]{3,2,1,0:T(8,128)(2,1)S(1)} %copy-done, ...), custom_call_target="tpu_custom_call" | custom-call | flops 4831838208 | bytes 6291456 | tf_op jit(solution)/shard_map/conv_backward/pallas_call | solution.py:388
  216.9 1.5 broadcast_select_fusion.1
  218.4 0.9 maximum_convert_fusion.1
  219.5 1.6 slice.47
  (113 shorter events, 4.6 us)
Async XLA Ops:
  0.6 50.1 %collective-permute-start.8 = (bf16[8,512,256]{2,1,0:T(8,128)(2,1)}, bf16[8,512,256]{2,1,0:T(8,128)(2,1)}, u32[]{:S(2)}, u32[]{:S(2)}) collective-permute-start(bf16[8,512,256]{2,1,0:T(8,128)(2,1)} %bitcast.16), channel_id=1, source_target_pairs={{0,4},{4,8},{8,12},{12,16},{16,20},{20,24},{24,28},{1,5},{5,9},{9,... | collective-permute-start | bytes 6291464 | tf_op jit(solution)/shard_map/ppermute | solution.py:205
  4.5 46.3 %collective-permute-start.7 = (bf16[8,512,256]{2,1,0:T(8,128)(2,1)}, bf16[8,512,256]{2,1,0:T(8,128)(2,1)}, u32[]{:S(2)}, u32[]{:S(2)}) collective-permute-start(bf16[8,512,256]{2,1,0:T(8,128)(2,1)} %bitcast.17), channel_id=1, source_target_pairs={{4,0},{8,4},{12,8},{16,12},{20,16},{24,20},{28,24},{5,1},{9,5},{13... | collective-permute-start | bytes 6291464 | tf_op jit(solution)/shard_map/ppermute | solution.py:205
  6.8 16.1 %collective-permute-start.1 = (bf16[8,1,64,256]{3,2,1,0:T(8,128)(2,1)S(1)}, bf16[8,1,64,256]{3,2,1,0:T(8,128)(2,1)S(1)}, u32[]{:S(2)}, u32[]{:S(2)}) collective-permute-start(bf16[8,1,64,256]{3,2,1,0:T(8,128)(2,1)S(1)} %get-tuple-element.20), channel_id=1, source_target_pairs={{1,0},{2,1},{3,2},{5,4},{6,5},{7,6},{9,8},{10,9},{11,10},{13,12},{... | collective-permute-start | bytes 786440 | tf_op jit(solution)/shard_map/ppermute | solution.py:205
  8.1 14.8 %collective-permute-start = (bf16[8,1,64,256]{3,2,1,0:T(8,128)(2,1)S(1)}, bf16[8,1,64,256]{3,2,1,0:T(8,128)(2,1)S(1)}, u32[]{:S(2)}, u32[]{:S(2)}) collective-permute-start(bf16[8,1,64,256]{3,2,1,0:T(8,128)(2,1)S(1)} %get-tuple-element.21), channel_id=1, source_target_pairs={{0,1},{1,2},{2,3},{4,5},{5,6},{6,7},{8,9},{9,10},{10,11},{12,13},{... | collective-permute-start | bytes 786440 | tf_op jit(solution)/shard_map/ppermute | solution.py:205
  20.9 21.2 %copy-start.8 = (f32[256]{0:T(256)S(1)}, f32[256]{0:T(256)}, u32[]{:S(2)}) copy-start(f32[256]{0:T(256)} %param.12) | copy-start | bytes 3076
  20.9 21.2 %copy-start.9 = (f32[256]{0:T(256)S(1)}, f32[256]{0:T(256)}, u32[]{:S(2)}) copy-start(f32[256]{0:T(256)} %param.13) | copy-start | bytes 3076
  22.9 10.2 %copy-start.14 = (bf16[8,1,64,256]{3,2,1,0:T(8,128)(2,1)}, bf16[8,1,64,256]{3,2,1,0:T(8,128)(2,1)S(1)}, u32[]{:S(2)}) copy-start(bf16[8,1,64,256]{3,2,1,0:T(8,128)(2,1)S(1)} %collective-permute-done.1.below_ref) | copy-start | bytes 786436
  23.0 1.7 copy-start.3
  24.6 1.3 copy-start.6
  25.9 7.3 %copy-start.16 = (bf16[8,1,64,256]{3,2,1,0:T(8,128)(2,1)}, bf16[8,1,64,256]{3,2,1,0:T(8,128)(2,1)S(1)}, u32[]{:S(2)}) copy-start(bf16[8,1,64,256]{3,2,1,0:T(8,128)(2,1)S(1)} %collective-permute-done.above_ref) | copy-start | bytes 786436
  25.9 12.3 %copy-start.5 = (bf16[3,256,256]{2,1,0:T(8,128)(2,1)S(1)}, bf16[3,256,256]{2,1,0:T(8,128)(2,1)}, u32[]{:S(2)}) copy-start(bf16[3,256,256]{2,1,0:T(8,128)(2,1)} %param.11) | copy-start | bytes 1179652
  33.2 5.3 %collective-permute-start.4 = (f32[8,2,256]{2,1,0:T(2,128)S(1)}, f32[8,2,256]{2,1,0:T(2,128)S(1)}, u32[]{:S(2)}, u32[]{:S(2)}) collective-permute-start(f32[8,2,256]{2,1,0:T(2,128)S(1)} %get-tuple-element.12.refs_0_.rest_0_), channel_id=1, source_target_pairs={{0,3},{1,0},{2,1},{3,2},{4,7},{5,4},{6,5},{7,6},{8,11},{9,8},{10,9... | collective-permute-start | bytes 49160 | tf_op jit(solution)/shard_map/ppermute | solution.py:211
  35.0 4.7 %collective-permute-start.3 = (f32[8,2,256]{2,1,0:T(2,128)S(1)}, f32[8,2,256]{2,1,0:T(2,128)S(1)}, u32[]{:S(2)}, u32[]{:S(2)}) collective-permute-start(f32[8,2,256]{2,1,0:T(2,128)S(1)} %get-tuple-element.12.refs_0_.rest_0_), channel_id=1, source_target_pairs={{0,2},{1,3},{2,0},{3,1},{4,6},{5,7},{6,4},{7,5},{8,10},{9,11},{10,... | collective-permute-start | bytes 49160 | tf_op jit(solution)/shard_map/ppermute | solution.py:211
  36.6 5.5 %collective-permute-start.2 = (f32[8,2,256]{2,1,0:T(2,128)S(1)}, f32[8,2,256]{2,1,0:T(2,128)S(1)}, u32[]{:S(2)}, u32[]{:S(2)}) collective-permute-start(f32[8,2,256]{2,1,0:T(2,128)S(1)} %get-tuple-element.12.refs_0_.rest_0_), channel_id=1, source_target_pairs={{0,1},{1,2},{2,3},{3,0},{4,5},{5,6},{6,7},{7,4},{8,9},{9,10},{10,1... | collective-permute-start | bytes 49160 | tf_op jit(solution)/shard_map/ppermute | solution.py:211
  42.2 8.5 %copy-start = (bf16[8,8,64,256]{3,2,1,0:T(8,128)(2,1)S(1)}, bf16[8,8,64,256]{3,2,1,0:T(8,128)(2,1)}, u32[]{:S(2)}) copy-start(bf16[8,8,64,256]{3,2,1,0:T(8,128)(2,1)} %cot_ref.1) | copy-start | bytes 6291460
  49.4 1.3 copy-start.1
  60.6 10.0 %copy-start.4 = (bf16[8,8,64,256]{3,2,1,0:T(8,128)(2,1)S(1)}, bf16[8,8,64,256]{3,2,1,0:T(8,128)(2,1)}, u32[]{:S(2)}) copy-start(bf16[8,8,64,256]{3,2,1,0:T(8,128)(2,1)} %x_ref.5) | copy-start | bytes 6291460
  60.7 10.0 %copy-start.15 = (bf16[8,1,64,256]{3,2,1,0:T(8,128)(2,1)S(1)}, bf16[8,1,64,256]{3,2,1,0:T(8,128)(2,1)}, u32[]{:S(2)}) copy-start(bf16[8,1,64,256]{3,2,1,0:T(8,128)(2,1)} %copy-done.14) | copy-start | bytes 786436
  60.7 10.0 %copy-start.17 = (bf16[8,1,64,256]{3,2,1,0:T(8,128)(2,1)S(1)}, bf16[8,1,64,256]{3,2,1,0:T(8,128)(2,1)}, u32[]{:S(2)}) copy-start(bf16[8,1,64,256]{3,2,1,0:T(8,128)(2,1)} %copy-done.16) | copy-start | bytes 786436
  60.7 10.0 %collective-permute-start.11 = (f32[8,2,256]{2,1,0:T(2,128)S(1)}, f32[8,2,256]{2,1,0:T(2,128)S(1)}, u32[]{:S(2)}, u32[]{:S(2)}) collective-permute-start(f32[8,2,256]{2,1,0:T(2,128)S(1)} %get-tuple-element.15.refs_4_), channel_id=1, source_target_pairs={{0,3},{1,0},{2,1},{3,2},{4,7},{5,4},{6,5},{7,6},{8,11},{9,8},{10,9... | collective-permute-start | bytes 49160 | tf_op jit(solution)/shard_map/ppermute | solution.py:211
  60.9 9.8 %collective-permute-start.10 = (f32[8,2,256]{2,1,0:T(2,128)S(1)}, f32[8,2,256]{2,1,0:T(2,128)S(1)}, u32[]{:S(2)}, u32[]{:S(2)}) collective-permute-start(f32[8,2,256]{2,1,0:T(2,128)S(1)} %get-tuple-element.15.refs_4_), channel_id=1, source_target_pairs={{0,2},{1,3},{2,0},{3,1},{4,6},{5,7},{6,4},{7,5},{8,10},{9,11},{10,... | collective-permute-start | bytes 49160 | tf_op jit(solution)/shard_map/ppermute | solution.py:211
  62.0 8.7 %collective-permute-start.9 = (f32[8,2,256]{2,1,0:T(2,128)S(1)}, f32[8,2,256]{2,1,0:T(2,128)S(1)}, u32[]{:S(2)}, u32[]{:S(2)}) collective-permute-start(f32[8,2,256]{2,1,0:T(2,128)S(1)} %get-tuple-element.15.refs_4_), channel_id=1, source_target_pairs={{0,1},{1,2},{2,3},{3,0},{4,5},{5,6},{6,7},{7,4},{8,9},{9,10},{10,1... | collective-permute-start | bytes 49160 | tf_op jit(solution)/shard_map/ppermute | solution.py:211
  85.2 3.3 %copy-start.10 = (bf16[8,64,256]{2,1,0:T(8,128)(2,1)}, bf16[8,64,256]{2,1,0:T(8,128)(2,1)S(1)}, u32[]{:S(2)}) copy-start(bf16[8,64,256]{2,1,0:T(8,128)(2,1)S(1)} %get-tuple-element.18) | copy-start | bytes 786436
  85.2 3.3 %copy-start.12 = (bf16[8,64,256]{2,1,0:T(8,128)(2,1)}, bf16[8,64,256]{2,1,0:T(8,128)(2,1)S(1)}, u32[]{:S(2)}) copy-start(bf16[8,64,256]{2,1,0:T(8,128)(2,1)S(1)} %get-tuple-element.17) | copy-start | bytes 786436
  85.2 3.3 %copy-start.18 = (bf16[8,512,256]{2,1,0:T(8,128)(2,1)}, bf16[8,512,256]{2,1,0:T(8,128)(2,1)S(1)}, u32[]{:S(2)}) copy-start(bf16[8,512,256]{2,1,0:T(8,128)(2,1)S(1)} %get-tuple-element.16.g_ref) | copy-start | bytes 6291460
  88.4 7.8 %collective-permute-start.14 = (bf16[1536,256]{1,0:T(8,128)(2,1)}, bf16[1536,256]{1,0:T(8,128)(2,1)}, u32[]{:S(2)}, u32[]{:S(2)}) collective-permute-start(bf16[1536,256]{1,0:T(8,128)(2,1)} %fusion.1), channel_id=1, source_target_pairs={{0,4},{4,0},{8,12},{12,8},{16,20},{20,16},{24,28},{28,24},{1,5},{5... | collective-permute-start | bytes 2359304 | tf_op jit(solution)/shard_map/ppermute | solution.py:221
  98.5 0.9 copy-start.20
  100.0 7.2 %collective-permute-start.23 = (bf16[384,256]{1,0:T(8,128)(2,1)}, bf16[384,256]{1,0:T(8,128)(2,1)S(1)}, u32[]{:S(2)}, u32[]{:S(2)}) collective-permute-start(bf16[384,256]{1,0:T(8,128)(2,1)} %dynamic-slice_convert_fusion), channel_id=1, source_target_pairs={{0,16},{4,20},{8,24},{12,28},{16,0},{20,4},{24,8},{28,12},{1,17},{... | collective-permute-start | bytes 589832 | tf_op jit(solution)/shard_map/ppermute | solution.py:221
  100.4 99.2 %collective-permute-start.6 = (bf16[8,512,256]{2,1,0:T(8,128)(2,1)}, bf16[8,512,256]{2,1,0:T(8,128)(2,1)}, u32[]{:S(2)}, u32[]{:S(2)}) collective-permute-start(bf16[8,512,256]{2,1,0:T(8,128)(2,1)} %copy-done.1), channel_id=1, source_target_pairs={{0,4},{4,8},{8,12},{12,16},{16,20},{20,24},{24,28},{1,5},{5,9},{9,... | collective-permute-start | bytes 6291464 | tf_op jit(solution)/shard_map/ppermute | solution.py:205
  103.5 96.1 %collective-permute-start.5 = (bf16[8,512,256]{2,1,0:T(8,128)(2,1)}, bf16[8,512,256]{2,1,0:T(8,128)(2,1)}, u32[]{:S(2)}, u32[]{:S(2)}) collective-permute-start(bf16[8,512,256]{2,1,0:T(8,128)(2,1)} %copy-done.1), channel_id=1, source_target_pairs={{4,0},{8,4},{12,8},{16,12},{20,16},{24,20},{28,24},{5,1},{9,5},{13... | collective-permute-start | bytes 6291464 | tf_op jit(solution)/shard_map/ppermute | solution.py:205
  104.8 52.0 %collective-permute-start.15 = (bf16[384,256]{1,0:T(8,128)(2,1)S(1)}, bf16[384,256]{1,0:T(8,128)(2,1)S(1)}, u32[]{:S(2)}, u32[]{:S(2)}) collective-permute-start(bf16[384,256]{1,0:T(8,128)(2,1)S(1)} %dynamic-slice_convert_fusion.1), channel_id=1, source_target_pairs={{0,8},{4,12},{8,0},{12,4},{16,24},{20,28},{24,16},{28,20},{1,9},{5... | collective-permute-start | bytes 589832 | tf_op jit(solution)/shard_map/ppermute | solution.py:221
  108.3 49.5 %collective-permute-start.24 = (bf16[192,256]{1,0:T(8,128)(2,1)S(1)}, bf16[192,256]{1,0:T(8,128)(2,1)S(1)}, u32[]{:S(2)}, u32[]{:S(2)}) collective-permute-start(bf16[192,256]{1,0:T(8,128)(2,1)S(1)} %dynamic-slice_convert_fusion.2), channel_id=1, source_target_pairs={{0,8},{4,12},{8,0},{12,4},{16,24},{20,28},{24,16},{28,20},{1,9},{5... | collective-permute-start | bytes 294920 | tf_op jit(solution)/shard_map/ppermute | solution.py:221
  156.9 4.7 %collective-permute-start.16 = (bf16[192,256]{1,0:T(8,128)(2,1)S(1)}, bf16[192,256]{1,0:T(8,128)(2,1)S(1)}, u32[]{:S(2)}, u32[]{:S(2)}) collective-permute-start(bf16[192,256]{1,0:T(8,128)(2,1)S(1)} %dynamic-slice_convert_fusion.3), channel_id=1, source_target_pairs={{0,16},{4,20},{8,24},{12,28},{16,0},{20,4},{24,8},{28,12},{1,17},{... | collective-permute-start | bytes 294920 | tf_op jit(solution)/shard_map/ppermute | solution.py:221
  157.9 6.2 %collective-permute-start.25 = (bf16[96,256]{1,0:T(8,128)(2,1)S(1)}, bf16[96,256]{1,0:T(8,128)(2,1)S(1)}, u32[]{:S(2)}, u32[]{:S(2)}) collective-permute-start(bf16[96,256]{1,0:T(8,128)(2,1)S(1)} %dynamic-slice_convert_fusion.4), channel_id=1, source_target_pairs={{0,1},{1,0},{2,3},{3,2},{4,5},{5,4},{6,7},{7,6},{8,9},{9,8},{10,11... | collective-permute-start | bytes 147464 | tf_op jit(solution)/shard_map/ppermute | solution.py:221
  161.6 4.6 %collective-permute-start.17 = (bf16[96,256]{1,0:T(8,128)(2,1)S(1)}, bf16[96,256]{1,0:T(8,128)(2,1)S(1)}, u32[]{:S(2)}, u32[]{:S(2)}) collective-permute-start(bf16[96,256]{1,0:T(8,128)(2,1)S(1)} %dynamic-slice_convert_fusion.5), channel_id=1, source_target_pairs={{0,1},{1,0},{2,3},{3,2},{4,5},{5,4},{6,7},{7,6},{8,9},{9,8},{10,11... | collective-permute-start | bytes 147464 | tf_op jit(solution)/shard_map/ppermute | solution.py:221
  164.2 5.1 %collective-permute-start.26 = (bf16[48,256]{1,0:T(8,128)(2,1)S(1)}, bf16[48,256]{1,0:T(8,128)(2,1)S(1)}, u32[]{:S(2)}, u32[]{:S(2)}) collective-permute-start(bf16[48,256]{1,0:T(8,128)(2,1)S(1)} %dynamic-slice_convert_fusion.6), channel_id=1, source_target_pairs={{0,2},{1,3},{2,0},{3,1},{4,6},{5,7},{6,4},{7,5},{8,10},{9,11},{10,... | collective-permute-start | bytes 73736 | tf_op jit(solution)/shard_map/ppermute | solution.py:221
  166.2 4.8 %collective-permute-start.18 = (bf16[48,256]{1,0:T(8,128)(2,1)S(1)}, bf16[48,256]{1,0:T(8,128)(2,1)S(1)}, u32[]{:S(2)}, u32[]{:S(2)}) collective-permute-start(bf16[48,256]{1,0:T(8,128)(2,1)S(1)} %dynamic-slice_convert_fusion.7), channel_id=1, source_target_pairs={{0,2},{1,3},{2,0},{3,1},{4,6},{5,7},{6,4},{7,5},{8,10},{9,11},{10,... | collective-permute-start | bytes 73736 | tf_op jit(solution)/shard_map/ppermute | solution.py:221
  169.3 4.8 %collective-permute-start.27 = (bf16[48,256]{1,0:T(8,128)(2,1)S(1)}, bf16[48,256]{1,0:T(8,128)(2,1)S(1)}, u32[]{:S(2)}, u32[]{:S(2)}) collective-permute-start(bf16[48,256]{1,0:T(8,128)(2,1)S(1)} %add_convert_fusion), channel_id=1, source_target_pairs={{0,2},{1,3},{2,0},{3,1},{4,6},{5,7},{6,4},{7,5},{8,10},{9,11},{10,... | collective-permute-start | bytes 73736 | tf_op jit(solution)/shard_map/ppermute | solution.py:228
  171.0 4.8 %collective-permute-start.19 = (bf16[48,256]{1,0:T(8,128)(2,1)S(1)}, bf16[48,256]{1,0:T(8,128)(2,1)S(1)}, u32[]{:S(2)}, u32[]{:S(2)}) collective-permute-start(bf16[48,256]{1,0:T(8,128)(2,1)S(1)} %add_convert_fusion.1), channel_id=1, source_target_pairs={{0,2},{1,3},{2,0},{3,1},{4,6},{5,7},{6,4},{7,5},{8,10},{9,11},{10,... | collective-permute-start | bytes 73736 | tf_op jit(solution)/shard_map/ppermute | solution.py:228
  174.1 4.2 %collective-permute-start.28 = (bf16[96,256]{1,0:T(8,128)(2,1)S(1)}, bf16[96,256]{1,0:T(8,128)(2,1)S(1)}, u32[]{:S(2)}, u32[]{:S(2)}) collective-permute-start(bf16[96,256]{1,0:T(8,128)(2,1)S(1)} %pad_maximum_fusion.6), channel_id=1, source_target_pairs={{0,1},{1,0},{2,3},{3,2},{4,5},{5,4},{6,7},{7,6},{8,9},{9,8},{10,11... | collective-permute-start | bytes 147464 | tf_op jit(solution)/shard_map/ppermute | solution.py:228
  175.9 4.4 %collective-permute-start.20 = (bf16[96,256]{1,0:T(8,128)(2,1)S(1)}, bf16[96,256]{1,0:T(8,128)(2,1)S(1)}, u32[]{:S(2)}, u32[]{:S(2)}) collective-permute-start(bf16[96,256]{1,0:T(8,128)(2,1)S(1)} %pad_maximum_fusion.5), channel_id=1, source_target_pairs={{0,1},{1,0},{2,3},{3,2},{4,5},{5,4},{6,7},{7,6},{8,9},{9,8},{10,11... | collective-permute-start | bytes 147464 | tf_op jit(solution)/shard_map/ppermute | solution.py:228
  178.3 4.7 %collective-permute-start.29 = (bf16[192,256]{1,0:T(8,128)(2,1)S(1)}, bf16[192,256]{1,0:T(8,128)(2,1)S(1)}, u32[]{:S(2)}, u32[]{:S(2)}) collective-permute-start(bf16[192,256]{1,0:T(8,128)(2,1)S(1)} %pad_maximum_fusion.4), channel_id=1, source_target_pairs={{0,8},{4,12},{8,0},{12,4},{16,24},{20,28},{24,16},{28,20},{1,9},{5... | collective-permute-start | bytes 294920 | tf_op jit(solution)/shard_map/ppermute | solution.py:228
  180.3 4.7 %collective-permute-start.21 = (bf16[192,256]{1,0:T(8,128)(2,1)S(1)}, bf16[192,256]{1,0:T(8,128)(2,1)S(1)}, u32[]{:S(2)}, u32[]{:S(2)}) collective-permute-start(bf16[192,256]{1,0:T(8,128)(2,1)S(1)} %pad_maximum_fusion.3), channel_id=1, source_target_pairs={{0,16},{4,20},{8,24},{12,28},{16,0},{20,4},{24,8},{28,12},{1,17},{... | collective-permute-start | bytes 294920 | tf_op jit(solution)/shard_map/ppermute | solution.py:228
  183.1 5.7 %collective-permute-start.30 = (bf16[384,256]{1,0:T(8,128)(2,1)S(1)}, bf16[384,256]{1,0:T(8,128)(2,1)S(1)}, u32[]{:S(2)}, u32[]{:S(2)}) collective-permute-start(bf16[384,256]{1,0:T(8,128)(2,1)S(1)} %pad_maximum_fusion.2), channel_id=1, source_target_pairs={{0,16},{4,20},{8,24},{12,28},{16,0},{20,4},{24,8},{28,12},{1,17},{... | collective-permute-start | bytes 589832 | tf_op jit(solution)/shard_map/ppermute | solution.py:228
  185.1 6.8 %copy-start.13 = (bf16[8,64,256]{2,1,0:T(8,128)(2,1)S(1)}, bf16[8,64,256]{2,1,0:T(8,128)(2,1)}, u32[]{:S(2)}) copy-start(bf16[8,64,256]{2,1,0:T(8,128)(2,1)} %copy-done.12) | copy-start | bytes 786436
  185.1 10.8 %copy-start.11 = (bf16[8,64,256]{2,1,0:T(8,128)(2,1)S(1)}, bf16[8,64,256]{2,1,0:T(8,128)(2,1)}, u32[]{:S(2)}) copy-start(bf16[8,64,256]{2,1,0:T(8,128)(2,1)} %copy-done.10) | copy-start | bytes 786436
  185.1 5.7 %collective-permute-start.22 = (bf16[384,256]{1,0:T(8,128)(2,1)S(1)}, bf16[384,256]{1,0:T(8,128)(2,1)S(1)}, u32[]{:S(2)}, u32[]{:S(2)}) collective-permute-start(bf16[384,256]{1,0:T(8,128)(2,1)S(1)} %pad_maximum_fusion.1), channel_id=1, source_target_pairs={{0,8},{4,12},{8,0},{12,4},{16,24},{20,28},{24,16},{28,20},{1,9},{5... | collective-permute-start | bytes 589832 | tf_op jit(solution)/shard_map/ppermute | solution.py:228
  188.9 7.0 %copy-start.21 = (bf16[384,256]{1,0:T(8,128)(2,1)}, bf16[384,256]{1,0:T(8,128)(2,1)S(1)}, u32[]{:S(2)}) copy-start(bf16[384,256]{1,0:T(8,128)(2,1)S(1)} %get-tuple-element.28) | copy-start | bytes 589828
  188.9 7.0 %copy-start.23 = (bf16[384,256]{1,0:T(8,128)(2,1)}, bf16[384,256]{1,0:T(8,128)(2,1)S(1)}, u32[]{:S(2)}) copy-start(bf16[384,256]{1,0:T(8,128)(2,1)S(1)} %get-tuple-element.29) | copy-start | bytes 589828
  190.9 5.0 %copy-start.25 = (bf16[384,256]{1,0:T(8,128)(2,1)}, bf16[384,256]{1,0:T(8,128)(2,1)S(1)}, u32[]{:S(2)}) copy-start(bf16[384,256]{1,0:T(8,128)(2,1)S(1)} %get-tuple-element.26) | copy-start | bytes 589828
  190.9 5.0 %copy-start.27 = (bf16[384,256]{1,0:T(8,128)(2,1)}, bf16[384,256]{1,0:T(8,128)(2,1)S(1)}, u32[]{:S(2)}) copy-start(bf16[384,256]{1,0:T(8,128)(2,1)S(1)} %get-tuple-element.27) | copy-start | bytes 589828
  191.9 25.0 %collective-permute-start.31 = (bf16[1536,256]{1,0:T(8,128)(2,1)}, bf16[1536,256]{1,0:T(8,128)(2,1)}, u32[]{:S(2)}, u32[]{:S(2)}) collective-permute-start(bf16[1536,256]{1,0:T(8,128)(2,1)} %pad_maximum_fusion), channel_id=1, source_target_pairs={{0,4},{4,0},{8,12},{12,8},{16,20},{20,16},{24,28},{28,24},{1,5},{5... | collective-permute-start | bytes 2359304 | tf_op jit(solution)/shard_map/ppermute | solution.py:228
  191.9 17.8 %collective-permute-start.12 = (bf16[8,64,256]{2,1,0:T(8,128)(2,1)S(1)}, bf16[8,64,256]{2,1,0:T(8,128)(2,1)S(1)}, u32[]{:S(2)}, u32[]{:S(2)}) collective-permute-start(bf16[8,64,256]{2,1,0:T(8,128)(2,1)S(1)} %copy-done.13), channel_id=1, source_target_pairs={{0,1},{1,2},{2,3},{4,5},{5,6},{6,7},{8,9},{9,10},{10,11},{12,13},{... | collective-permute-start | bytes 786440 | tf_op jit(solution)/shard_map/ppermute | solution.py:205
  195.9 13.8 %collective-permute-start.13 = (bf16[8,64,256]{2,1,0:T(8,128)(2,1)S(1)}, bf16[8,64,256]{2,1,0:T(8,128)(2,1)S(1)}, u32[]{:S(2)}, u32[]{:S(2)}) collective-permute-start(bf16[8,64,256]{2,1,0:T(8,128)(2,1)S(1)} %copy-done.11), channel_id=1, source_target_pairs={{1,0},{2,1},{3,2},{5,4},{6,5},{7,6},{9,8},{10,9},{11,10},{13,12},{... | collective-permute-start | bytes 786440 | tf_op jit(solution)/shard_map/ppermute | solution.py:205
  199.6 1.6 copy-start.2
  201.2 8.6 %copy-start.7 = (bf16[3,3,256,256]{3,2,1,0:T(8,128)(2,1)S(1)}, bf16[3,3,256,256]{3,2,1,0:T(8,128)(2,1)}, u32[]{:S(2)}) copy-start(bf16[3,3,256,256]{3,2,1,0:T(8,128)(2,1)} %copy.13) | copy-start | bytes 3538948
  201.2 8.6 %copy-start.19 = (bf16[8,512,256]{2,1,0:T(8,128)(2,1)S(1)}, bf16[8,512,256]{2,1,0:T(8,128)(2,1)}, u32[]{:S(2)}) copy-start(bf16[8,512,256]{2,1,0:T(8,128)(2,1)} %copy-done.18) | copy-start | bytes 6291460
  209.7 7.1 %copy-start.22 = (bf16[384,256]{1,0:T(8,128)(2,1)S(1)}, bf16[384,256]{1,0:T(8,128)(2,1)}, u32[]{:S(2)}) copy-start(bf16[384,256]{1,0:T(8,128)(2,1)} %copy-done.21) | copy-start | bytes 589828
  209.8 7.1 %copy-start.24 = (bf16[384,256]{1,0:T(8,128)(2,1)S(1)}, bf16[384,256]{1,0:T(8,128)(2,1)}, u32[]{:S(2)}) copy-start(bf16[384,256]{1,0:T(8,128)(2,1)} %copy-done.23) | copy-start | bytes 589828
  209.8 7.1 %copy-start.26 = (bf16[384,256]{1,0:T(8,128)(2,1)S(1)}, bf16[384,256]{1,0:T(8,128)(2,1)}, u32[]{:S(2)}) copy-start(bf16[384,256]{1,0:T(8,128)(2,1)} %copy-done.25) | copy-start | bytes 589828
  209.8 7.1 %copy-start.28 = (bf16[384,256]{1,0:T(8,128)(2,1)S(1)}, bf16[384,256]{1,0:T(8,128)(2,1)}, u32[]{:S(2)}) copy-start(bf16[384,256]{1,0:T(8,128)(2,1)} %copy-done.27) | copy-start | bytes 589828

commit v2 on v1

v2 whole, which is shorter than its diff:
```python
import functools

import jax
import jax.numpy as jnp
from jax import lax
from jax.experimental import pallas as pl
from jax.experimental.pallas import tpu as pltpu
from jax.sharding import PartitionSpec as P

GROUPS = 32
NORM_EPS = 1e-05
BF16 = jnp.bfloat16
F32 = jnp.float32
VMEM_LIMIT = 24 * 2**20


def params():
    return pltpu.CompilerParams(
        vmem_limit_bytes=VMEM_LIMIT, dimension_semantics=("arbitrary",)
    )


def light():
    return pl.CostEstimate(flops=1000, bytes_accessed=1000, transcendentals=0)


def dot(a, b):
    return jnp.dot(a, b, preferred_element_type=F32)


def dot_rows(a, b):
    return lax.dot_general(a, b, (((0,), (0,)), ((), ())), preferred_element_type=F32)


def group_total(row, group_size):
    channels = row.shape[-1]
    lane = lax.broadcasted_iota(jnp.int32, row.shape, 1)
    step = 1
    while step < group_size:
        up = pltpu.roll(row, channels - step, axis=1)
        down = pltpu.roll(row, step, axis=1)
        row = row + jnp.where((lane & step) == 0, up, down)
        step *= 2
    return row


def frame_stats(part_refs, b, entries, group_size):
    total = part_refs[0][b]
    for ref in part_refs[1:]:
        total = total + ref[b]
    return group_total(total, group_size) / entries


def sigmoid(x):
    return 0.5 * jnp.tanh(0.5 * x) + 0.5


def mean_and_inv(part_refs, b, entries, group_size):
    both = frame_stats(part_refs, b, entries, group_size)
    mean = both[0:1]
    inv = lax.rsqrt(both[1:2] - mean * mean + NORM_EPS)
    return mean, inv


def column_sums(first, second, out_ref, b=0):
    out_ref[b, 0:1, :] = jnp.sum(first, axis=0, keepdims=True)
    out_ref[b, 1:2, :] = jnp.sum(second, axis=0, keepdims=True)


def with_halo(above_ref, mid, below_ref):
    width, channels = above_ref.shape[-2:]
    return jnp.concatenate(
        [above_ref[...].reshape(width, channels), mid, below_ref[...].reshape(width, channels)],
        axis=0,
    )


def from_left(y, width):
    col = lax.broadcasted_iota(jnp.int32, y.shape, 0) & (width - 1)
    return jnp.where(col == 0, 0.0, pltpu.roll(y, 1, axis=0))


def from_right(y, width):
    col = lax.broadcasted_iota(jnp.int32, y.shape, 0) & (width - 1)
    return jnp.where(col == width - 1, 0.0, pltpu.roll(y, y.shape[0] - 1, axis=0))


def slot_sources(clip_ref, dil_ref, first, local, frames):
    slot = first + local
    start1 = clip_ref[0]
    filled = start1 + clip_ref[1]
    in_first = slot < start1
    d = jnp.where(in_first, dil_ref[0], dil_ref[1])
    low = jnp.where(in_first, 0, start1)
    high = jnp.where(in_first, start1, filled)
    used = slot < filled
    later, earlier = local + d, local - d
    later_live = used & (slot + d < high)
    earlier_live = used & (slot - d >= low)
    later_which = jnp.where(later_live, jnp.where(later < frames, 1, 2), 0)
    earlier_which = jnp.where(earlier_live, jnp.where(earlier >= 0, 1, 2), 0)
    return (later, later_which), (earlier, earlier_which), used


def conv_kernel(x_ref, above_ref, below_ref, w_ref, out_ref, sums_ref):
    _, rows, width, channels = x_ref.shape
    pixels = rows * width
    padded = with_halo(above_ref, x_ref[...].reshape(pixels, channels), below_ref)
    lhs = jnp.concatenate([padded[i * width : i * width + pixels] for i in range(3)], axis=1)
    y = [dot(lhs, w_ref[:, j].reshape(3 * channels, channels)) for j in range(3)]
    out = y[1] + from_left(y[0], width) + from_right(y[2], width)
    out_ref[0] = out
    column_sums(out, out * out, sums_ref)


def act_kernel(n, entries, group_size, first_ref, clip_ref, dil_ref, *refs):
    parts, (conv_ref, gain_ref, shift_ref, act_ref, normed_ref, slope_ref) = refs[:n], refs[n:]
    step = conv_ref.shape[0]
    for b in range(step):
        mean, inv = mean_and_inv(parts, b, entries, group_size)
        normed = (conv_ref[b] - mean) * inv
        shaped = normed * gain_ref[...] + shift_ref[...]
        sig = sigmoid(shaped)
        slot = first_ref[0] + pl.program_id(0) * step + b
        used = slot < clip_ref[0] + clip_ref[1]
        act_ref[b] = jnp.where(used, shaped * sig, 0.0).astype(BF16)
        normed_ref[b] = normed
        slope_ref[b] = sig * (1.0 + shaped * (1.0 - sig)) * gain_ref[...]


def transpose_kernel(x_ref, above_ref, below_ref, out_ref):
    step, rows, width, channels = x_ref.shape
    pixels = rows * width
    for b in range(step):
        padded = with_halo(above_ref.at[b], x_ref[b].reshape(pixels, channels), below_ref.at[b])
        for i in range(3):
            out_ref[i, :, b * pixels : (b + 1) * pixels] = padded[i * width : i * width + pixels].T


def gather_taps(frames, scalars, own_up, nxt_a, nxt_b, mid, own_dn, prv_a, prv_b, cat_ref, up_slot):
    first_ref, clip_ref, dil_ref = scalars
    later, earlier, used = slot_sources(clip_ref, dil_ref, first_ref[0], pl.program_id(0), frames)
    channels = mid.shape[-1]
    half = frames // 2

    def put(slot, ref):
        cat_ref[:, slot * channels : (slot + 1) * channels] = ref[0]

    def clear(slot):
        cat_ref[:, slot * channels : (slot + 1) * channels] = jnp.zeros(
            (cat_ref.shape[0], channels), cat_ref.dtype
        )

    for slot, (index, which), own, low, high, shift in (
        (up_slot, later, own_up, nxt_a, nxt_b, -frames),
        (2 - up_slot, earlier, own_dn, prv_a, prv_b, frames),
    ):
        in_low = index + shift < half
        pl.when(which == 1)(functools.partial(put, slot, own))
        pl.when((which == 2) & in_low)(functools.partial(put, slot, low))
        pl.when((which == 2) & jnp.logical_not(in_low))(functools.partial(put, slot, high))
        pl.when(which == 0)(functools.partial(clear, slot))
    pl.when(used)(functools.partial(put, 1, mid))
    pl.when(jnp.logical_not(used))(functools.partial(clear, 1))


def grad_act_kernel(frames, *refs):
    scalars, taps = refs[:3], refs[3:10]
    tw_ref, normed_ref, slope_ref, gn_ref, sums_ref, cat_ref = refs[10:]
    gather_taps(frames, scalars, *taps, cat_ref, 0)
    grad_act = dot(cat_ref[...], tw_ref[...]).astype(BF16).astype(F32)
    gn = grad_act * slope_ref[0]
    gn_ref[0] = gn
    column_sums(gn, gn * normed_ref[0], sums_ref)


def temporal_grad_kernel(frames, *refs):
    scalars, taps = refs[:3], refs[3:10]
    act_ref, out_ref, cat_ref = refs[10:]
    channels = act_ref.shape[-1]
    gather_taps(frames, scalars, *taps, cat_ref, 0)
    part = dot_rows(act_ref[0], cat_ref[...])

    @pl.when(pl.program_id(0) == 0)
    def _():
        out_ref[...] = jnp.zeros_like(out_ref)

    for k in range(3):
        out_ref[k] += part[:, k * channels : (k + 1) * channels]


def weight_grad_kernel(n, entries, group_size, core_ref, xt_ref, normed_ref, gn_ref, temporal_ref, *refs):
    parts, grad_parts = refs[:n], refs[n : 2 * n]
    g_ref, first_ref, last_ref, send_ref, keep_ref, moved_ref, acc_ref = refs[2 * n :]
    step, pixels, channels = normed_ref.shape
    width = first_ref.shape[1]
    for b in range(step):
        _, inv = mean_and_inv(parts, b, entries, group_size)
        means = frame_stats(grad_parts, b, entries, group_size)
        wide = inv * (gn_ref[b] - means[0:1] - normed_ref[b] * means[1:2])
        grad = wide.astype(BF16)
        g_ref[b] = grad
        first_ref[b] = grad[:width]
        last_ref[b] = grad[pixels - width :]
        here = slice(b * pixels, (b + 1) * pixels)
        moved_ref[here, :channels] = from_right(wide, width).astype(BF16)
        moved_ref[here, channels : 2 * channels] = grad
        moved_ref[here, 2 * channels :] = from_left(wide, width).astype(BF16)

    at = pl.program_id(0)
    for i in range(3):
        part = dot(xt_ref[i], moved_ref[...])

        @pl.when(at == 0)
        def _():
            acc_ref[i] = part

        @pl.when(at > 0)
        def _():
            acc_ref[i] += part

    @pl.when(at == pl.num_programs(0) - 1)
    def _():
        half = channels // 2
        kept = pl.multiple_of(core_ref[0] * half, half)
        sent = pl.multiple_of((1 - core_ref[0]) * half, half)
        for i in range(3):
            for j in range(3):
                lanes = slice(j * channels, (j + 1) * channels)
                keep_ref[3 * i + j] = acc_ref[i, pl.ds(kept, half), lanes]
                send_ref[3 * i + j] = acc_ref[i, pl.ds(sent, half), lanes].astype(BF16)
        for k in range(3):
            keep_ref[9 + k] = temporal_ref[k, pl.ds(kept, half), :]
            send_ref[9 + k] = temporal_ref[k, pl.ds(sent, half), :].astype(BF16)


def conv_back_kernel(g_ref, above_ref, below_ref, cot_ref, w_ref, out_ref):
    _, rows, width, channels = cot_ref.shape
    pixels = rows * width
    padded = with_halo(above_ref, g_ref[0], below_ref)
    lhs = jnp.concatenate([padded[(2 - i) * width : (2 - i) * width + pixels] for i in range(3)], axis=1)
    z = [dot(lhs, w_ref[j]) for j in range(3)]
    out = z[1] + from_right(z[0], width) + from_left(z[2], width)
    out = out + cot_ref[...].reshape(pixels, channels).astype(F32)
    out_ref[...] = out.astype(BF16).reshape(out_ref.shape)


def out_kernel(frames, *refs):
    scalars, taps = refs[:3], refs[3:10]
    tw_ref, x_ref, out_ref, cat_ref = refs[10:]
    gather_taps(frames, scalars, *taps, cat_ref, 2)
    _, rows, width, channels = x_ref.shape
    temporal_out = dot(cat_ref[...], tw_ref[...]).astype(BF16).astype(F32)
    out = x_ref[...].reshape(rows * width, channels).astype(F32) + temporal_out
    out_ref[...] = out.astype(BF16).reshape(out_ref.shape)


def neighbours(axis, low, high):
    size = lax.axis_size(axis)
    up = [(i, i + 1) for i in range(size - 1)]
    down = [(j, i) for i, j in up]
    return lax.ppermute(high, axis, up), lax.ppermute(low, axis, down)


def frame_neighbours(x):
    size, frames = lax.axis_size("tm"), x.shape[0]
    low, high = x[: frames // 2], x[frames // 2 :]
    prev_low, next_low = neighbours("tm", low, low)
    if size != 8:
        prev_high, next_high = neighbours("tm", high, high)
        return (prev_low, prev_high), (next_low, next_high)
    relayed = lax.ppermute(high, "tm", [(3, 7), (4, 0)])
    me = lax.axis_index("tm")
    up = [(i, i + 1) for i in range(7) if i != 3] + [(7, 4)]
    down = [(i + 1, i) for i in range(7) if i != 3] + [(0, 3)]
    prev_high = lax.ppermute(jnp.where(me == 7, relayed, high), "tm", up)
    next_high = lax.ppermute(jnp.where(me == 0, relayed, high), "tm", down)
    return (prev_low, prev_high), (next_low, next_high)


def spread_parts(part, axis):
    size = lax.axis_size(axis)
    return [part] + [
        lax.ppermute(part, axis, [(i, (i + s) % size) for i in range(size)]) for s in range(1, size)
    ]


def scatter_sum(x, axis, me, count, pairs):
    block = x.shape[1] // count

    def take(k):
        return lax.dynamic_slice_in_dim(x, k * block, block, 1)

    total = take(me)
    got = [lax.ppermute(take(me ^ s).astype(BF16), axis, pairs(s)) for s in range(1, count)]
    for g in got:
        total = total + g.astype(F32)
    return total


def gather_blocks(x, axis, me, count, pairs):
    out = jnp.zeros((count,) + x.shape, x.dtype)
    got = [(me, x)] + [(me ^ s, lax.ppermute(x, axis, pairs(s))) for s in range(1, count)]
    for k, g in got:
        out = lax.dynamic_update_index_in_dim(out, g, k, 0)
    return out


def sum_everywhere(send, keep):
    tm, n = lax.axis_size("tm"), lax.axis_size("space")
    chips = tm // 2
    me = lax.axis_index("tm")
    core, chip, deep = me & 1, me >> 1, lax.axis_index("space")
    other_core = [(i, i ^ 1) for i in range(tm)]

    def in_plane(s):
        return [(i, i ^ (2 * s)) for i in range(tm)]

    def in_line(s):
        return [(i, i ^ s) for i in range(n)]

    x = keep + lax.ppermute(send, "tm", other_core).astype(F32)
    x = scatter_sum(x, "tm", chip, chips, in_plane)
    x = scatter_sum(x, "space", deep, n, in_line).astype(BF16)
    x = gather_blocks(x, "space", deep, n, in_line)
    x = gather_blocks(x, "tm", chip, chips, in_plane)
    got = lax.ppermute(x, "tm", other_core)
    both = jnp.stack([jnp.where(core == 0, x, got), jnp.where(core == 0, got, x)])
    tiles, channels = send.shape[0], send.shape[2]
    return both.transpose(3, 0, 1, 2, 4, 5).reshape(tiles, channels, channels).astype(F32)


def per_device(frames_in, cotangent, spatial, temporal, norm_gain, norm_shift, clip_frames, dilation):
    frames, rows, width, channels = frames_in.shape
    pixels = rows * width
    n = lax.axis_size("space")
    group_size = channels // GROUPS
    entries = float(rows * n * width * group_size)
    gain, shift = norm_gain[None], norm_shift[None]
    me = lax.axis_index("tm").astype(jnp.int32)
    scalars = ((me * frames)[None], clip_frames, dilation)
    half = frames // 2

    def per_frame(*dims, step=1):
        return pl.BlockSpec((step,) + dims, lambda f, *_: (f,) + (0,) * len(dims))

    def whole(*dims):
        return pl.BlockSpec(dims, lambda f, *_: (0,) * len(dims))

    x_spec, px_spec = per_frame(rows, width, channels), per_frame(pixels, channels)
    edge_spec, row_spec = per_frame(1, width, channels), per_frame(width, channels)
    sum_spec = per_frame(2, channels)
    chan_spec = whole(1, channels)

    def tap(side, which, low, count, offset):
        def index(f, first_ref, clip_ref, dil_ref):
            found = slot_sources(clip_ref, dil_ref, first_ref[0], f, frames)[side][0]
            return (jnp.clip(found + offset - low, 0, count - 1), 0, 0)

        return pl.BlockSpec((1, pixels, channels), index)

    taps = [
        tap(0, 1, 0, frames, 0), tap(0, 2, 0, half, -frames), tap(0, 2, half, half, -frames),
        px_spec,
        tap(1, 1, 0, frames, 0), tap(1, 2, 0, half, frames), tap(1, 2, half, half, frames),
    ]
    cat = pltpu.VMEM((pixels, 3 * channels), BF16)
    shape = jax.ShapeDtypeStruct

    def call(kernel, name, grid, in_specs, out_specs, out_shape, prefetch=0, scratch=()):
        return pl.pallas_call(
            kernel,
            grid_spec=pltpu.PrefetchScalarGridSpec(
                num_scalar_prefetch=prefetch,
                grid=(grid,),
                in_specs=in_specs,
                out_specs=out_specs,
                scratch_shapes=list(scratch),
            ),
            out_shape=out_shape,
            compiler_params=params(),
            cost_estimate=light(),
            name=name,
        )

    def around(mid, prev, nxt):
        return (mid, *nxt, mid, mid, *prev)

    above, below = neighbours("space", frames_in[:, :1], frames_in[:, rows - 1 :])
    cot = cotangent.reshape(frames, pixels, channels)
    cot_taps = around(cot, *frame_neighbours(cot))

    conv_out, sums = call(
        conv_kernel, "conv_forward", frames,
        [x_spec, edge_spec, edge_spec, whole(3, 3, channels, channels)],
        [px_spec, sum_spec],
        [shape((frames, pixels, channels), F32), shape((frames, 2, channels), F32)],
    )(frames_in, above, below, spatial)
    parts = spread_parts(sums, "space")

    pair_px, pair_sum = per_frame(pixels, channels, step=2), per_frame(2, channels, step=2)
    act, normed, slope = call(
        functools.partial(act_kernel, n, entries, group_size), "activation", frames // 2,
        [pair_sum] * n + [pair_px, chan_spec, chan_spec],
        [pair_px] * 3,
        [shape((frames, pixels, channels), t) for t in (BF16, F32, F32)],
        prefetch=3,
    )(*scalars, *parts, conv_out, gain, shift)
    act_taps = around(act, *frame_neighbours(act))

    pair_edge = per_frame(1, width, channels, step=2)
    x_turned = call(
        transpose_kernel, "turn_windows", frames // 2,
        [per_frame(rows, width, channels, step=2), pair_edge, pair_edge],
        pl.BlockSpec((3, channels, 2 * pixels), lambda f, *_: (0, 0, f)),
        shape((3, channels, frames * pixels), BF16),
    )(frames_in, above, below)

    grad_normed, grad_sums = call(
        functools.partial(grad_act_kernel, frames), "grad_activation", frames,
        taps + [whole(3 * channels, channels), px_spec, px_spec],
        [px_spec, sum_spec],
        [shape((frames, pixels, channels), F32), shape((frames, 2, channels), F32)],
        prefetch=3, scratch=[cat],
    )(*scalars, *cot_taps, temporal.transpose(0, 2, 1).reshape(3 * channels, channels), normed, slope)
    grad_parts = spread_parts(grad_sums, "space")

    temporal_part = call(
        functools.partial(temporal_grad_kernel, frames), "temporal_grad", frames,
        taps + [px_spec], whole(3, channels, channels), shape((3, channels, channels), F32),
        prefetch=3, scratch=[cat],
    )(*scalars, *cot_taps, act)

    halves = (12, channels // 2, channels)
    grad_conv, first_rows, last_rows, send, keep = call(
        functools.partial(weight_grad_kernel, n, entries, group_size), "weight_grad", frames // 2,
        [pl.BlockSpec((3, channels, 2 * pixels), lambda f, *_: (0, 0, f)), pair_px, pair_px, whole(3, channels, channels)]
        + [pair_sum] * (2 * n),
        [pair_px, per_frame(width, channels, step=2), per_frame(width, channels, step=2), whole(*halves), whole(*halves)],
        [
            shape((frames, pixels, channels), BF16),
            shape((frames, width, channels), BF16),
            shape((frames, width, channels), BF16),
            shape(halves, BF16),
            shape(halves, F32),
        ],
        prefetch=1,
        scratch=[pltpu.VMEM((2 * pixels, 3 * channels), BF16), pltpu.VMEM((3, channels, 3 * channels), F32)],
    )((me & 1)[None], x_turned, normed, grad_normed, temporal_part, *parts, *grad_parts)

    total = sum_everywhere(send, keep)

    grad_above, grad_below = neighbours("space", first_rows, last_rows)
    back_weights = spatial.transpose(1, 0, 3, 2).reshape(3, 3 * channels, channels)
    in_grad = call(
        conv_back_kernel, "conv_backward", frames,
        [px_spec, row_spec, row_spec, x_spec, whole(3, 3 * channels, channels)],
        x_spec, shape(frames_in.shape, BF16),
    )(grad_conv, grad_above, grad_below, cotangent, back_weights)

    out_frames = call(
        functools.partial(out_kernel, frames), "temporal_forward", frames,
        taps + [whole(3 * channels, channels), x_spec], x_spec, shape(frames_in.shape, BF16),
        prefetch=3, scratch=[cat],
    )(*scalars, *act_taps, temporal.reshape(3 * channels, channels), frames_in)

    return (out_frames, in_grad, total[:9].reshape(spatial.shape), total[9:])


def solution(mesh):
    tiles = P("tm", "space", None, None)
    return jax.shard_map(
        per_device,
        mesh=mesh,
        in_specs=(tiles, tiles, P(), P(), P(), P(), P(), P()),
        out_specs=(tiles, tiles, P(), P()),
        check_vma=False,
    )
```

time: 222 us -> 247 us (1.11)
  local copies, waits for them, and re-layouts: 15.6 us -> 42.4 us
  starting transfers between devices: 52.4 us -> 63.2 us
  other arithmetic: 16.3 us -> 10.6 us
  Pallas kernels: 62.4 us -> 59 us
    ppermute x18 -> x20, waiting for transfers between devices: 68.1 us -> 39.3 us  [the longest x6 19.6 us: scatter_sum(): lax.ppermute(take(me ^ s).astype(BF16), axis, pairs(s))]
    unnamed x58 -> x104, local copies, waits for them, and re-layouts: 6.83 us -> 27.3 us
    ppermute x8, waiting for transfers between devices: 0.02 us -> 20.3 us  [neighbours(): return (lax.ppermute(high, axis, up), lax.ppermute(low, axis, down))]
    ppermute x18 -> x20, starting transfers between devices: 24.4 us -> 34.8 us  [the longest x6 10.5 us: gather_blocks(): lax.ppermute(x, axis, pairs(s))]
    ppermute x6, waiting for transfers between devices: 3.69 us -> 10 us  [spread_parts(): lax.ppermute(part, axis, [(i, (i + s) % size) for i in range(size)])]
    min x2 -> x0, other arithmetic: 3.91 us -> none  [the longest x1 1.96 us: slot_info(): jnp.clip(up - frames, 0, last)]
    slice x4 -> x7, local copies, waits for them, and re-layouts: 4.29 us -> 8.07 us  [the longest x2 5.16 us: frame_neighbours(): low, high = (x[:frames // 2], x[frames // 2:])]
    pallas_call x7 -> x8, Pallas kernels: 62.4 us -> 59 us  [the longest x1 12.9 us: per_device(): call(functools.partial(weight_grad_kernel, n, entries, group_size), 'weig...]
  transfers between devices with their start and end apart: 32 -> 34, of which waited for: 17 -> 14; matrix products, arithmetic and copies ran while one was open for 7% -> 7% of each run, Pallas kernels for 17% -> 15%
where the time goes in v2:
time: 247 us; the launch traced here: 246 us
  waiting for transfers between devices  69.6 us (28%)
  starting transfers between devices  63.2 us (26%)
  Pallas kernels  59 us (24%)
  local copies, waits for them, and re-layouts  42.4 us (17%)
  other arithmetic  10.6 us (4%)
    unnamed x104, local copies, waits for them, and re-layouts  27.3 us
    ppermute x8, starting transfers between devices, neighbours(): return (lax.ppermute(high, axis, up), lax.ppermute(low, axis, down))  21.5 us
    ppermute x8, waiting for transfers between devices, neighbours(): return (lax.ppermute(high, axis, up), lax.ppermute(low, axis, down))  20.3 us
    ppermute x6, waiting for transfers between devices, scatter_sum(): lax.ppermute(take(me ^ s).astype(BF16), axis, pairs(s))  19.6 us
    pallas_call x1, Pallas kernels, per_device(): call(functools.partial(weight_grad_kernel, n, entries, group_size), 'weig...  12.9 us
    ppermute x6, starting transfers between devices, gather_blocks(): lax.ppermute(x, axis, pairs(s))  10.5 us
    ppermute x2, waiting for transfers between devices, frame_neighbours(): relayed = lax.ppermute(high, 'tm', [(3, 7), (4, 0)])  10.4 us
    ppermute x6, waiting for transfers between devices, spread_parts(): lax.ppermute(part, axis, [(i, (i + s) % size) for i in range(size)])  10 us
  transfers between devices with their start and end apart: 34, of which 14 were waited for; matrix products, arithmetic and copies ran while one was open for 7% of the time, Pallas kernels for 15%

profile of v2, /device:TPU:0, one launch (start us, length us, event | category | flops | bytes accessed | tf_op | source)
XLA Modules:
  0.0 246.1 jit_solution(10806867209297086485)
XLA Ops:
  0.6 2.8 %fusion = (bf16[4,8,64,256]{3,2,1,0:T(8,128)(2,1)S(1)}, bf16[4,8,64,256]{3,2,1,0:T(8,128)(2,1)}) fusion(bf16[8,8,64,256]{3,2,1,0:T(8,128)(2,1)} %cot_ref.1), kind=kLoop, calls=%fused_computation.24 | loop fusion | bytes 4194304 | tf_op jit(solution)/shard_map/slice | solution.py:267
  3.4 1.3 collective-permute-start.11
  4.7 1.3 collective-permute-start.10
  6.0 4.0 %collective-permute-start.13 = (bf16[4,512,256]{2,1,0:T(8,128)(2,1)}, bf16[4,512,256]{2,1,0:T(8,128)(2,1)}, u32[]{:S(2)}, u32[]{:S(2)}) collective-permute-start(bf16[4,512,256]{2,1,0:T(8,128)(2,1)} %bitcast.6), channel_id=1, source_target_pairs={{0,4},{4,8},{8,12},{12,16},{16,20},{20,24},{24,28},{1,5},{5,9},{9,... | collective-permute-start | bytes 3145736 | tf_op jit(solution)/shard_map/ppermute | solution.py:262
  10.0 10.4 %collective-permute-done.11 = bf16[4,512,256]{2,1,0:T(8,128)(2,1)S(1)} collective-permute-done((bf16[4,512,256]{2,1,0:T(8,128)(2,1)S(1)}, bf16[4,512,256]{2,1,0:T(8,128)(2,1)S(1)}, u32[]{:S(2)}, u32[]{:S(2)}) %collective-permute-start.11) | collective-permute-done | bytes 1048608 | tf_op jit(solution)/shard_map/ppermute | solution.py:272
  20.4 1.5 broadcast_select_fusion
  21.9 2.1 collective-permute-start.12
  24.1 3.2 %collective-permute-start.14 = (bf16[4,512,256]{2,1,0:T(8,128)(2,1)}, bf16[4,512,256]{2,1,0:T(8,128)(2,1)}, u32[]{:S(2)}, u32[]{:S(2)}) collective-permute-start(bf16[4,512,256]{2,1,0:T(8,128)(2,1)} %get-tuple-element.32), channel_id=1, source_target_pairs={{0,4},{4,8},{8,12},{16,20},{20,24},{24,28},{28,16},{1,5},{5,9},{9,... | collective-permute-start | bytes 3145736 | tf_op jit(solution)/shard_map/ppermute | solution.py:276
  27.3 4.7 %collective-permute-start = (bf16[8,1,64,256]{3,2,1,0:T(8,128)(2,1)S(1)}, bf16[8,1,64,256]{3,2,1,0:T(8,128)(2,1)S(1)}, u32[]{:S(2)}, u32[]{:S(2)}) collective-permute-start(bf16[8,1,64,256]{3,2,1,0:T(8,128)(2,1)S(1)} %get-tuple-element.38), channel_id=1, source_target_pairs={{0,1},{1,2},{2,3},{4,5},{5,6},{6,7},{8,9},{9,10},{10,11},{12,13},{... | collective-permute-start | bytes 786440 | tf_op jit(solution)/shard_map/ppermute | solution.py:262
  32.1 4.7 %collective-permute-done.above_ref = bf16[8,1,64,256]{3,2,1,0:T(8,128)(2,1)S(1)} collective-permute-done((bf16[8,1,64,256]{3,2,1,0:T(8,128)(2,1)S(1)}, bf16[8,1,64,256]{3,2,1,0:T(8,128)(2,1)S(1)}, u32[]{:S(2)}, u32[]{:S(2)}) %collective-permute-start) | collective-permute-done | bytes 262176 | tf_op jit(solution)/shard_map/ppermute | solution.py:262
  36.8 1.3 collective-permute-start.1
  38.1 7.7 %collective-permute-done.1.below_ref = bf16[8,1,64,256]{3,2,1,0:T(8,128)(2,1)S(1)} collective-permute-done((bf16[8,1,64,256]{3,2,1,0:T(8,128)(2,1)S(1)}, bf16[8,1,64,256]{3,2,1,0:T(8,128)(2,1)S(1)}, u32[]{:S(2)}, u32[]{:S(2)}) %collective-permute-start.1) | collective-permute-done | bytes 262176 | tf_op jit(solution)/shard_map/ppermute | solution.py:262
  45.8 6.4 %conv_forward.1 = (f32[8,512,256]{2,1,0:T(8,128)S(1)}, f32[8,2,256]{2,1,0:T(2,128)S(1)}) custom-call(bf16[8,8,64,256]{3,2,1,0:T(8,128)(2,1)S(1)} %copy-done.4, bf16[8,1,64,256]{3,2,1,0:T(8,128)(2,1)S(1)} %collective-permute-done.above_ref, bf16[8,1,64,256]{3,2,1,0:T(8,128)(2,1)S(1)} %collective-permute-done.1.below_ref, bf16[3,3,256,256]{3,2,1,0:T(8,128)(2,1)S(1)} %copy-done.9), custom_call_target="tpu_custom_call" | custom-call | flops 1000 | bytes 1000 | tf_op jit(solution)/shard_map/conv_forward/pallas_call | solution.py:393
  52.2 2.0 copy-done.13
  54.2 1.8 collective-permute-start.2
  56.0 3.8 %collective-permute-done.2.refs_1_ = f32[8,2,256]{2,1,0:T(2,128)S(1)} collective-permute-done((f32[8,2,256]{2,1,0:T(2,128)S(1)}, f32[8,2,256]{2,1,0:T(2,128)S(1)}, u32[]{:S(2)}, u32[]{:S(2)}) %collective-permute-start.2) | collective-permute-done | bytes 16416 | tf_op jit(solution)/shard_map/ppermute | solution.py:284
  60.8 3.7 %collective-permute-done.3.refs_2_ = f32[8,2,256]{2,1,0:T(2,128)S(1)} collective-permute-done((f32[8,2,256]{2,1,0:T(2,128)S(1)}, f32[8,2,256]{2,1,0:T(2,128)S(1)}, u32[]{:S(2)}, u32[]{:S(2)}) %collective-permute-start.3) | collective-permute-done | bytes 16416 | tf_op jit(solution)/shard_map/ppermute | solution.py:284
  65.8 2.4 collective-permute-done.4.refs_3_
  68.8 2.2 copy-done.14
  75.9 5.0 %activation.1 = (bf16[8,512,256]{2,1,0:T(8,128)(2,1)S(1)}, f32[8,512,256]{2,1,0:T(8,128)S(1)}, f32[8,512,256]{2,1,0:T(8,128)S(1)}) custom-call(s32[1]{0:T(128)} %bitcast.first_ref.refs_0_, s32[2]{0:T(128)S(1)} %copy-done.35, s32[2]{0:T(128)S(1)} %copy-done.39, f32[8,2,256]{2,1,0:T(2,128)S(1)} %get-tuple-element.16.refs_0_, f32[8,2,256]{2,1,0:T(2,128)S(1)} %copy-done.27, ...), custom_call_target="tpu_custom_call" | custom-call | flops 1000 | bytes 1000 | tf_op jit(solution)/shard_map/activation/pallas_call | solution.py:402
  80.9 1.3 copy-done.1
  82.2 8.9 %grad_activation.1 = (f32[8,512,256]{2,1,0:T(8,128)S(1)}, f32[8,2,256]{2,1,0:T(2,128)}) custom-call(s32[1]{0:T(128)} %bitcast.first_ref.refs_0_, s32[2]{0:T(128)S(1)} %copy-done.36, s32[2]{0:T(128)S(1)} %copy-done.40, bf16[8,512,256]{2,1,0:T(8,128)(2,1)S(1)} %bitcast.38, bf16[4,512,256]{2,1,0:T(8,128)(2,1)} %collective-permute-done.10.refs_4_, ...), custom_call_target="tpu_custom_call" | custom-call | flops 1000 | bytes 1000 | tf_op jit(solution)/shard_map/grad_activation/pallas_call | solution.py:419
  91.1 2.0 copy-done.11
  93.1 2.8 %collective-permute-start.16 = (f32[8,2,256]{2,1,0:T(2,128)}, f32[8,2,256]{2,1,0:T(2,128)}, u32[]{:S(2)}, u32[]{:S(2)}) collective-permute-start(f32[8,2,256]{2,1,0:T(2,128)} %get-tuple-element.22.refs_4_), channel_id=1, source_target_pairs={{0,2},{1,3},{2,0},{3,1},{4,6},{5,7},{6,4},{7,5},{8,10},{9,11},{10,... | collective-permute-start | bytes 49160 | tf_op jit(solution)/shard_map/ppermute | solution.py:284
  95.9 1.1 collective-permute-start.17
  97.0 1.6 copy-done.5
  99.5 2.0 turn_windows.1.xt_ref
  101.6 8.4 %temporal_grad.1.temporal_ref = f32[3,256,256]{2,1,0:T(8,128)S(1)} custom-call(s32[1]{0:T(128)} %bitcast.first_ref.refs_0_, s32[2]{0:T(128)S(1)} %copy-done.37, s32[2]{0:T(128)S(1)} %copy-done.41, bf16[8,512,256]{2,1,0:T(8,128)(2,1)S(1)} %bitcast.41, bf16[4,512,256]{2,1,0:T(8,128)(2,1)} %collective-permute-done.10.refs_4_, ...), custom_call_target="tpu_custom_call" | custom-call | flops 1000 | bytes 1000 | tf_op jit(solution)/shard_map/temporal_grad/pallas_call | solution.py:428
  110.1 12.9 %weight_grad.1 = (bf16[8,512,256]{2,1,0:T(8,128)(2,1)S(1)}, bf16[8,64,256]{2,1,0:T(8,128)(2,1)S(1)}, bf16[8,64,256]{2,1,0:T(8,128)(2,1)S(1)}, bf16[12,128,256]{2,1,0:T(8,128)(2,1)}, f32[12,128,256]{2,1,0:T(8,128)S(1)}) custom-call(s32[1]{0:T(128)} %bitcast.4.core_ref, bf16[3,256,4096]{2,1,0:T(8,128)(2,1)S(1)} %turn_windows.1.xt_ref, ...), custom_call_target="tpu_custom_call" | custom-call | flops 1000 | bytes 1000 | tf_op jit(solution)/shard_map/weight_grad/pallas_call | solution.py:435
  123.0 1.3 copy-done.15
  124.4 1.1 copy-done.17
  126.9 2.4 slice.37
  129.3 1.3 collective-permute-start.6
  130.6 1.3 convert_add_fusion
  132.0 1.1 copy-done.50
  133.9 3.6 %collective-permute-start.22 = (bf16[12,32,256]{2,1,0:T(8,128)(2,1)}, bf16[12,32,256]{2,1,0:T(8,128)(2,1)}, u32[]{:S(2)}, u32[]{:S(2)}) collective-permute-start(bf16[12,32,256]{2,1,0:T(8,128)(2,1)} %get-tuple-element.43), channel_id=1, source_target_pairs={{0,16},{4,20},{8,24},{12,28},{16,0},{20,4},{24,8},{28,12},{1,17},{... | collective-permute-start | bytes 589832 | tf_op jit(solution)/shard_map/ppermute | solution.py:295
  137.5 1.5 collective-permute-start.23
  139.0 3.0 %collective-permute-done.21 = bf16[12,32,256]{2,1,0:T(8,128)(2,1)} collective-permute-done((bf16[12,32,256]{2,1,0:T(8,128)(2,1)}, bf16[12,32,256]{2,1,0:T(8,128)(2,1)}, u32[]{:S(2)}, u32[]{:S(2)}) %collective-permute-start.21) | collective-permute-done | bytes 196640 | tf_op jit(solution)/shard_map/ppermute | solution.py:295
  142.0 12.7 %collective-permute-done.22 = bf16[12,32,256]{2,1,0:T(8,128)(2,1)} collective-permute-done((bf16[12,32,256]{2,1,0:T(8,128)(2,1)}, bf16[12,32,256]{2,1,0:T(8,128)(2,1)}, u32[]{:S(2)}, u32[]{:S(2)}) %collective-permute-start.22) | collective-permute-done | bytes 196640 | tf_op jit(solution)/shard_map/ppermute | solution.py:295
  154.8 1.4 convert_add_fusion.1
  158.0 1.1 collective-permute-start.25
  159.1 2.3 collective-permute-start.26
  161.4 1.6 collective-permute-done.25
  163.0 2.2 collective-permute-done.26
  166.8 3.7 %broadcast_select_fusion.1 = (bf16[4,512,256]{2,1,0:T(8,128)(2,1)}, bf16[4,512,256]{2,1,0:T(8,128)(2,1)}, bf16[4,512,256]{2,1,0:T(8,128)(2,1)}) fusion(bf16[4,512,256]{2,1,0:T(8,128)(2,1)} %collective-permute-done.6, pred[]{:T(512)S(6)} %eq.13, bf16[8,512,256]{2,1,0:T(8,128)(2,1)} %copy-done.1, pred[]{:T(512)S(6)} %eq.12), kind=kLoop, calls=%fused_computation.3 | loop fusion | flops 1048576 | bytes 6291458 | tf_op jit(solution)/shard_map/jit(_where)/select_n | solution.py:276
  170.6 1.3 collective-permute-start.5
  171.8 4.0 %collective-permute-start.8 = (bf16[4,512,256]{2,1,0:T(8,128)(2,1)}, bf16[4,512,256]{2,1,0:T(8,128)(2,1)}, u32[]{:S(2)}, u32[]{:S(2)}) collective-permute-start(bf16[4,512,256]{2,1,0:T(8,128)(2,1)} %get-tuple-element.36), channel_id=1, source_target_pairs={{0,4},{4,8},{8,12},{12,16},{16,20},{20,24},{24,28},{1,5},{5,9},{9,... | collective-permute-start | bytes 3145736 | tf_op jit(solution)/shard_map/ppermute | solution.py:262
  175.9 3.4 %collective-permute-start.18 = (bf16[8,64,256]{2,1,0:T(8,128)(2,1)S(1)}, bf16[8,64,256]{2,1,0:T(8,128)(2,1)S(1)}, u32[]{:S(2)}, u32[]{:S(2)}) collective-permute-start(bf16[8,64,256]{2,1,0:T(8,128)(2,1)S(1)} %copy-done.48), channel_id=1, source_target_pairs={{0,1},{1,2},{2,3},{4,5},{5,6},{6,7},{8,9},{9,10},{10,11},{12,13},{... | collective-permute-start | bytes 786440 | tf_op jit(solution)/shard_map/ppermute | solution.py:262
  180.1 2.9 %collective-permute-start.29 = (bf16[12,8,256]{2,1,0:T(8,128)(2,1)S(1)}, bf16[12,8,256]{2,1,0:T(8,128)(2,1)S(1)}, u32[]{:S(2)}, u32[]{:S(2)}) collective-permute-start(bf16[12,8,256]{2,1,0:T(8,128)(2,1)S(1)} %get-tuple-element.29), channel_id=1, source_target_pairs={{0,3},{1,2},{2,1},{3,0},{4,7},{5,6},{6,5},{7,4},{8,11},{9,10},{10,... | collective-permute-start | bytes 147464 | tf_op jit(solution)/shard_map/ppermute | solution.py:303
  183.0 2.6 %collective-permute-done.28 = bf16[12,8,256]{2,1,0:T(8,128)(2,1)S(1)} collective-permute-done((bf16[12,8,256]{2,1,0:T(8,128)(2,1)S(1)}, bf16[12,8,256]{2,1,0:T(8,128)(2,1)S(1)}, u32[]{:S(2)}, u32[]{:S(2)}) %collective-permute-start.28) | collective-permute-done | bytes 49184 | tf_op jit(solution)/shard_map/ppermute | solution.py:303
  187.9 6.1 %collective-permute-done.30 = bf16[4,12,8,256]{3,2,1,0:T(8,128)(2,1)S(1)} collective-permute-done((bf16[4,12,8,256]{3,2,1,0:T(8,128)(2,1)S(1)}, bf16[4,12,8,256]{3,2,1,0:T(8,128)(2,1)S(1)}, u32[]{:S(2)}, u32[]{:S(2)}) %collective-permute-start.30) | collective-permute-done | bytes 196640 | tf_op jit(solution)/shard_map/ppermute | solution.py:303
  194.0 6.1 %collective-permute-start.32 = (bf16[4,12,8,256]{3,2,1,0:T(8,128)(2,1)S(1)}, bf16[4,12,8,256]{3,2,1,0:T(8,128)(2,1)S(1)}, u32[]{:S(2)}, u32[]{:S(2)}) collective-permute-start(bf16[4,12,8,256]{3,2,1,0:T(8,128)(2,1)S(1)} %bitcast_dynamic-update-slice_fusion.4), channel_id=1, source_target_pairs={{0,24},{4,28},{8,16},{12,20},{16,8},{20,12},{24,0},{28,4},{1,25},{... | collective-permute-start | bytes 589832 | tf_op jit(solution)/shard_map/ppermute | solution.py:303
  200.8 3.3 %collective-permute-start.7 = (bf16[4,512,256]{2,1,0:T(8,128)(2,1)}, bf16[4,512,256]{2,1,0:T(8,128)(2,1)}, u32[]{:S(2)}, u32[]{:S(2)}) collective-permute-start(bf16[4,512,256]{2,1,0:T(8,128)(2,1)} %get-tuple-element.31), channel_id=1, source_target_pairs={{4,0},{8,4},{12,8},{20,16},{24,20},{28,24},{0,12},{5,1},{9,5},{13,... | collective-permute-start | bytes 3145736 | tf_op jit(solution)/shard_map/ppermute | solution.py:277
  204.1 3.6 %collective-permute-start.9 = (bf16[4,512,256]{2,1,0:T(8,128)(2,1)}, bf16[4,512,256]{2,1,0:T(8,128)(2,1)}, u32[]{:S(2)}, u32[]{:S(2)}) collective-permute-start(bf16[4,512,256]{2,1,0:T(8,128)(2,1)} %get-tuple-element.30), channel_id=1, source_target_pairs={{0,4},{4,8},{8,12},{16,20},{20,24},{24,28},{28,16},{1,5},{5,9},{9,... | collective-permute-start | bytes 3145736 | tf_op jit(solution)/shard_map/ppermute | solution.py:276
  207.7 1.5 collective-permute-start.19
  210.6 7.9 %collective-permute-done.19.below_ref = bf16[8,64,256]{2,1,0:T(8,128)(2,1)S(1)} collective-permute-done((bf16[8,64,256]{2,1,0:T(8,128)(2,1)S(1)}, bf16[8,64,256]{2,1,0:T(8,128)(2,1)S(1)}, u32[]{:S(2)}, u32[]{:S(2)}) %collective-permute-start.19) | collective-permute-done | bytes 262176 | tf_op jit(solution)/shard_map/ppermute | solution.py:262
  219.2 1.5 copy.21
  220.7 1.3 copy-done.10
  222.0 1.6 copy-done.16
  224.5 7.1 %conv_backward.1 = bf16[8,8,64,256]{3,2,1,0:T(8,128)(2,1)} custom-call(bf16[8,512,256]{2,1,0:T(8,128)(2,1)S(1)} %copy-done.16, bf16[8,64,256]{2,1,0:T(8,128)(2,1)S(1)} %collective-permute-done.18.above_ref, bf16[8,64,256]{2,1,0:T(8,128)(2,1)S(1)} %copy-done.25, bf16[8,8,64,256]{3,2,1,0:T(8,128)(2,1)S(1)} %copy-done, bf16[3,768,256]{2,1,0:T(8,128)(2,1)S(1)} %bitcast.45), custom_call_target="tpu_custom_call" | custom-call | flops 1000 | bytes 1000 | tf_op jit(solution)/shard_map/conv_backward/pallas_call | solution.py:455
  231.7 8.4 %temporal_forward.1 = bf16[8,8,64,256]{3,2,1,0:T(8,128)(2,1)} custom-call(s32[1]{0:T(128)} %bitcast.first_ref.refs_0_, s32[2]{0:T(128)S(1)} %copy-done.38, s32[2]{0:T(128)S(1)} %copy-done.42, bf16[8,512,256]{2,1,0:T(8,128)(2,1)S(1)} %copy-done.3, bf16[4,512,256]{2,1,0:T(8,128)(2,1)} %collective-permute-done.5.refs_4_, ...), custom_call_target="tpu_custom_call" | custom-call | flops 1000 | bytes 1000 | tf_op jit(solution)/shard_map/temporal_forward/pallas_call | solution.py:461
  240.1 1.5 select_bitcast_fusion.1
  242.0 1.4 copy-done.49
  243.4 1.7 copy.22
  (144 shorter events, 22.8 us)
Async XLA Ops:
  3.4 17.0 %collective-permute-start.11 = (bf16[4,512,256]{2,1,0:T(8,128)(2,1)S(1)}, bf16[4,512,256]{2,1,0:T(8,128)(2,1)S(1)}, u32[]{:S(2)}, u32[]{:S(2)}) collective-permute-start(bf16[4,512,256]{2,1,0:T(8,128)(2,1)S(1)} %bitcast.51), channel_id=1, source_target_pairs={{12,28},{16,0},{13,29},{17,1},{14,30},{18,2},{15,31},{19,3}} | collective-permute-start | bytes 3145736 | tf_op jit(solution)/shard_map/ppermute | solution.py:272
  4.7 77.5 %collective-permute-start.10 = (bf16[4,512,256]{2,1,0:T(8,128)(2,1)}, bf16[4,512,256]{2,1,0:T(8,128)(2,1)}, u32[]{:S(2)}, u32[]{:S(2)}) collective-permute-start(bf16[4,512,256]{2,1,0:T(8,128)(2,1)} %bitcast.6), channel_id=1, source_target_pairs={{4,0},{8,4},{12,8},{16,12},{20,16},{24,20},{28,24},{5,1},{9,5},{13... | collective-permute-start | bytes 3145736 | tf_op jit(solution)/shard_map/ppermute | solution.py:262
  6.0 76.2 %collective-permute-start.13 = (bf16[4,512,256]{2,1,0:T(8,128)(2,1)}, bf16[4,512,256]{2,1,0:T(8,128)(2,1)}, u32[]{:S(2)}, u32[]{:S(2)}) collective-permute-start(bf16[4,512,256]{2,1,0:T(8,128)(2,1)} %bitcast.6), channel_id=1, source_target_pairs={{0,4},{4,8},{8,12},{12,16},{16,20},{20,24},{24,28},{1,5},{5,9},{9,... | collective-permute-start | bytes 3145736 | tf_op jit(solution)/shard_map/ppermute | solution.py:262
  10.0 17.3 %copy-start.4 = (bf16[8,8,64,256]{3,2,1,0:T(8,128)(2,1)S(1)}, bf16[8,8,64,256]{3,2,1,0:T(8,128)(2,1)}, u32[]{:S(2)}) copy-start(bf16[8,8,64,256]{3,2,1,0:T(8,128)(2,1)} %x_ref.3) | copy-start | bytes 6291460
  10.0 35.8 %copy-start.9 = (bf16[3,3,256,256]{3,2,1,0:T(8,128)(2,1)S(1)}, bf16[3,3,256,256]{3,2,1,0:T(8,128)(2,1)}, u32[]{:S(2)}) copy-start(bf16[3,3,256,256]{3,2,1,0:T(8,128)(2,1)} %w_ref.1) | copy-start | bytes 3538948
  21.9 60.2 %collective-permute-start.12 = (bf16[4,512,256]{2,1,0:T(8,128)(2,1)}, bf16[4,512,256]{2,1,0:T(8,128)(2,1)}, u32[]{:S(2)}, u32[]{:S(2)}) collective-permute-start(bf16[4,512,256]{2,1,0:T(8,128)(2,1)} %get-tuple-element.33), channel_id=1, source_target_pairs={{4,0},{8,4},{12,8},{20,16},{24,20},{28,24},{0,12},{5,1},{9,5},{13,... | collective-permute-start | bytes 3145736 | tf_op jit(solution)/shard_map/ppermute | solution.py:277
  24.1 58.1 %collective-permute-start.14 = (bf16[4,512,256]{2,1,0:T(8,128)(2,1)}, bf16[4,512,256]{2,1,0:T(8,128)(2,1)}, u32[]{:S(2)}, u32[]{:S(2)}) collective-permute-start(bf16[4,512,256]{2,1,0:T(8,128)(2,1)} %get-tuple-element.32), channel_id=1, source_target_pairs={{0,4},{4,8},{8,12},{16,20},{20,24},{24,28},{28,16},{1,5},{5,9},{9,... | collective-permute-start | bytes 3145736 | tf_op jit(solution)/shard_map/ppermute | solution.py:276
  27.3 37.6 %copy-start.19 = (bf16[3,256,256]{2,1,0:T(8,128)(2,1)S(1)}, bf16[3,256,256]{2,1,0:T(8,128)(2,1)}, u32[]{:S(2)}) copy-start(bf16[3,256,256]{2,1,0:T(8,128)(2,1)} %param.11) | copy-start | bytes 1179652
  27.3 9.5 %collective-permute-start = (bf16[8,1,64,256]{3,2,1,0:T(8,128)(2,1)S(1)}, bf16[8,1,64,256]{3,2,1,0:T(8,128)(2,1)S(1)}, u32[]{:S(2)}, u32[]{:S(2)}) collective-permute-start(bf16[8,1,64,256]{3,2,1,0:T(8,128)(2,1)S(1)} %get-tuple-element.38), channel_id=1, source_target_pairs={{0,1},{1,2},{2,3},{4,5},{5,6},{6,7},{8,9},{9,10},{10,11},{12,13},{... | collective-permute-start | bytes 786440 | tf_op jit(solution)/shard_map/ppermute | solution.py:262
  36.8 8.9 %collective-permute-start.1 = (bf16[8,1,64,256]{3,2,1,0:T(8,128)(2,1)S(1)}, bf16[8,1,64,256]{3,2,1,0:T(8,128)(2,1)S(1)}, u32[]{:S(2)}, u32[]{:S(2)}) collective-permute-start(bf16[8,1,64,256]{3,2,1,0:T(8,128)(2,1)S(1)} %get-tuple-element.37), channel_id=1, source_target_pairs={{1,0},{2,1},{3,2},{5,4},{6,5},{7,6},{9,8},{10,9},{11,10},{13,12},{... | collective-permute-start | bytes 786440 | tf_op jit(solution)/shard_map/ppermute | solution.py:262
  45.8 6.4 %copy-start.22 = (bf16[8,1,64,256]{3,2,1,0:T(8,128)(2,1)}, bf16[8,1,64,256]{3,2,1,0:T(8,128)(2,1)S(1)}, u32[]{:S(2)}) copy-start(bf16[8,1,64,256]{3,2,1,0:T(8,128)(2,1)S(1)} %collective-permute-done.1.below_ref) | copy-start | bytes 786436
  52.2 2.0 copy-start.13
  54.2 5.6 %collective-permute-start.2 = (f32[8,2,256]{2,1,0:T(2,128)S(1)}, f32[8,2,256]{2,1,0:T(2,128)S(1)}, u32[]{:S(2)}, u32[]{:S(2)}) collective-permute-start(f32[8,2,256]{2,1,0:T(2,128)S(1)} %get-tuple-element.16.refs_0_), channel_id=1, source_target_pairs={{0,1},{1,2},{2,3},{3,0},{4,5},{5,6},{6,7},{7,4},{8,9},{9,10},{10,1... | collective-permute-start | bytes 49160 | tf_op jit(solution)/shard_map/ppermute | solution.py:284
  59.8 9.0 %copy-start.26 = (f32[8,2,256]{2,1,0:T(2,128)}, f32[8,2,256]{2,1,0:T(2,128)S(1)}, u32[]{:S(2)}) copy-start(f32[8,2,256]{2,1,0:T(2,128)S(1)} %collective-permute-done.2.refs_1_) | copy-start | bytes 49156
  59.8 4.6 %collective-permute-start.3 = (f32[8,2,256]{2,1,0:T(2,128)S(1)}, f32[8,2,256]{2,1,0:T(2,128)S(1)}, u32[]{:S(2)}, u32[]{:S(2)}) collective-permute-start(f32[8,2,256]{2,1,0:T(2,128)S(1)} %get-tuple-element.16.refs_0_), channel_id=1, source_target_pairs={{0,2},{1,3},{2,0},{3,1},{4,6},{5,7},{6,4},{7,5},{8,10},{9,11},{10,... | collective-permute-start | bytes 49160 | tf_op jit(solution)/shard_map/ppermute | solution.py:284
  64.5 4.4 %copy-start.29 = (f32[8,2,256]{2,1,0:T(2,128)}, f32[8,2,256]{2,1,0:T(2,128)S(1)}, u32[]{:S(2)}) copy-start(f32[8,2,256]{2,1,0:T(2,128)S(1)} %collective-permute-done.3.refs_2_) | copy-start | bytes 49156
  64.5 3.7 %collective-permute-start.4 = (f32[8,2,256]{2,1,0:T(2,128)S(1)}, f32[8,2,256]{2,1,0:T(2,128)S(1)}, u32[]{:S(2)}, u32[]{:S(2)}) collective-permute-start(f32[8,2,256]{2,1,0:T(2,128)S(1)} %get-tuple-element.16.refs_0_), channel_id=1, source_target_pairs={{0,3},{1,0},{2,1},{3,2},{4,7},{5,4},{6,5},{7,6},{8,11},{9,8},{10,9... | collective-permute-start | bytes 49160 | tf_op jit(solution)/shard_map/ppermute | solution.py:284
  68.8 2.2 copy-start.14
  75.9 6.4 %copy-start = (bf16[8,8,64,256]{3,2,1,0:T(8,128)(2,1)S(1)}, bf16[8,8,64,256]{3,2,1,0:T(8,128)(2,1)}, u32[]{:S(2)}) copy-start(bf16[8,8,64,256]{3,2,1,0:T(8,128)(2,1)} %cot_ref.1) | copy-start | bytes 6291460
  75.9 6.4 %copy-start.21 = (bf16[3,256,256]{2,1,0:T(8,128)(2,1)S(1)}, bf16[3,256,256]{2,1,0:T(8,128)(2,1)}, u32[]{:S(2)}) copy-start(bf16[3,256,256]{2,1,0:T(8,128)(2,1)} %copy.20) | copy-start | bytes 1179652
  75.9 6.4 %copy-start.36 = (s32[2]{0:T(128)S(1)}, s32[2]{0:T(128)}, u32[]{:S(2)}) copy-start(s32[2]{0:T(128)} %refs_1_.5) | copy-start | bytes 28
  75.9 6.4 %copy-start.40 = (s32[2]{0:T(128)S(1)}, s32[2]{0:T(128)}, u32[]{:S(2)}) copy-start(s32[2]{0:T(128)} %refs_2_.5) | copy-start | bytes 28
  82.2 8.9 %copy-start.7 = (f32[8,512,256]{2,1,0:T(8,128)}, f32[8,512,256]{2,1,0:T(8,128)S(1)}, u32[]{:S(2)}) copy-start(f32[8,512,256]{2,1,0:T(8,128)S(1)} %get-tuple-element.19.refs_11_.normed_ref) | copy-start | bytes 12582916
  91.1 2.0 copy-start.11
  93.1 16.9 %collective-permute-start.15 = (f32[8,2,256]{2,1,0:T(2,128)}, f32[8,2,256]{2,1,0:T(2,128)}, u32[]{:S(2)}, u32[]{:S(2)}) collective-permute-start(f32[8,2,256]{2,1,0:T(2,128)} %get-tuple-element.22.refs_4_), channel_id=1, source_target_pairs={{0,1},{1,2},{2,3},{3,0},{4,5},{5,6},{6,7},{7,4},{8,9},{9,10},{10,1... | collective-permute-start | bytes 49160 | tf_op jit(solution)/shard_map/ppermute | solution.py:284
  93.1 16.9 %collective-permute-start.16 = (f32[8,2,256]{2,1,0:T(2,128)}, f32[8,2,256]{2,1,0:T(2,128)}, u32[]{:S(2)}, u32[]{:S(2)}) collective-permute-start(f32[8,2,256]{2,1,0:T(2,128)} %get-tuple-element.22.refs_4_), channel_id=1, source_target_pairs={{0,2},{1,3},{2,0},{3,1},{4,6},{5,7},{6,4},{7,5},{8,10},{9,11},{10,... | collective-permute-start | bytes 49160 | tf_op jit(solution)/shard_map/ppermute | solution.py:284
  95.9 14.2 %collective-permute-start.17 = (f32[8,2,256]{2,1,0:T(2,128)}, f32[8,2,256]{2,1,0:T(2,128)}, u32[]{:S(2)}, u32[]{:S(2)}) collective-permute-start(f32[8,2,256]{2,1,0:T(2,128)} %get-tuple-element.22.refs_4_), channel_id=1, source_target_pairs={{0,3},{1,0},{2,1},{3,2},{4,7},{5,4},{6,5},{7,6},{8,11},{9,8},{10,9... | collective-permute-start | bytes 49160 | tf_op jit(solution)/shard_map/ppermute | solution.py:284
  99.5 2.0 copy-start.2
  99.5 2.0 copy-start.37
  99.5 2.0 copy-start.41
  101.6 8.5 %copy-start.8 = (f32[8,512,256]{2,1,0:T(8,128)S(1)}, f32[8,512,256]{2,1,0:T(8,128)}, u32[]{:S(2)}) copy-start(f32[8,512,256]{2,1,0:T(8,128)} %copy-done.7) | copy-start | bytes 12582916
  101.6 8.5 %copy-start.12 = (f32[8,512,256]{2,1,0:T(8,128)S(1)}, f32[8,512,256]{2,1,0:T(8,128)}, u32[]{:S(2)}) copy-start(f32[8,512,256]{2,1,0:T(8,128)} %copy-done.11) | copy-start | bytes 12582916
  101.6 8.5 %copy-start.28 = (f32[8,2,256]{2,1,0:T(2,128)S(1)}, f32[8,2,256]{2,1,0:T(2,128)}, u32[]{:S(2)}) copy-start(f32[8,2,256]{2,1,0:T(2,128)} %copy-done.26) | copy-start | bytes 49156
  101.6 8.5 %copy-start.31 = (f32[8,2,256]{2,1,0:T(2,128)S(1)}, f32[8,2,256]{2,1,0:T(2,128)}, u32[]{:S(2)}) copy-start(f32[8,2,256]{2,1,0:T(2,128)} %copy-done.29) | copy-start | bytes 49156
  101.6 8.5 %copy-start.34 = (f32[8,2,256]{2,1,0:T(2,128)S(1)}, f32[8,2,256]{2,1,0:T(2,128)}, u32[]{:S(2)}) copy-start(f32[8,2,256]{2,1,0:T(2,128)} %copy-done.32) | copy-start | bytes 49156
  126.9 3.7 %collective-permute-start.20 = (bf16[12,128,256]{2,1,0:T(8,128)(2,1)}, bf16[12,128,256]{2,1,0:T(8,128)(2,1)}, u32[]{:S(2)}, u32[]{:S(2)}) collective-permute-start(bf16[12,128,256]{2,1,0:T(8,128)(2,1)} %get-tuple-element.27), channel_id=1, source_target_pairs={{0,4},{4,0},{8,12},{12,8},{16,20},{20,16},{24,28},{28,24},{1,5},{5... | collective-permute-start | bytes 2359304 | tf_op jit(solution)/shard_map/ppermute | solution.py:322
  126.9 3.7 %copy-start.18 = (f32[12,128,256]{2,1,0:T(8,128)S(1)}, f32[12,128,256]{2,1,0:T(8,128)}, u32[]{:S(2)}) copy-start(f32[12,128,256]{2,1,0:T(8,128)} %copy-done.17) | copy-start | bytes 4718596
  129.3 37.5 %collective-permute-start.6 = (bf16[4,512,256]{2,1,0:T(8,128)(2,1)}, bf16[4,512,256]{2,1,0:T(8,128)(2,1)}, u32[]{:S(2)}, u32[]{:S(2)}) collective-permute-start(bf16[4,512,256]{2,1,0:T(8,128)(2,1)} %slice.37), channel_id=1, source_target_pairs={{12,28},{16,0},{13,29},{17,1},{14,30},{18,2},{15,31},{19,3}} | collective-permute-start | bytes 3145736 | tf_op jit(solution)/shard_map/ppermute | solution.py:272
  133.9 8.1 %collective-permute-start.21 = (bf16[12,32,256]{2,1,0:T(8,128)(2,1)}, bf16[12,32,256]{2,1,0:T(8,128)(2,1)}, u32[]{:S(2)}, u32[]{:S(2)}) collective-permute-start(bf16[12,32,256]{2,1,0:T(8,128)(2,1)} %get-tuple-element.41), channel_id=1, source_target_pairs={{0,8},{4,12},{8,0},{12,4},{16,24},{20,28},{24,16},{28,20},{1,9},{5... | collective-permute-start | bytes 589832 | tf_op jit(solution)/shard_map/ppermute | solution.py:295
  133.9 20.8 %collective-permute-start.22 = (bf16[12,32,256]{2,1,0:T(8,128)(2,1)}, bf16[12,32,256]{2,1,0:T(8,128)(2,1)}, u32[]{:S(2)}, u32[]{:S(2)}) collective-permute-start(bf16[12,32,256]{2,1,0:T(8,128)(2,1)} %get-tuple-element.43), channel_id=1, source_target_pairs={{0,16},{4,20},{8,24},{12,28},{16,0},{20,4},{24,8},{28,12},{1,17},{... | collective-permute-start | bytes 589832 | tf_op jit(solution)/shard_map/ppermute | solution.py:295
  137.5 17.2 %collective-permute-start.23 = (bf16[12,32,256]{2,1,0:T(8,128)(2,1)S(1)}, bf16[12,32,256]{2,1,0:T(8,128)(2,1)}, u32[]{:S(2)}, u32[]{:S(2)}) collective-permute-start(bf16[12,32,256]{2,1,0:T(8,128)(2,1)S(1)} %get-tuple-element.42), channel_id=1, source_target_pairs={{0,24},{4,28},{8,16},{12,20},{16,8},{20,12},{24,0},{28,4},{1,25},{... | collective-permute-start | bytes 589832 | tf_op jit(solution)/shard_map/ppermute | solution.py:295
  156.9 4.5 %collective-permute-start.24 = (bf16[12,8,256]{2,1,0:T(8,128)(2,1)S(1)}, bf16[12,8,256]{2,1,0:T(8,128)(2,1)S(1)}, u32[]{:S(2)}, u32[]{:S(2)}) collective-permute-start(bf16[12,8,256]{2,1,0:T(8,128)(2,1)S(1)} %get-tuple-element.44), channel_id=1, source_target_pairs={{0,1},{1,0},{2,3},{3,2},{4,5},{5,4},{6,7},{7,6},{8,9},{9,8},{10,11... | collective-permute-start | bytes 147464 | tf_op jit(solution)/shard_map/ppermute | solution.py:295
  158.0 5.0 %collective-permute-start.25 = (bf16[12,8,256]{2,1,0:T(8,128)(2,1)S(1)}, bf16[12,8,256]{2,1,0:T(8,128)(2,1)S(1)}, u32[]{:S(2)}, u32[]{:S(2)}) collective-permute-start(bf16[12,8,256]{2,1,0:T(8,128)(2,1)S(1)} %get-tuple-element.46), channel_id=1, source_target_pairs={{0,2},{1,3},{2,0},{3,1},{4,6},{5,7},{6,4},{7,5},{8,10},{9,11},{10,... | collective-permute-start | bytes 147464 | tf_op jit(solution)/shard_map/ppermute | solution.py:295
  159.1 6.1 %collective-permute-start.26 = (bf16[12,8,256]{2,1,0:T(8,128)(2,1)S(1)}, bf16[12,8,256]{2,1,0:T(8,128)(2,1)}, u32[]{:S(2)}, u32[]{:S(2)}) collective-permute-start(bf16[12,8,256]{2,1,0:T(8,128)(2,1)S(1)} %get-tuple-element.45), channel_id=1, source_target_pairs={{0,3},{1,2},{2,1},{3,0},{4,7},{5,6},{6,5},{7,4},{8,11},{9,10},{10,... | collective-permute-start | bytes 147464 | tf_op jit(solution)/shard_map/ppermute | solution.py:295
  166.2 9.7 %copy-start.48 = (bf16[8,64,256]{2,1,0:T(8,128)(2,1)S(1)}, bf16[8,64,256]{2,1,0:T(8,128)(2,1)}, u32[]{:S(2)}) copy-start(bf16[8,64,256]{2,1,0:T(8,128)(2,1)} %copy-done.47) | copy-start | bytes 786436
  166.2 41.5 %copy-start.46 = (bf16[8,64,256]{2,1,0:T(8,128)(2,1)S(1)}, bf16[8,64,256]{2,1,0:T(8,128)(2,1)}, u32[]{:S(2)}) copy-start(bf16[8,64,256]{2,1,0:T(8,128)(2,1)} %copy-done.45) | copy-start | bytes 786436
  166.2 13.9 %collective-permute-start.27 = (bf16[12,8,256]{2,1,0:T(8,128)(2,1)S(1)}, bf16[12,8,256]{2,1,0:T(8,128)(2,1)S(1)}, u32[]{:S(2)}, u32[]{:S(2)}) collective-permute-start(bf16[12,8,256]{2,1,0:T(8,128)(2,1)S(1)} %get-tuple-element.29), channel_id=1, source_target_pairs={{0,1},{1,0},{2,3},{3,2},{4,5},{5,4},{6,7},{7,6},{8,9},{9,8},{10,11... | collective-permute-start | bytes 147464 | tf_op jit(solution)/shard_map/ppermute | solution.py:303
  170.6 61.1 %collective-permute-start.5 = (bf16[4,512,256]{2,1,0:T(8,128)(2,1)}, bf16[4,512,256]{2,1,0:T(8,128)(2,1)}, u32[]{:S(2)}, u32[]{:S(2)}) collective-permute-start(bf16[4,512,256]{2,1,0:T(8,128)(2,1)} %get-tuple-element.36), channel_id=1, source_target_pairs={{4,0},{8,4},{12,8},{16,12},{20,16},{24,20},{28,24},{5,1},{9,5},{13... | collective-permute-start | bytes 3145736 | tf_op jit(solution)/shard_map/ppermute | solution.py:262
  171.8 59.8 %collective-permute-start.8 = (bf16[4,512,256]{2,1,0:T(8,128)(2,1)}, bf16[4,512,256]{2,1,0:T(8,128)(2,1)}, u32[]{:S(2)}, u32[]{:S(2)}) collective-permute-start(bf16[4,512,256]{2,1,0:T(8,128)(2,1)} %get-tuple-element.36), channel_id=1, source_target_pairs={{0,4},{4,8},{8,12},{12,16},{16,20},{20,24},{24,28},{1,5},{5,9},{9,... | collective-permute-start | bytes 3145736 | tf_op jit(solution)/shard_map/ppermute | solution.py:262
  175.9 24.9 %collective-permute-start.18 = (bf16[8,64,256]{2,1,0:T(8,128)(2,1)S(1)}, bf16[8,64,256]{2,1,0:T(8,128)(2,1)S(1)}, u32[]{:S(2)}, u32[]{:S(2)}) collective-permute-start(bf16[8,64,256]{2,1,0:T(8,128)(2,1)S(1)} %copy-done.48), channel_id=1, source_target_pairs={{0,1},{1,2},{2,3},{4,5},{5,6},{6,7},{8,9},{9,10},{10,11},{12,13},{... | collective-permute-start | bytes 786440 | tf_op jit(solution)/shard_map/ppermute | solution.py:262
  179.3 6.3 %collective-permute-start.28 = (bf16[12,8,256]{2,1,0:T(8,128)(2,1)S(1)}, bf16[12,8,256]{2,1,0:T(8,128)(2,1)S(1)}, u32[]{:S(2)}, u32[]{:S(2)}) collective-permute-start(bf16[12,8,256]{2,1,0:T(8,128)(2,1)S(1)} %get-tuple-element.29), channel_id=1, source_target_pairs={{0,2},{1,3},{2,0},{3,1},{4,6},{5,7},{6,4},{7,5},{8,10},{9,11},{10,... | collective-permute-start | bytes 147464 | tf_op jit(solution)/shard_map/ppermute | solution.py:303
  180.1 6.0 %collective-permute-start.29 = (bf16[12,8,256]{2,1,0:T(8,128)(2,1)S(1)}, bf16[12,8,256]{2,1,0:T(8,128)(2,1)S(1)}, u32[]{:S(2)}, u32[]{:S(2)}) collective-permute-start(bf16[12,8,256]{2,1,0:T(8,128)(2,1)S(1)} %get-tuple-element.29), channel_id=1, source_target_pairs={{0,3},{1,2},{2,1},{3,0},{4,7},{5,6},{6,5},{7,4},{8,11},{9,10},{10,... | collective-permute-start | bytes 147464 | tf_op jit(solution)/shard_map/ppermute | solution.py:303
  186.2 7.8 %collective-permute-start.30 = (bf16[4,12,8,256]{3,2,1,0:T(8,128)(2,1)S(1)}, bf16[4,12,8,256]{3,2,1,0:T(8,128)(2,1)S(1)}, u32[]{:S(2)}, u32[]{:S(2)}) collective-permute-start(bf16[4,12,8,256]{3,2,1,0:T(8,128)(2,1)S(1)} %bitcast_dynamic-update-slice_fusion.4), channel_id=1, source_target_pairs={{0,8},{4,12},{8,0},{12,4},{16,24},{20,28},{24,16},{28,20},{1,9},{5... | collective-permute-start | bytes 589832 | tf_op jit(solution)/shard_map/ppermute | solution.py:303
  186.2 18.0 %collective-permute-start.31 = (bf16[4,12,8,256]{3,2,1,0:T(8,128)(2,1)S(1)}, bf16[4,12,8,256]{3,2,1,0:T(8,128)(2,1)S(1)}, u32[]{:S(2)}, u32[]{:S(2)}) collective-permute-start(bf16[4,12,8,256]{3,2,1,0:T(8,128)(2,1)S(1)} %bitcast_dynamic-update-slice_fusion.4), channel_id=1, source_target_pairs={{0,16},{4,20},{8,24},{12,28},{16,0},{20,4},{24,8},{28,12},{1,17},{... | collective-permute-start | bytes 589832 | tf_op jit(solution)/shard_map/ppermute | solution.py:303
  194.0 13.7 %collective-permute-start.32 = (bf16[4,12,8,256]{3,2,1,0:T(8,128)(2,1)S(1)}, bf16[4,12,8,256]{3,2,1,0:T(8,128)(2,1)S(1)}, u32[]{:S(2)}, u32[]{:S(2)}) collective-permute-start(bf16[4,12,8,256]{3,2,1,0:T(8,128)(2,1)S(1)} %bitcast_dynamic-update-slice_fusion.4), channel_id=1, source_target_pairs={{0,24},{4,28},{8,16},{12,20},{16,8},{20,12},{24,0},{28,4},{1,25},{... | collective-permute-start | bytes 589832 | tf_op jit(solution)/shard_map/ppermute | solution.py:303
  200.8 30.8 %collective-permute-start.7 = (bf16[4,512,256]{2,1,0:T(8,128)(2,1)}, bf16[4,512,256]{2,1,0:T(8,128)(2,1)}, u32[]{:S(2)}, u32[]{:S(2)}) collective-permute-start(bf16[4,512,256]{2,1,0:T(8,128)(2,1)} %get-tuple-element.31), channel_id=1, source_target_pairs={{4,0},{8,4},{12,8},{20,16},{24,20},{28,24},{0,12},{5,1},{9,5},{13,... | collective-permute-start | bytes 3145736 | tf_op jit(solution)/shard_map/ppermute | solution.py:277
  204.1 27.5 %collective-permute-start.9 = (bf16[4,512,256]{2,1,0:T(8,128)(2,1)}, bf16[4,512,256]{2,1,0:T(8,128)(2,1)}, u32[]{:S(2)}, u32[]{:S(2)}) collective-permute-start(bf16[4,512,256]{2,1,0:T(8,128)(2,1)} %get-tuple-element.30), channel_id=1, source_target_pairs={{0,4},{4,8},{8,12},{16,20},{20,24},{24,28},{28,16},{1,5},{5,9},{9,... | collective-permute-start | bytes 3145736 | tf_op jit(solution)/shard_map/ppermute | solution.py:276
  207.7 10.8 %collective-permute-start.19 = (bf16[8,64,256]{2,1,0:T(8,128)(2,1)S(1)}, bf16[8,64,256]{2,1,0:T(8,128)(2,1)S(1)}, u32[]{:S(2)}, u32[]{:S(2)}) collective-permute-start(bf16[8,64,256]{2,1,0:T(8,128)(2,1)S(1)} %copy-done.46), channel_id=1, source_target_pairs={{1,0},{2,1},{3,2},{5,4},{6,5},{7,6},{9,8},{10,9},{11,10},{13,12},{... | collective-permute-start | bytes 786440 | tf_op jit(solution)/shard_map/ppermute | solution.py:262
  219.2 20.9 %collective-permute-start.33 = (bf16[4,4,12,8,256]{4,3,2,1,0:T(8,128)(2,1)}, bf16[4,4,12,8,256]{4,3,2,1,0:T(8,128)(2,1)}, u32[]{:S(2)}, u32[]{:S(2)}) collective-permute-start(bf16[4,4,12,8,256]{4,3,2,1,0:T(8,128)(2,1)} %bitcast_dynamic-update-slice_fusion), channel_id=1, source_target_pairs={{0,4},{4,0},{8,12},{12,8},{16,20},{20,16},{24,28},{28,24},{1,5},{5... | collective-permute-start | bytes 2359304 | tf_op jit(solution)/shard_map/ppermute | solution.py:327
  224.5 7.1 %copy-start.3 = (bf16[8,512,256]{2,1,0:T(8,128)(2,1)S(1)}, bf16[8,512,256]{2,1,0:T(8,128)(2,1)}, u32[]{:S(2)}) copy-start(bf16[8,512,256]{2,1,0:T(8,128)(2,1)} %copy-done.1) | copy-start | bytes 6291460
  224.5 7.1 %copy-start.6 = (bf16[8,8,64,256]{3,2,1,0:T(8,128)(2,1)S(1)}, bf16[8,8,64,256]{3,2,1,0:T(8,128)(2,1)}, u32[]{:S(2)}) copy-start(bf16[8,8,64,256]{3,2,1,0:T(8,128)(2,1)} %x_ref.3) | copy-start | bytes 6291460
  224.5 7.1 %copy-start.20 = (bf16[3,256,256]{2,1,0:T(8,128)(2,1)S(1)}, bf16[3,256,256]{2,1,0:T(8,128)(2,1)}, u32[]{:S(2)}) copy-start(bf16[3,256,256]{2,1,0:T(8,128)(2,1)} %param.11) | copy-start | bytes 1179652
  224.5 7.1 %copy-start.38 = (s32[2]{0:T(128)S(1)}, s32[2]{0:T(128)}, u32[]{:S(2)}) copy-start(s32[2]{0:T(128)} %refs_1_.5) | copy-start | bytes 28
  224.5 7.1 %copy-start.42 = (s32[2]{0:T(128)S(1)}, s32[2]{0:T(128)}, u32[]{:S(2)}) copy-start(s32[2]{0:T(128)} %refs_2_.5) | copy-start | bytes 28
  (23 other events, 22.9 us)

commit v3 on v2

v3 whole, which is shorter than its diff:
```python
import functools

import jax
import jax.numpy as jnp
from jax import lax
from jax.experimental import pallas as pl
from jax.experimental.pallas import tpu as pltpu
from jax.sharding import PartitionSpec as P

GROUPS = 32
NORM_EPS = 1e-05
BF16 = jnp.bfloat16
F32 = jnp.float32
VMEM_LIMIT = 20 * 2**20


def call(kernel, name, operands, out_shape, flops=0, moved=0, scratch=()):
    vmem = pl.BlockSpec(memory_space=pltpu.VMEM)
    smem = pl.BlockSpec(memory_space=pltpu.SMEM)
    return pl.pallas_call(
        kernel,
        in_specs=[smem if x.dtype == jnp.int32 else vmem for x in operands],
        out_specs=jax.tree.map(lambda _: vmem, out_shape),
        out_shape=out_shape,
        scratch_shapes=list(scratch),
        compiler_params=pltpu.CompilerParams(vmem_limit_bytes=VMEM_LIMIT),
        cost_estimate=pl.CostEstimate(flops=int(flops), bytes_accessed=int(moved), transcendentals=0),
        name=name,
    )(*operands)


def dot(a, b):
    return jnp.dot(a, b, preferred_element_type=F32)


def dot_rows(a, b):
    return lax.dot_general(a, b, (((0,), (0,)), ((), ())), preferred_element_type=F32)


def group_total(row, group_size):
    channels = row.shape[-1]
    lane = lax.broadcasted_iota(jnp.int32, row.shape, 1)
    step = 1
    while step < group_size:
        up = pltpu.roll(row, channels - step, axis=1)
        down = pltpu.roll(row, step, axis=1)
        row = row + jnp.where((lane & step) == 0, up, down)
        step *= 2
    return row


def frame_stats(part_refs, f, entries, group_size):
    total = part_refs[0][f]
    for ref in part_refs[1:]:
        total = total + ref[f]
    return group_total(total, group_size) / entries


def sigmoid(x):
    return 0.5 * jnp.tanh(0.5 * x) + 0.5


def mean_and_inv(part_refs, f, entries, group_size):
    both = frame_stats(part_refs, f, entries, group_size)
    mean = both[0:1]
    inv = lax.rsqrt(both[1:2] - mean * mean + NORM_EPS)
    return mean, inv


def column_sums(first, second):
    return jnp.concatenate(
        [jnp.sum(first, axis=0, keepdims=True), jnp.sum(second, axis=0, keepdims=True)], axis=0
    )


def put_windows(above, mid, below, lhs_ref, at, order):
    width, (pixels, channels) = above.shape[0], mid.shape
    first, mid_at, last = (slice(k * channels, (k + 1) * channels) for k in order)
    lhs_ref[at : at + width, first] = above
    lhs_ref[at + width : at + pixels, first] = mid[: pixels - width]
    lhs_ref[at : at + pixels, mid_at] = mid
    lhs_ref[at : at + pixels - width, last] = mid[width:]
    lhs_ref[at + pixels - width : at + pixels, last] = below


def from_left(y, width):
    col = lax.broadcasted_iota(jnp.int32, y.shape, 0) & (width - 1)
    return jnp.where(col == 0, 0.0, pltpu.roll(y, 1, axis=0))


def from_right(y, width):
    col = lax.broadcasted_iota(jnp.int32, y.shape, 0) & (width - 1)
    return jnp.where(col == width - 1, 0.0, pltpu.roll(y, y.shape[0] - 1, axis=0))


def slot_sources(clip_ref, dil_ref, local, frames):
    slot = lax.axis_index("tm") * frames + local
    start1 = clip_ref[0]
    filled = start1 + clip_ref[1]
    in_first = slot < start1
    d = jnp.where(in_first, dil_ref[0], dil_ref[1])
    low = jnp.where(in_first, 0, start1)
    high = jnp.where(in_first, start1, filled)
    used = slot < filled
    later, earlier = local + d, local - d
    later_live = used & (slot + d < high)
    earlier_live = used & (slot - d >= low)
    later_which = jnp.where(later_live, jnp.where(later < frames, 1, 2), 0)
    earlier_which = jnp.where(earlier_live, jnp.where(earlier >= 0, 1, 2), 0)
    return (later, later_which), (earlier, earlier_which), used


def gather_taps(clip_ref, dil_ref, local, own, nxt, prv, corner, cat_ref, at, up_slot):
    frames, pixels, channels = own.shape
    later, earlier, used = slot_sources(clip_ref, dil_ref, local, frames)
    me, half = lax.axis_index("tm"), frames // 2

    def put(slot, ref, index):
        cat_ref[pl.ds(at, pixels), slot * channels : (slot + 1) * channels] = ref[index]

    def clear(slot):
        cat_ref[pl.ds(at, pixels), slot * channels : (slot + 1) * channels] = jnp.zeros((pixels, channels), BF16)

    for slot, (index, which), other, shift, turn in (
        (up_slot, later, nxt, -frames, 3),
        (2 - up_slot, earlier, prv, frames, 4),
    ):
        beyond = which == 2
        there = jnp.clip(index + shift, 0, frames - 1)
        pl.when(which == 1)(functools.partial(put, slot, own, jnp.clip(index, 0, frames - 1)))
        pl.when(which == 0)(functools.partial(clear, slot))
        if corner:
            by_corner = beyond & (me == turn)
            low, high = by_corner & (there < half), by_corner & (there >= half)
            pl.when(low)(functools.partial(put, slot, corner[0], jnp.minimum(there, half - 1)))
            pl.when(high)(functools.partial(put, slot, corner[1], jnp.maximum(there - half, 0)))
            beyond = beyond & (me != turn)
        pl.when(beyond)(functools.partial(put, slot, other, there))
    pl.when(used)(functools.partial(put, 1, own, local))
    pl.when(jnp.logical_not(used))(functools.partial(clear, 1))


def loop(count, body):
    def step(k, carry):
        body(k)
        return carry

    lax.fori_loop(0, count, step, 0)


def conv_kernel(x_ref, above_ref, below_ref, w_ref, out_ref, sums_ref, lhs_ref):
    frames, rows, width, channels = x_ref.shape
    pixels = rows * width

    def body(pair):
        for b in range(2):
            f = 2 * pair + b
            mid = x_ref[f].reshape(pixels, channels)
            put_windows(above_ref[f, 0], mid, below_ref[f, 0], lhs_ref, b * pixels, (0, 1, 2))
        lhs = lhs_ref[...]
        y = [dot(lhs, w_ref[:, j].reshape(3 * channels, channels)) for j in range(3)]
        out = y[1] + from_left(y[0], width) + from_right(y[2], width)
        for b in range(2):
            one = out[b * pixels : (b + 1) * pixels]
            out_ref[2 * pair + b] = one
            sums_ref[2 * pair + b] = column_sums(one, one * one)

    loop(frames // 2, body)


def act_kernel(n, entries, group_size, clip_ref, *refs):
    parts, (conv_ref, gain_ref, shift_ref, act_ref, normed_ref, slope_ref) = refs[:n], refs[n:]
    frames = conv_ref.shape[0]
    first = lax.axis_index("tm") * frames
    filled = clip_ref[0] + clip_ref[1]

    def body(f):
        mean, inv = mean_and_inv(parts, f, entries, group_size)
        normed = (conv_ref[f] - mean) * inv
        shaped = normed * gain_ref[...] + shift_ref[...]
        sig = sigmoid(shaped)
        act_ref[f] = jnp.where(first + f < filled, shaped * sig, 0.0).astype(BF16)
        normed_ref[f] = normed.astype(BF16)
        slope_ref[f] = (sig * (1.0 + shaped * (1.0 - sig)) * gain_ref[...]).astype(BF16)

    loop(frames, body)


def turn_kernel(x_ref, above_ref, below_ref, act_ref, xt_ref, at_ref, lhs_ref):
    frames, rows, width, channels = x_ref.shape
    pixels = rows * width

    def body(f):
        mid = x_ref[f].reshape(pixels, channels)
        put_windows(above_ref[f, 0], mid, below_ref[f, 0], lhs_ref, 0, (0, 1, 2))
        lanes = pl.ds(pl.multiple_of(f * pixels, pixels), pixels)
        for i in range(3):
            block = slice(i * channels, (i + 1) * channels)
            xt_ref[block, lanes] = lhs_ref[:, block].T
        at_ref[:, lanes] = act_ref[f].T

    loop(frames, body)


def grad_act_kernel(corners, clip_ref, dil_ref, own, nxt, prv, *refs):
    corner, (tw_ref, normed_ref, slope_ref, ga_ref, cat_ref, sums_ref) = refs[:corners], refs[corners:]
    frames, pixels, _ = own.shape

    def body(pair):
        rows = pl.ds(pl.multiple_of(2 * pair * pixels, 2 * pixels), 2 * pixels)
        for b in range(2):
            at = pl.multiple_of((2 * pair + b) * pixels, pixels)
            gather_taps(clip_ref, dil_ref, 2 * pair + b, own, nxt, prv, corner, cat_ref, at, 0)
        grad_act = dot(cat_ref[rows], tw_ref[...]).astype(BF16)
        for b in range(2):
            f = 2 * pair + b
            one = grad_act[b * pixels : (b + 1) * pixels]
            ga_ref[f] = one
            gn = one.astype(F32) * slope_ref[f].astype(F32)
            sums_ref[f] = column_sums(gn, gn * normed_ref[f].astype(F32))

    loop(frames // 2, body)


def temporal_grad_kernel(at_ref, cat_ref, out_ref):
    out_ref[...] = dot(at_ref[...], cat_ref[...])


def weight_grad_kernel(n, entries, group_size, xt_ref, normed_ref, slope_ref, ga_ref, temporal_ref, *refs):
    parts, grad_parts = refs[:n], refs[n : 2 * n]
    g_ref, first_ref, last_ref, send_ref, keep_ref, moved_ref, acc_ref = refs[2 * n :]
    frames, pixels, channels = normed_ref.shape
    width = first_ref.shape[2]

    def body(f):
        _, inv = mean_and_inv(parts, f, entries, group_size)
        means = frame_stats(grad_parts, f, entries, group_size)
        gn = ga_ref[f].astype(F32) * slope_ref[f].astype(F32)
        wide = inv * (gn - means[0:1] - normed_ref[f].astype(F32) * means[1:2])
        grad = wide.astype(BF16)
        g_ref[f] = grad
        first_ref[f, 0] = grad[:width]
        last_ref[f, 0] = grad[pixels - width :]
        here = pl.ds(pl.multiple_of(f * pixels, pixels), pixels)
        moved_ref[here, :channels] = from_right(wide, width).astype(BF16)
        moved_ref[here, channels : 2 * channels] = grad
        moved_ref[here, 2 * channels :] = from_left(wide, width).astype(BF16)

    loop(frames, body)
    for j in range(3):
        lanes = slice(j * channels, (j + 1) * channels)
        acc_ref[: 3 * channels, lanes] = dot(xt_ref[...], moved_ref[:, lanes])
    acc_ref[3 * channels :, :] = temporal_ref[...]

    chips, depth, block, _ = keep_ref.shape
    half = chips * depth * block
    core = lax.axis_index("tm") & 1

    def hand_out(kept, sent):
        for p in range(chips):
            for z in range(depth):
                at = (p * depth + z) * block
                keep_ref[p, z] = acc_ref[kept + at : kept + at + block]
                send_ref[p, z] = acc_ref[sent + at : sent + at + block].astype(BF16)

    pl.when(core == 0)(functools.partial(hand_out, 0, half))
    pl.when(core == 1)(functools.partial(hand_out, half, 0))


def conv_back_kernel(g_ref, above_ref, below_ref, cot_ref, w_ref, out_ref, lhs_ref):
    frames, rows, width, channels = cot_ref.shape
    pixels = rows * width

    def body(pair):
        for b in range(2):
            f = 2 * pair + b
            put_windows(above_ref[f, 0], g_ref[f], below_ref[f, 0], lhs_ref, b * pixels, (2, 1, 0))
        lhs = lhs_ref[...]
        z = [dot(lhs, w_ref[j]) for j in range(3)]
        out = z[1] + from_right(z[0], width) + from_left(z[2], width)
        for b in range(2):
            one = out[b * pixels : (b + 1) * pixels].reshape(rows, width, channels)
            out_ref[2 * pair + b] = (one + cot_ref[2 * pair + b].astype(F32)).astype(BF16)

    loop(frames // 2, body)


def out_kernel(corners, clip_ref, dil_ref, own, nxt, prv, *refs):
    corner, (tw_ref, x_ref, out_ref, cat_ref) = refs[:corners], refs[corners:]
    frames, rows, width, channels = x_ref.shape
    pixels = rows * width

    def body(pair):
        for b in range(2):
            gather_taps(clip_ref, dil_ref, 2 * pair + b, own, nxt, prv, corner, cat_ref, b * pixels, 2)
        temporal_out = dot(cat_ref[...], tw_ref[...]).astype(BF16).astype(F32)
        for b in range(2):
            one = temporal_out[b * pixels : (b + 1) * pixels].reshape(rows, width, channels)
            out_ref[2 * pair + b] = (x_ref[2 * pair + b].astype(F32) + one).astype(BF16)

    loop(frames // 2, body)


def core_sum_kernel(keep_ref, got_ref, own_ref, *send_refs):
    chip = lax.axis_index("tm") >> 1
    own_ref[...] = keep_ref[chip] + got_ref[chip].astype(F32)
    for s, ref in enumerate(send_refs, 1):
        ref[...] = (keep_ref[chip ^ s] + got_ref[chip ^ s].astype(F32)).astype(BF16)


def sum_kernel(count, own_ref, *refs):
    total = own_ref[...]
    for ref in refs[:count]:
        total = total + ref[...].astype(F32)
    refs[count][...] = total.astype(BF16)


def sum_split_kernel(count, own_ref, *refs):
    got, (mine_ref, *send_refs) = refs[:count], refs[count:]
    deep = lax.axis_index("space")

    def block(k):
        total = own_ref[k]
        for ref in got:
            total = total + ref[k].astype(F32)
        return total

    mine_ref[...] = block(deep)
    for s, ref in enumerate(send_refs, 1):
        ref[...] = block(deep ^ s).astype(BF16)


def place_kernel(axis, shift, *refs):
    me = lax.axis_index(axis) >> shift
    for s, ref in enumerate(refs[:-1]):
        refs[-1][me ^ s] = ref[...]


def finish_kernel(mine_ref, got_ref, spatial_ref, temporal_ref):
    chips, depth, block, _ = mine_ref.shape
    channels = spatial_ref.shape[-1]

    def write(pair):
        for c in range(2):
            for p in range(chips):
                for z in range(depth):
                    row = ((c * chips + p) * depth + z) * block
                    values = pair[c][p, z].astype(F32)
                    i, at = row // channels, row % channels
                    for k in range(3):
                        lanes = values[:, k * channels : (k + 1) * channels]
                        if i < 3:
                            spatial_ref[i, k, at : at + block] = lanes
                        else:
                            temporal_ref[k, at : at + block] = lanes

    core = lax.axis_index("tm") & 1
    pl.when(core == 0)(functools.partial(write, (mine_ref, got_ref)))
    pl.when(core == 1)(functools.partial(write, (got_ref, mine_ref)))


def neighbours(axis, low, high):
    size = lax.axis_size(axis)
    up = [(i, i + 1) for i in range(size - 1)]
    down = [(j, i) for i, j in up]
    return lax.ppermute(high, axis, up), lax.ppermute(low, axis, down)


def frame_neighbours(x):
    size, frames = lax.axis_size("tm"), x.shape[0]
    if size != 8:
        prev, nxt = neighbours("tm", x, x)
        return [nxt, prev]
    near = [i for i in range(7) if i != 3]
    prev = lax.ppermute(x, "tm", [(i, i + 1) for i in near])
    nxt = lax.ppermute(x, "tm", [(i + 1, i) for i in near])
    high = lax.ppermute(x[frames // 2 :], "tm", [(3, 7), (4, 0)])
    low = lax.ppermute(x[: frames // 2], "tm", [(3, 4), (4, 3)])
    high = lax.ppermute(high, "tm", [(7, 4), (0, 3)])
    return [nxt, prev, low, high]


def spread_parts(part, axis):
    size = lax.axis_size(axis)
    return [part] + [
        lax.ppermute(part, axis, [(i, (i + s) % size) for i in range(size)]) for s in range(1, size)
    ]


def per_device(frames_in, cotangent, spatial, temporal, norm_gain, norm_shift, clip_frames, dilation):
    frames, rows, width, channels = frames_in.shape
    pixels = rows * width
    n, tm = lax.axis_size("space"), lax.axis_size("tm")
    chips = tm // 2
    group_size = channels // GROUPS
    entries = float(rows * n * width * group_size)
    gain, shift = norm_gain[None], norm_shift[None]
    big = frames * pixels * channels
    shape = jax.ShapeDtypeStruct
    per_px = (frames, pixels, channels)
    windows = pltpu.VMEM((2 * pixels, 3 * channels), BF16)

    above, below = neighbours("space", frames_in[:, :1], frames_in[:, rows - 1 :])
    cot = cotangent.reshape(per_px)
    cot_around = frame_neighbours(cot)
    corners = len(cot_around) - 2

    conv_out, sums = call(
        conv_kernel, "conv_forward", [frames_in, above, below, spatial],
        [shape(per_px, F32), shape((frames, 2, channels), F32)],
        18 * big * channels, 8 * big, [windows],
    )
    parts = spread_parts(sums, "space")
    act, normed, slope = call(
        functools.partial(act_kernel, n, entries, group_size), "activation",
        [clip_frames, *parts, conv_out, gain, shift],
        [shape(per_px, BF16)] * 3, 10 * big, 10 * big,
    )
    act_around = frame_neighbours(act)
    x_turned, act_turned = call(
        turn_kernel, "turned", [frames_in, above, below, act],
        [shape((3 * channels, frames * pixels), BF16), shape((channels, frames * pixels), BF16)],
        0, 12 * big, [pltpu.VMEM((pixels, 3 * channels), BF16)],
    )

    grad_act, cot_cat, grad_sums = call(
        functools.partial(grad_act_kernel, corners), "grad_activation",
        [clip_frames, dilation, cot, *cot_around, temporal.transpose(0, 2, 1).reshape(3 * channels, channels), normed, slope],
        [shape(per_px, BF16), shape((frames * pixels, 3 * channels), BF16), shape((frames, 2, channels), F32)],
        6 * big * channels, 16 * big,
    )
    grad_parts = spread_parts(grad_sums, "space")
    temporal_part = call(
        temporal_grad_kernel, "temporal_grad", [act_turned, cot_cat],
        shape((channels, 3 * channels), F32), 6 * big * channels, 8 * big,
    )

    block = 2 * channels // (chips * n)
    lanes = 3 * channels
    grad_conv, first_rows, last_rows, send, keep = call(
        functools.partial(weight_grad_kernel, n, entries, group_size), "weight_grad",
        [x_turned, normed, slope, grad_act, temporal_part, *parts, *grad_parts],
        [shape(per_px, BF16)] + [shape((frames, 1, width, channels), BF16)] * 2
        + [shape((chips, n, block, lanes), BF16), shape((chips, n, block, lanes), F32)],
        18 * big * channels, 12 * big,
        [pltpu.VMEM((frames * pixels, lanes), BF16), pltpu.VMEM((4 * channels, lanes), F32)],
    )

    def other_chip(s):
        return [(i, i ^ (2 * s)) for i in range(tm)]

    def other_plane(s):
        return [(i, i ^ s) for i in range(n)]

    other_core = [(i, i ^ 1) for i in range(tm)]
    got = lax.ppermute(send, "tm", other_core)
    own, *sends = call(
        core_sum_kernel, "core_sum", [keep, got],
        [shape((n, block, lanes), F32)] + [shape((n, block, lanes), BF16)] * (chips - 1), 0, 4 * big,
    )
    gots = [lax.ppermute(x, "tm", other_chip(s)) for s, x in enumerate(sends, 1)]

    out_frames = call(
        functools.partial(out_kernel, corners), "temporal_forward",
        [clip_frames, dilation, act, *act_around, temporal.reshape(3 * channels, channels), frames_in],
        shape(frames_in.shape, BF16), 6 * big * channels, 10 * big, [windows],
    )
    own, out_frames = lax.optimization_barrier((own, out_frames))

    own, *sends = call(
        functools.partial(sum_split_kernel, chips - 1), "plane_sum", [own, *gots],
        [shape((block, lanes), F32)] + [shape((block, lanes), BF16)] * (n - 1), 0, big,
    )
    gots = [lax.ppermute(x, "space", other_plane(s)) for s, x in enumerate(sends, 1)]
    own = call(
        functools.partial(sum_kernel, n - 1), "line_sum", [own, *gots], shape((block, lanes), BF16), 0, big
    )
    gots = [lax.ppermute(own, "space", other_plane(s)) for s in range(1, n)]
    own = call(
        functools.partial(place_kernel, "space", 0), "line_place", [own, *gots], shape((n, block, lanes), BF16), 0, big
    )
    gots = [lax.ppermute(own, "tm", other_chip(s)) for s in range(1, chips)]

    grad_above, grad_below = neighbours("space", first_rows, last_rows)
    back_weights = spatial.transpose(1, 0, 3, 2).reshape(3, 3 * channels, channels)
    in_grad = call(
        conv_back_kernel, "conv_backward", [grad_conv, grad_above, grad_below, cotangent, back_weights],
        shape(frames_in.shape, BF16), 18 * big * channels, 8 * big, [windows],
    )
    own, in_grad = lax.optimization_barrier((own, in_grad))

    own = call(
        functools.partial(place_kernel, "tm", 1), "plane_place", [own, *gots], shape((chips, n, block, lanes), BF16), 0, big
    )
    got = lax.ppermute(own, "tm", other_core)
    spatial_grad, temporal_grad = call(
        finish_kernel, "finish", [own, got], [shape(spatial.shape, F32), shape(temporal.shape, F32)], 0, 4 * big
    )
    return (out_frames, in_grad, spatial_grad, temporal_grad)


def solution(mesh):
    tiles = P("tm", "space", None, None)
    return jax.shard_map(
        per_device,
        mesh=mesh,
        in_specs=(tiles, tiles, P(), P(), P(), P(), P(), P()),
        out_specs=(tiles, tiles, P(), P()),
        check_vma=False,
    )
```

time: 247 us -> 160 us (0.65)
  waiting for transfers between devices: 69.6 us -> 30.7 us
  local copies, waits for them, and re-layouts: 42.4 us -> 12.5 us
  other arithmetic: 10.6 us -> 0 us
  Pallas kernels: 59 us -> 50 us
    ppermute x20 -> x24, waiting for transfers between devices: 39.3 us -> 11.9 us  [the longest x3 3.96 us: per_device(): lax.ppermute(x, 'space', other_plane(s))]
    unnamed x104 -> x44, local copies, waits for them, and re-layouts: 27.3 us -> 8.41 us
    ppermute x8 -> x4, waiting for transfers between devices: 20.3 us -> 7.43 us  [neighbours(): return (lax.ppermute(high, axis, up), lax.ppermute(low, axis, down))]
    ppermute x20 -> x24, starting transfers between devices: 34.8 us -> 47.3 us  [the longest x2 14.4 us: frame_neighbours(): high = lax.ppermute(high, 'tm', [(7, 4), (0, 3)])]
    ppermute x8 -> x4, starting transfers between devices: 21.5 us -> 11.6 us  [neighbours(): return (lax.ppermute(high, axis, up), lax.ppermute(low, axis, down))]
    pallas_call x8 -> x14, Pallas kernels: 59 us -> 50 us  [call(): pl.pallas_call(kernel, in_specs=[smem if x.dtype == jnp.int32 else vmem f...]
    select_n x2 -> x0, other arithmetic: 5.27 us -> none  [frame_neighbours(): prev_high = lax.ppermute(jnp.where(me == 7, relayed, high), 'tm', up)]
    slice x7 -> x2, local copies, waits for them, and re-layouts: 8.07 us -> 3.21 us  [frame_neighbours(): high = lax.ppermute(x[frames // 2:], 'tm', [(3, 7), (4, 0)])]
  transfers between devices with their start and end apart: 34 -> 34, of which waited for: 14 -> 12; matrix products, arithmetic and copies ran while one was open for 7% -> 3% of each run, Pallas kernels for 15% -> 30%
where the time goes in v3:
time: 160 us
  starting transfers between devices  65.5 us (41%)
  Pallas kernels  50 us (31%)
  waiting for transfers between devices  30.7 us (19%)
  local copies, waits for them, and re-layouts  12.5 us (8%)
    pallas_call x14, Pallas kernels, call(): pl.pallas_call(kernel, in_specs=[smem if x.dtype == jnp.int32 else vmem f...  50 us
    ppermute x2, starting transfers between devices, frame_neighbours(): high = lax.ppermute(high, 'tm', [(7, 4), (0, 3)])  14.4 us
    ppermute x4, starting transfers between devices, neighbours(): return (lax.ppermute(high, axis, up), lax.ppermute(low, axis, down))  11.6 us
    ppermute x6, waiting for transfers between devices, spread_parts(): lax.ppermute(part, axis, [(i, (i + s) % size) for i in range(size)])  11.3 us
    ppermute x2, starting transfers between devices, frame_neighbours(): prev = lax.ppermute(x, 'tm', [(i, i + 1) for i in near])  9.12 us
    unnamed x44, local copies, waits for them, and re-layouts  8.41 us
    ppermute x4, waiting for transfers between devices, neighbours(): return (lax.ppermute(high, axis, up), lax.ppermute(low, axis, down))  7.43 us
    ppermute x6, starting transfers between devices, spread_parts(): lax.ppermute(part, axis, [(i, (i + s) % size) for i in range(size)])  6.57 us
  transfers between devices with their start and end apart: 34, of which 12 were waited for; matrix products, arithmetic and copies ran while one was open for 3% of the time, Pallas kernels for 30%

profile of v3, /device:TPU:0, one launch (start us, length us, event | category | flops | bytes accessed | tf_op | source)
XLA Modules:
  0.0 159.8 jit_solution(6544659811813112579)
XLA Ops:
  0.7 1.6 collective-permute-start.5
  2.2 1.7 %fusion.1 = (bf16[4,8,64,256]{3,2,1,0:T(8,128)(2,1)S(1)}, bf16[4,8,64,256]{3,2,1,0:T(8,128)(2,1)S(1)}) fusion(bf16[8,8,64,256]{3,2,1,0:T(8,128)(2,1)} %cot_ref.1), kind=kLoop, calls=%fused_computation.1 | loop fusion | bytes 4194304 | tf_op jit(solution)/shard_map/slice | solution.py:377
  3.9 1.3 collective-permute-start.8
  5.2 4.7 %collective-permute-start.6 = (bf16[8,512,256]{2,1,0:T(8,128)(2,1)}, bf16[8,512,256]{2,1,0:T(8,128)(2,1)}, u32[]{:S(2)}, u32[]{:S(2)}) collective-permute-start(bf16[8,512,256]{2,1,0:T(8,128)(2,1)} %bitcast.2.own), channel_id=1, source_target_pairs={{0,4},{4,8},{8,12},{16,20},{20,24},{24,28},{1,5},{5,9},{9,13},{17,... | collective-permute-start | bytes 6291464 | tf_op jit(solution)/shard_map/ppermute | solution.py:375
  10.0 4.9 %collective-permute-start = (bf16[8,1,64,256]{3,2,1,0:T(8,128)(2,1)S(1)}, bf16[8,1,64,256]{3,2,1,0:T(8,128)(2,1)S(1)}, u32[]{:S(2)}, u32[]{:S(2)}) collective-permute-start(bf16[8,1,64,256]{3,2,1,0:T(8,128)(2,1)S(1)} %get-tuple-element.67), channel_id=1, source_target_pairs={{0,1},{1,2},{2,3},{4,5},{5,6},{6,7},{8,9},{9,10},{10,11},{12,13},{... | collective-permute-start | bytes 786440 | tf_op jit(solution)/shard_map/ppermute | solution.py:366
  14.9 1.3 collective-permute-start.1
  16.2 4.2 %collective-permute-done.above_ref = bf16[8,1,64,256]{3,2,1,0:T(8,128)(2,1)S(1)} collective-permute-done((bf16[8,1,64,256]{3,2,1,0:T(8,128)(2,1)S(1)}, bf16[8,1,64,256]{3,2,1,0:T(8,128)(2,1)S(1)}, u32[]{:S(2)}, u32[]{:S(2)}) %collective-permute-start) | collective-permute-done | bytes 262176 | tf_op jit(solution)/shard_map/ppermute | solution.py:366
  20.4 0.8 collective-permute-start.7
  21.2 3.3 %collective-permute-done.1.below_ref = bf16[8,1,64,256]{3,2,1,0:T(8,128)(2,1)S(1)} collective-permute-done((bf16[8,1,64,256]{3,2,1,0:T(8,128)(2,1)S(1)}, bf16[8,1,64,256]{3,2,1,0:T(8,128)(2,1)S(1)}, u32[]{:S(2)}, u32[]{:S(2)}) %collective-permute-start.1) | collective-permute-done | bytes 262176 | tf_op jit(solution)/shard_map/ppermute | solution.py:366
  24.5 5.6 %conv_forward.1 = (f32[8,512,256]{2,1,0:T(8,128)S(1)}, f32[8,2,256]{2,1,0:T(2,128)S(1)}) custom-call(bf16[8,8,64,256]{3,2,1,0:T(8,128)(2,1)S(1)} %copy-done, bf16[8,1,64,256]{3,2,1,0:T(8,128)(2,1)S(1)} %collective-permute-done.above_ref, bf16[8,1,64,256]{3,2,1,0:T(8,128)(2,1)S(1)} %collective-permute-done.1.below_ref, bf16[3,3,256,256]{3,2,1,0:T(8,128)(2,1)S(1)} %copy-done.11), custom_call_target="tpu_custom_call" | custom-call | flops 4831838208 | bytes 8388608 | tf_op jit(solution)/shard_map/conv_forward/pallas_call | solution.py:20
  30.1 1.6 %collective-permute-start.2 = (f32[8,2,256]{2,1,0:T(2,128)S(1)}, f32[8,2,256]{2,1,0:T(2,128)S(1)}, u32[]{:S(2)}, u32[]{:S(2)}) collective-permute-start(f32[8,2,256]{2,1,0:T(2,128)S(1)} %get-tuple-element.33.refs_0_), channel_id=1, source_target_pairs={{0,1},{1,2},{2,3},{3,0},{4,5},{5,6},{6,7},{7,4},{8,9},{9,10},{10,1... | collective-permute-start | bytes 49160 | tf_op jit(solution)/shard_map/ppermute | solution.py:386
  31.8 4.0 %collective-permute-done.2.refs_1_ = f32[8,2,256]{2,1,0:T(2,128)S(1)} collective-permute-done((f32[8,2,256]{2,1,0:T(2,128)S(1)}, f32[8,2,256]{2,1,0:T(2,128)S(1)}, u32[]{:S(2)}, u32[]{:S(2)}) %collective-permute-start.2) | collective-permute-done | bytes 16416 | tf_op jit(solution)/shard_map/ppermute | solution.py:386
  35.7 0.9 collective-permute-start.3
  36.6 3.8 %collective-permute-done.3.refs_2_ = f32[8,2,256]{2,1,0:T(2,128)S(1)} collective-permute-done((f32[8,2,256]{2,1,0:T(2,128)S(1)}, f32[8,2,256]{2,1,0:T(2,128)S(1)}, u32[]{:S(2)}, u32[]{:S(2)}) %collective-permute-start.3) | collective-permute-done | bytes 16416 | tf_op jit(solution)/shard_map/ppermute | solution.py:386
  40.4 0.2 collective-permute-start.4
  40.6 3.5 %collective-permute-done.4.refs_3_ = f32[8,2,256]{2,1,0:T(2,128)S(1)} collective-permute-done((f32[8,2,256]{2,1,0:T(2,128)S(1)}, f32[8,2,256]{2,1,0:T(2,128)S(1)}, u32[]{:S(2)}, u32[]{:S(2)}) %collective-permute-start.4) | collective-permute-done | bytes 16416 | tf_op jit(solution)/shard_map/ppermute | solution.py:386
  44.1 6.1 %activation.1 = (bf16[8,512,256]{2,1,0:T(8,128)(2,1)S(1)}, bf16[8,512,256]{2,1,0:T(8,128)(2,1)S(1)}, bf16[8,512,256]{2,1,0:T(8,128)(2,1)S(1)}) custom-call(s32[2]{0:T(128)S(1)} %copy-done.15, f32[8,2,256]{2,1,0:T(2,128)S(1)} %get-tuple-element.33.refs_0_, f32[8,2,256]{2,1,0:T(2,128)S(1)} %collective-permute-done.2.refs_1_, ...), custom_call_target="tpu_custom_call" | custom-call | flops 10485760 | bytes 10485760 | tf_op jit(solution)/shard_map/activation/pallas_call | solution.py:20
  50.3 2.3 %collective-permute-start.9 = (bf16[4,512,256]{2,1,0:T(8,128)(2,1)}, bf16[4,512,256]{2,1,0:T(8,128)(2,1)}, u32[]{:S(2)}, u32[]{:S(2)}) collective-permute-start(bf16[4,512,256]{2,1,0:T(8,128)(2,1)} %collective-permute-done.8), channel_id=1, source_target_pairs={{28,16},{0,12},{29,17},{1,13},{30,18},{2,14},{31,19},{3,15}} | collective-permute-start | bytes 3145736 | tf_op jit(solution)/shard_map/ppermute | solution.py:379
  52.6 1.5 fusion
  54.1 1.3 collective-permute-start.17
  55.4 1.0 copy-done.13
  56.4 1.3 collective-permute-start.14
  57.8 1.3 copy-done.3
  59.1 4.4 %collective-permute-start.15 = (bf16[8,512,256]{2,1,0:T(8,128)(2,1)S(1)}, bf16[8,512,256]{2,1,0:T(8,128)(2,1)}, u32[]{:S(2)}, u32[]{:S(2)}) collective-permute-start(bf16[8,512,256]{2,1,0:T(8,128)(2,1)S(1)} %get-tuple-element.35.act_ref.own), channel_id=1, source_target_pairs={{0,4},{4,8},{8,12},{16,20},{20,24},{24,28},{1,5},{5,9},{9,13},{17,... | collective-permute-start | bytes 6291464 | tf_op jit(solution)/shard_map/ppermute | solution.py:375
  63.5 0.2 copy.12
  63.6 1.6 copy-done.1
  65.2 2.7 %turned.1 = (bf16[768,4096]{1,0:T(8,128)(2,1)S(1)}, bf16[256,4096]{1,0:T(8,128)(2,1)S(1)}) custom-call(bf16[8,8,64,256]{3,2,1,0:T(8,128)(2,1)S(1)} %copy-done.1, bf16[8,1,64,256]{3,2,1,0:T(8,128)(2,1)S(1)} %collective-permute-done.above_ref, bf16[8,1,64,256]{3,2,1,0:T(8,128)(2,1)S(1)} %collective-permute-done.1.below_ref, ...), custom_call_target="tpu_custom_call" | custom-call | bytes 12582912 | tf_op jit(solution)/shard_map/turned/pallas_call | solution.py:20
  68.0 1.6 copy-done.8
  69.6 1.2 copy-done.14
  70.8 6.1 %grad_activation.1 = (bf16[8,512,256]{2,1,0:T(8,128)(2,1)S(1)}, bf16[4096,768]{1,0:T(8,128)(2,1)S(1)}, f32[8,2,256]{2,1,0:T(2,128)S(1)}) custom-call(s32[2]{0:T(128)S(1)} %copy-done.15, s32[2]{0:T(128)S(1)} %copy-done.16, bf16[8,512,256]{2,1,0:T(8,128)(2,1)} %bitcast.2.own, bf16[8,512,256]{2,1,0:T(8,128)(2,1)S(1)} %copy-done.4, ...), custom_call_target="tpu_custom_call" | custom-call | flops 1610612736 | bytes 16777216 | tf_op jit(solution)/shard_map/grad_activation/pallas_call | solution.py:20
  77.0 3.3 %collective-permute-start.11 = (f32[8,2,256]{2,1,0:T(2,128)S(1)}, f32[8,2,256]{2,1,0:T(2,128)S(1)}, u32[]{:S(2)}, u32[]{:S(2)}) collective-permute-start(f32[8,2,256]{2,1,0:T(2,128)S(1)} %get-tuple-element.42.refs_4_), channel_id=1, source_target_pairs={{0,2},{1,3},{2,0},{3,1},{4,6},{5,7},{6,4},{7,5},{8,10},{9,11},{10,... | collective-permute-start | bytes 49160 | tf_op jit(solution)/shard_map/ppermute | solution.py:386
  80.3 0.5 collective-permute-start.12
  80.8 1.8 %temporal_grad.1.temporal_ref = f32[256,768]{1,0:T(8,128)S(1)} custom-call(bf16[256,4096]{1,0:T(8,128)(2,1)S(1)} %get-tuple-element.40.at_ref, bf16[4096,768]{1,0:T(8,128)(2,1)S(1)} %get-tuple-element.41.cat_ref), custom_call_target="tpu_custom_call" | custom-call | flops 1610612736 | bytes 8388608 | tf_op jit(solution)/shard_map/temporal_grad/pallas_call | solution.py:20
  82.7 0.7 collective-permute-start.16
  83.4 12.1 %collective-permute-start.18 = (bf16[4,512,256]{2,1,0:T(8,128)(2,1)}, bf16[4,512,256]{2,1,0:T(8,128)(2,1)S(1)}, u32[]{:S(2)}, u32[]{:S(2)}) collective-permute-start(bf16[4,512,256]{2,1,0:T(8,128)(2,1)} %collective-permute-done.17), channel_id=1, source_target_pairs={{28,16},{0,12},{29,17},{1,13},{30,18},{2,14},{31,19},{3,15}} | collective-permute-start | bytes 3145736 | tf_op jit(solution)/shard_map/ppermute | solution.py:379
  95.5 9.9 %weight_grad.1 = (bf16[8,512,256]{2,1,0:T(8,128)(2,1)S(1)}, bf16[8,1,64,256]{3,2,1,0:T(8,128)(2,1)S(1)}, bf16[8,1,64,256]{3,2,1,0:T(8,128)(2,1)S(1)}, bf16[4,4,3...) custom-call(bf16[768,4096]{1,0:T(8,128)(2,1)S(1)} %get-tuple-element.36.xt_ref, bf16[8,512,256]{2,1,0:T(8,128)(2,1)S(1)} %copy-done.6, ...), custom_call_target="tpu_custom_call" | custom-call | flops 4831838208 | bytes 12582912 | tf_op jit(solution)/shard_map/weight_grad/pallas_call | solution.py:20
  105.5 0.1 collective-permute-start.13
  105.6 2.3 %collective-permute-done.13.got_ref = bf16[4,4,32,768]{3,2,1,0:T(8,128)(2,1)S(1)} collective-permute-done((bf16[4,4,32,768]{3,2,1,0:T(8,128)(2,1)S(1)}, bf16[4,4,32,768]{3,2,1,0:T(8,128)(2,1)S(1)}, u32[]{:S(2)}, u32[]{:S(2)}) %collective-permute-start.13) | collective-permute-done | bytes 786464 | tf_op jit(solution)/shard_map/ppermute | solution.py:456
  107.8 0.2 core_sum.1
  108.0 0.1 collective-permute-start.19
  108.1 0.6 collective-permute-start.20
  108.7 2.9 %collective-permute-start.21 = (bf16[4,32,768]{2,1,0:T(8,128)(2,1)S(1)}, bf16[4,32,768]{2,1,0:T(8,128)(2,1)S(1)}, u32[]{:S(2)}, u32[]{:S(2)}) collective-permute-start(bf16[4,32,768]{2,1,0:T(8,128)(2,1)S(1)} %get-tuple-element.50), channel_id=1, source_target_pairs={{0,24},{4,28},{8,16},{12,20},{16,8},{20,12},{24,0},{28,4},{1,25},{... | collective-permute-start | bytes 589832 | tf_op jit(solution)/shard_map/ppermute | solution.py:461
  111.6 3.9 %collective-permute-start.28 = (bf16[8,1,64,256]{3,2,1,0:T(8,128)(2,1)S(1)}, bf16[8,1,64,256]{3,2,1,0:T(8,128)(2,1)S(1)}, u32[]{:S(2)}, u32[]{:S(2)}) collective-permute-start(bf16[8,1,64,256]{3,2,1,0:T(8,128)(2,1)S(1)} %get-tuple-element.56), channel_id=1, source_target_pairs={{0,1},{1,2},{2,3},{4,5},{5,6},{6,7},{8,9},{9,10},{10,11},{12,13},{... | collective-permute-start | bytes 786440 | tf_op jit(solution)/shard_map/ppermute | solution.py:366
  115.5 1.5 collective-permute-start.29
  117.0 6.9 %temporal_forward.1 = bf16[8,8,64,256]{3,2,1,0:T(8,128)(2,1)} custom-call(s32[2]{0:T(128)S(1)} %copy-done.15, s32[2]{0:T(128)S(1)} %copy-done.16, bf16[8,512,256]{2,1,0:T(8,128)(2,1)S(1)} %get-tuple-element.35.act_ref.own, bf16[8,512,256]{2,1,0:T(8,128)(2,1)} %collective-permute-done.14.nxt, bf16[8,512,256]{2,1,0:T(8,128)(2,1)} %collective-permute-done.15.prv, ...), custom_call_target="tpu_custom_call" | custom-call | flops 1610612736 | bytes 10485760 | tf_op jit(solution)/shard_map/temporal_forward/pallas_call | solution.py:20
  123.9 0.1 plane_sum.1
  124.0 2.7 %collective-permute-start.22 = (bf16[32,768]{1,0:T(8,128)(2,1)S(1)}, bf16[32,768]{1,0:T(8,128)(2,1)S(1)}, u32[]{:S(2)}, u32[]{:S(2)}) collective-permute-start(bf16[32,768]{1,0:T(8,128)(2,1)S(1)} %get-tuple-element.52), channel_id=1, source_target_pairs={{0,1},{1,0},{2,3},{3,2},{4,5},{5,4},{6,7},{7,6},{8,9},{9,8},{10,11... | collective-permute-start | bytes 147464 | tf_op jit(solution)/shard_map/ppermute | solution.py:474
  126.7 0.5 collective-permute-start.23
  127.2 1.9 %collective-permute-start.24 = (bf16[32,768]{1,0:T(8,128)(2,1)S(1)}, bf16[32,768]{1,0:T(8,128)(2,1)S(1)}, u32[]{:S(2)}, u32[]{:S(2)}) collective-permute-start(bf16[32,768]{1,0:T(8,128)(2,1)S(1)} %get-tuple-element.54), channel_id=1, source_target_pairs={{0,3},{1,2},{2,1},{3,0},{4,7},{5,6},{6,5},{7,4},{8,11},{9,10},{10,... | collective-permute-start | bytes 147464 | tf_op jit(solution)/shard_map/ppermute | solution.py:474
  129.2 2.6 %collective-permute-done.23.refs_1_ = bf16[32,768]{1,0:T(8,128)(2,1)S(1)} collective-permute-done((bf16[32,768]{1,0:T(8,128)(2,1)S(1)}, bf16[32,768]{1,0:T(8,128)(2,1)S(1)}, u32[]{:S(2)}, u32[]{:S(2)}) %collective-permute-start.23) | collective-permute-done | bytes 49184 | tf_op jit(solution)/shard_map/ppermute | solution.py:474
  131.8 1.4 collective-permute-done.24.refs_2_
  133.3 2.6 %collective-permute-start.26 = (bf16[32,768]{1,0:T(8,128)(2,1)S(1)}, bf16[32,768]{1,0:T(8,128)(2,1)S(1)}, u32[]{:S(2)}, u32[]{:S(2)}) collective-permute-start(bf16[32,768]{1,0:T(8,128)(2,1)S(1)} %line_sum.1.refs_0_), channel_id=1, source_target_pairs={{0,2},{1,3},{2,0},{3,1},{4,6},{5,7},{6,4},{7,5},{8,10},{9,11},{10,... | collective-permute-start | bytes 147464 | tf_op jit(solution)/shard_map/ppermute | solution.py:478
  135.8 1.8 %collective-permute-start.27 = (bf16[32,768]{1,0:T(8,128)(2,1)S(1)}, bf16[32,768]{1,0:T(8,128)(2,1)S(1)}, u32[]{:S(2)}, u32[]{:S(2)}) collective-permute-start(bf16[32,768]{1,0:T(8,128)(2,1)S(1)} %line_sum.1.refs_0_), channel_id=1, source_target_pairs={{0,3},{1,2},{2,1},{3,0},{4,7},{5,6},{6,5},{7,4},{8,11},{9,10},{10,... | collective-permute-start | bytes 147464 | tf_op jit(solution)/shard_map/ppermute | solution.py:478
  137.6 0.7 copy.13
  138.4 0.2 collective-permute-done.26.refs_2_
  138.6 3.1 %collective-permute-done.27.refs_3_ = bf16[32,768]{1,0:T(8,128)(2,1)S(1)} collective-permute-done((bf16[32,768]{1,0:T(8,128)(2,1)S(1)}, bf16[32,768]{1,0:T(8,128)(2,1)S(1)}, u32[]{:S(2)}, u32[]{:S(2)}) %collective-permute-start.27) | collective-permute-done | bytes 49184 | tf_op jit(solution)/shard_map/ppermute | solution.py:478
  141.8 0.2 collective-permute-start.30
  141.9 0.5 collective-permute-start.31
  142.4 2.9 %collective-permute-start.32 = (bf16[4,32,768]{2,1,0:T(8,128)(2,1)S(1)}, bf16[4,32,768]{2,1,0:T(8,128)(2,1)S(1)}, u32[]{:S(2)}, u32[]{:S(2)}) collective-permute-start(bf16[4,32,768]{2,1,0:T(8,128)(2,1)S(1)} %line_place.1.refs_0_), channel_id=1, source_target_pairs={{0,24},{4,28},{8,16},{12,20},{16,8},{20,12},{24,0},{28,4},{1,25},{... | collective-permute-start | bytes 589832 | tf_op jit(solution)/shard_map/ppermute | solution.py:482
  145.3 1.6 copy-done.20
  146.9 8.6 %conv_backward.1 = bf16[8,8,64,256]{3,2,1,0:T(8,128)(2,1)} custom-call(bf16[8,512,256]{2,1,0:T(8,128)(2,1)S(1)} %copy-done.20, bf16[8,1,64,256]{3,2,1,0:T(8,128)(2,1)S(1)} %collective-permute-done.28.above_ref, bf16[8,1,64,256]{3,2,1,0:T(8,128)(2,1)} %collective-permute-done.29.below_ref, bf16[8,8,64,256]{3,2,1,0:T(8,128)(2,1)} %cot_ref.1, ...), custom_call_target="tpu_custom_call" | custom-call | flops 4831838208 | bytes 8388608 | tf_op jit(solution)/shard_map/conv_backward/pallas_call | solution.py:20
  155.6 0.1 collective-permute-start.33
  155.7 2.3 %collective-permute-done.33.got_ref = bf16[4,4,32,768]{3,2,1,0:T(8,128)(2,1)S(1)} collective-permute-done((bf16[4,4,32,768]{3,2,1,0:T(8,128)(2,1)S(1)}, bf16[4,4,32,768]{3,2,1,0:T(8,128)(2,1)S(1)}, u32[]{:S(2)}, u32[]{:S(2)}) %collective-permute-start.33) | collective-permute-done | bytes 786464 | tf_op jit(solution)/shard_map/ppermute | solution.py:495
  157.9 1.9 %finish.1 = (f32[3,3,256,256]{3,2,1,0:T(8,128)}, f32[3,256,256]{2,1,0:T(8,128)}) custom-call(bf16[4,4,32,768]{3,2,1,0:T(8,128)(2,1)S(1)} %plane_place.1.mine_ref, bf16[4,4,32,768]{3,2,1,0:T(8,128)(2,1)S(1)} %collective-permute-done.33.got_ref), custom_call_target="tpu_custom_call" | custom-call | bytes 4194304 | tf_op jit(solution)/shard_map/finish/pallas_call | solution.py:20
  (67 shorter events, 0.5 us)
Async XLA Ops:
  0.6 9.3 %copy-start = (bf16[8,8,64,256]{3,2,1,0:T(8,128)(2,1)S(1)}, bf16[8,8,64,256]{3,2,1,0:T(8,128)(2,1)}, u32[]{:S(2)}) copy-start(bf16[8,8,64,256]{3,2,1,0:T(8,128)(2,1)} %refs_3_.1) | copy-start | bytes 6291460
  0.6 23.9 %copy-start.11 = (bf16[3,3,256,256]{3,2,1,0:T(8,128)(2,1)S(1)}, bf16[3,3,256,256]{3,2,1,0:T(8,128)(2,1)}, u32[]{:S(2)}) copy-start(bf16[3,3,256,256]{3,2,1,0:T(8,128)(2,1)} %w_ref.1) | copy-start | bytes 3538948
  0.7 57.1 %collective-permute-start.5 = (bf16[8,512,256]{2,1,0:T(8,128)(2,1)}, bf16[8,512,256]{2,1,0:T(8,128)(2,1)S(1)}, u32[]{:S(2)}, u32[]{:S(2)}) collective-permute-start(bf16[8,512,256]{2,1,0:T(8,128)(2,1)} %bitcast.2.own), channel_id=1, source_target_pairs={{4,0},{8,4},{12,8},{20,16},{24,20},{28,24},{5,1},{9,5},{13,9},{21,... | collective-permute-start | bytes 6291464 | tf_op jit(solution)/shard_map/ppermute | solution.py:376
  3.9 46.4 %collective-permute-start.8 = (bf16[4,512,256]{2,1,0:T(8,128)(2,1)S(1)}, bf16[4,512,256]{2,1,0:T(8,128)(2,1)}, u32[]{:S(2)}, u32[]{:S(2)}) collective-permute-start(bf16[4,512,256]{2,1,0:T(8,128)(2,1)S(1)} %bitcast.18), channel_id=1, source_target_pairs={{12,28},{16,0},{13,29},{17,1},{14,30},{18,2},{15,31},{19,3}} | collective-permute-start | bytes 3145736 | tf_op jit(solution)/shard_map/ppermute | solution.py:377
  5.2 62.8 %collective-permute-start.6 = (bf16[8,512,256]{2,1,0:T(8,128)(2,1)}, bf16[8,512,256]{2,1,0:T(8,128)(2,1)}, u32[]{:S(2)}, u32[]{:S(2)}) collective-permute-start(bf16[8,512,256]{2,1,0:T(8,128)(2,1)} %bitcast.2.own), channel_id=1, source_target_pairs={{0,4},{4,8},{8,12},{16,20},{20,24},{24,28},{1,5},{5,9},{9,13},{17,... | collective-permute-start | bytes 6291464 | tf_op jit(solution)/shard_map/ppermute | solution.py:375
  10.0 10.4 %collective-permute-start = (bf16[8,1,64,256]{3,2,1,0:T(8,128)(2,1)S(1)}, bf16[8,1,64,256]{3,2,1,0:T(8,128)(2,1)S(1)}, u32[]{:S(2)}, u32[]{:S(2)}) collective-permute-start(bf16[8,1,64,256]{3,2,1,0:T(8,128)(2,1)S(1)} %get-tuple-element.67), channel_id=1, source_target_pairs={{0,1},{1,2},{2,3},{4,5},{5,6},{6,7},{8,9},{9,10},{10,11},{12,13},{... | collective-permute-start | bytes 786440 | tf_op jit(solution)/shard_map/ppermute | solution.py:366
  14.9 9.6 %collective-permute-start.1 = (bf16[8,1,64,256]{3,2,1,0:T(8,128)(2,1)S(1)}, bf16[8,1,64,256]{3,2,1,0:T(8,128)(2,1)S(1)}, u32[]{:S(2)}, u32[]{:S(2)}) collective-permute-start(bf16[8,1,64,256]{3,2,1,0:T(8,128)(2,1)S(1)} %get-tuple-element.66), channel_id=1, source_target_pairs={{1,0},{2,1},{3,2},{5,4},{6,5},{7,6},{9,8},{10,9},{11,10},{13,12},{... | collective-permute-start | bytes 786440 | tf_op jit(solution)/shard_map/ppermute | solution.py:366
  20.4 23.7 %copy-start.15 = (s32[2]{0:T(128)S(1)}, s32[2]{0:T(128)}, u32[]{:S(2)}) copy-start(s32[2]{0:T(128)} %clip_ref.5) | copy-start | bytes 28
  20.4 23.7 %copy-start.17 = (f32[256]{0:T(256)S(1)}, f32[256]{0:T(256)}, u32[]{:S(2)}) copy-start(f32[256]{0:T(256)} %param.12) | copy-start | bytes 3076
  20.4 23.7 %copy-start.18 = (f32[256]{0:T(256)S(1)}, f32[256]{0:T(256)}, u32[]{:S(2)}) copy-start(f32[256]{0:T(256)} %param.13) | copy-start | bytes 3076
  20.4 35.0 %collective-permute-start.7 = (bf16[4,512,256]{2,1,0:T(8,128)(2,1)S(1)}, bf16[4,512,256]{2,1,0:T(8,128)(2,1)S(1)}, u32[]{:S(2)}, u32[]{:S(2)}) collective-permute-start(bf16[4,512,256]{2,1,0:T(8,128)(2,1)S(1)} %bitcast.17), channel_id=1, source_target_pairs={{12,16},{16,12},{13,17},{17,13},{14,18},{18,14},{15,19},{19,15}} | collective-permute-start | bytes 3145736 | tf_op jit(solution)/shard_map/ppermute | solution.py:378
  30.1 5.6 %collective-permute-start.2 = (f32[8,2,256]{2,1,0:T(2,128)S(1)}, f32[8,2,256]{2,1,0:T(2,128)S(1)}, u32[]{:S(2)}, u32[]{:S(2)}) collective-permute-start(f32[8,2,256]{2,1,0:T(2,128)S(1)} %get-tuple-element.33.refs_0_), channel_id=1, source_target_pairs={{0,1},{1,2},{2,3},{3,0},{4,5},{5,6},{6,7},{7,4},{8,9},{9,10},{10,1... | collective-permute-start | bytes 49160 | tf_op jit(solution)/shard_map/ppermute | solution.py:386
  35.7 4.6 %collective-permute-start.3 = (f32[8,2,256]{2,1,0:T(2,128)S(1)}, f32[8,2,256]{2,1,0:T(2,128)S(1)}, u32[]{:S(2)}, u32[]{:S(2)}) collective-permute-start(f32[8,2,256]{2,1,0:T(2,128)S(1)} %get-tuple-element.33.refs_0_), channel_id=1, source_target_pairs={{0,2},{1,3},{2,0},{3,1},{4,6},{5,7},{6,4},{7,5},{8,10},{9,11},{10,... | collective-permute-start | bytes 49160 | tf_op jit(solution)/shard_map/ppermute | solution.py:386
  40.4 3.7 %collective-permute-start.4 = (f32[8,2,256]{2,1,0:T(2,128)S(1)}, f32[8,2,256]{2,1,0:T(2,128)S(1)}, u32[]{:S(2)}, u32[]{:S(2)}) collective-permute-start(f32[8,2,256]{2,1,0:T(2,128)S(1)} %get-tuple-element.33.refs_0_), channel_id=1, source_target_pairs={{0,3},{1,0},{2,1},{3,2},{4,7},{5,4},{6,5},{7,6},{8,11},{9,8},{10,9... | collective-permute-start | bytes 49160 | tf_op jit(solution)/shard_map/ppermute | solution.py:386
  50.3 3.8 %copy-start.5 = (bf16[8,512,256]{2,1,0:T(8,128)(2,1)}, bf16[8,512,256]{2,1,0:T(8,128)(2,1)S(1)}, u32[]{:S(2)}) copy-start(bf16[8,512,256]{2,1,0:T(8,128)(2,1)S(1)} %get-tuple-element.37.refs_3_.normed_ref) | copy-start | bytes 6291460
  50.3 3.8 %copy-start.7 = (bf16[8,512,256]{2,1,0:T(8,128)(2,1)}, bf16[8,512,256]{2,1,0:T(8,128)(2,1)S(1)}, u32[]{:S(2)}) copy-start(bf16[8,512,256]{2,1,0:T(8,128)(2,1)S(1)} %get-tuple-element.38.refs_4_.slope_ref) | copy-start | bytes 6291460
  50.3 17.7 %collective-permute-start.9 = (bf16[4,512,256]{2,1,0:T(8,128)(2,1)}, bf16[4,512,256]{2,1,0:T(8,128)(2,1)}, u32[]{:S(2)}, u32[]{:S(2)}) collective-permute-start(bf16[4,512,256]{2,1,0:T(8,128)(2,1)} %collective-permute-done.8), channel_id=1, source_target_pairs={{28,16},{0,12},{29,17},{1,13},{30,18},{2,14},{31,19},{3,15}} | collective-permute-start | bytes 3145736 | tf_op jit(solution)/shard_map/ppermute | solution.py:379
  52.6 10.9 %copy-start.10 = (bf16[3,256,256]{2,1,0:T(8,128)(2,1)S(1)}, bf16[3,256,256]{2,1,0:T(8,128)(2,1)}, u32[]{:S(2)}) copy-start(bf16[3,256,256]{2,1,0:T(8,128)(2,1)} %param.11) | copy-start | bytes 1179652
  54.1 26.2 %collective-permute-start.17 = (bf16[4,512,256]{2,1,0:T(8,128)(2,1)}, bf16[4,512,256]{2,1,0:T(8,128)(2,1)}, u32[]{:S(2)}, u32[]{:S(2)}) collective-permute-start(bf16[4,512,256]{2,1,0:T(8,128)(2,1)} %get-tuple-element.62), channel_id=1, source_target_pairs={{12,28},{16,0},{13,29},{17,1},{14,30},{18,2},{15,31},{19,3}} | collective-permute-start | bytes 3145736 | tf_op jit(solution)/shard_map/ppermute | solution.py:377
  55.4 1.0 copy-start.13
  56.4 52.3 %collective-permute-start.14 = (bf16[8,512,256]{2,1,0:T(8,128)(2,1)S(1)}, bf16[8,512,256]{2,1,0:T(8,128)(2,1)}, u32[]{:S(2)}, u32[]{:S(2)}) collective-permute-start(bf16[8,512,256]{2,1,0:T(8,128)(2,1)S(1)} %get-tuple-element.35.act_ref.own), channel_id=1, source_target_pairs={{4,0},{8,4},{12,8},{20,16},{24,20},{28,24},{5,1},{9,5},{13,9},{21,... | collective-permute-start | bytes 6291464 | tf_op jit(solution)/shard_map/ppermute | solution.py:376
  57.7 1.3 copy-start.3
  59.1 52.5 %collective-permute-start.15 = (bf16[8,512,256]{2,1,0:T(8,128)(2,1)S(1)}, bf16[8,512,256]{2,1,0:T(8,128)(2,1)}, u32[]{:S(2)}, u32[]{:S(2)}) collective-permute-start(bf16[8,512,256]{2,1,0:T(8,128)(2,1)S(1)} %get-tuple-element.35.act_ref.own), channel_id=1, source_target_pairs={{0,4},{4,8},{8,12},{16,20},{20,24},{24,28},{1,5},{5,9},{9,13},{17,... | collective-permute-start | bytes 6291464 | tf_op jit(solution)/shard_map/ppermute | solution.py:375
  63.6 1.6 copy-start.1
  65.2 2.8 %copy-start.4 = (bf16[8,512,256]{2,1,0:T(8,128)(2,1)S(1)}, bf16[8,512,256]{2,1,0:T(8,128)(2,1)}, u32[]{:S(2)}) copy-start(bf16[8,512,256]{2,1,0:T(8,128)(2,1)} %copy-done.3) | copy-start | bytes 6291460
  65.2 2.8 %copy-start.6 = (bf16[8,512,256]{2,1,0:T(8,128)(2,1)S(1)}, bf16[8,512,256]{2,1,0:T(8,128)(2,1)}, u32[]{:S(2)}) copy-start(bf16[8,512,256]{2,1,0:T(8,128)(2,1)} %copy-done.5) | copy-start | bytes 6291460
  65.2 2.8 %copy-start.16 = (s32[2]{0:T(128)S(1)}, s32[2]{0:T(128)}, u32[]{:S(2)}) copy-start(s32[2]{0:T(128)} %dil_ref.3) | copy-start | bytes 28
  68.0 1.6 copy-start.8
  69.6 1.2 copy-start.14
  76.9 5.8 %collective-permute-start.10 = (f32[8,2,256]{2,1,0:T(2,128)S(1)}, f32[8,2,256]{2,1,0:T(2,128)S(1)}, u32[]{:S(2)}, u32[]{:S(2)}) collective-permute-start(f32[8,2,256]{2,1,0:T(2,128)S(1)} %get-tuple-element.42.refs_4_), channel_id=1, source_target_pairs={{0,1},{1,2},{2,3},{3,0},{4,5},{5,6},{6,7},{7,4},{8,9},{9,10},{10,1... | collective-permute-start | bytes 49160 | tf_op jit(solution)/shard_map/ppermute | solution.py:386
  77.0 6.4 %collective-permute-start.11 = (f32[8,2,256]{2,1,0:T(2,128)S(1)}, f32[8,2,256]{2,1,0:T(2,128)S(1)}, u32[]{:S(2)}, u32[]{:S(2)}) collective-permute-start(f32[8,2,256]{2,1,0:T(2,128)S(1)} %get-tuple-element.42.refs_4_), channel_id=1, source_target_pairs={{0,2},{1,3},{2,0},{3,1},{4,6},{5,7},{6,4},{7,5},{8,10},{9,11},{10,... | collective-permute-start | bytes 49160 | tf_op jit(solution)/shard_map/ppermute | solution.py:386
  80.3 15.2 %collective-permute-start.12 = (f32[8,2,256]{2,1,0:T(2,128)S(1)}, f32[8,2,256]{2,1,0:T(2,128)S(1)}, u32[]{:S(2)}, u32[]{:S(2)}) collective-permute-start(f32[8,2,256]{2,1,0:T(2,128)S(1)} %get-tuple-element.42.refs_4_), channel_id=1, source_target_pairs={{0,3},{1,0},{2,1},{3,2},{4,7},{5,4},{6,5},{7,6},{8,11},{9,8},{10,9... | collective-permute-start | bytes 49160 | tf_op jit(solution)/shard_map/ppermute | solution.py:386
  80.8 1.9 %copy-start.21 = (bf16[4,512,256]{2,1,0:T(8,128)(2,1)S(1)}, bf16[4,512,256]{2,1,0:T(8,128)(2,1)}, u32[]{:S(2)}) copy-start(bf16[4,512,256]{2,1,0:T(8,128)(2,1)} %get-tuple-element.63) | copy-start | bytes 3145732
  80.8 14.7 %copy-start.9 = (bf16[8,512,256]{2,1,0:T(8,128)(2,1)S(1)}, bf16[8,512,256]{2,1,0:T(8,128)(2,1)}, u32[]{:S(2)}) copy-start(bf16[8,512,256]{2,1,0:T(8,128)(2,1)} %copy-done.7) | copy-start | bytes 6291460
  82.7 25.4 %collective-permute-start.16 = (bf16[4,512,256]{2,1,0:T(8,128)(2,1)S(1)}, bf16[4,512,256]{2,1,0:T(8,128)(2,1)S(1)}, u32[]{:S(2)}, u32[]{:S(2)}) collective-permute-start(bf16[4,512,256]{2,1,0:T(8,128)(2,1)S(1)} %copy-done.21), channel_id=1, source_target_pairs={{12,16},{16,12},{13,17},{17,13},{14,18},{18,14},{15,19},{19,15}} | collective-permute-start | bytes 3145736 | tf_op jit(solution)/shard_map/ppermute | solution.py:378
  83.4 32.1 %collective-permute-start.18 = (bf16[4,512,256]{2,1,0:T(8,128)(2,1)}, bf16[4,512,256]{2,1,0:T(8,128)(2,1)S(1)}, u32[]{:S(2)}, u32[]{:S(2)}) collective-permute-start(bf16[4,512,256]{2,1,0:T(8,128)(2,1)} %collective-permute-done.17), channel_id=1, source_target_pairs={{28,16},{0,12},{29,17},{1,13},{30,18},{2,14},{31,19},{3,15}} | collective-permute-start | bytes 3145736 | tf_op jit(solution)/shard_map/ppermute | solution.py:379
  105.5 18.4 %copy-start.19 = (bf16[8,512,256]{2,1,0:T(8,128)(2,1)}, bf16[8,512,256]{2,1,0:T(8,128)(2,1)S(1)}, u32[]{:S(2)}) copy-start(bf16[8,512,256]{2,1,0:T(8,128)(2,1)S(1)} %get-tuple-element.55.g_ref) | copy-start | bytes 6291460
  105.5 11.5 %copy-start.2 = (bf16[8,8,64,256]{3,2,1,0:T(8,128)(2,1)S(1)}, bf16[8,8,64,256]{3,2,1,0:T(8,128)(2,1)}, u32[]{:S(2)}) copy-start(bf16[8,8,64,256]{3,2,1,0:T(8,128)(2,1)} %refs_3_.1) | copy-start | bytes 6291460
  105.5 2.4 %collective-permute-start.13 = (bf16[4,4,32,768]{3,2,1,0:T(8,128)(2,1)S(1)}, bf16[4,4,32,768]{3,2,1,0:T(8,128)(2,1)S(1)}, u32[]{:S(2)}, u32[]{:S(2)}) collective-permute-start(bf16[4,4,32,768]{3,2,1,0:T(8,128)(2,1)S(1)} %get-tuple-element.44), channel_id=1, source_target_pairs={{0,4},{4,0},{8,12},{12,8},{16,20},{20,16},{24,28},{28,24},{1,5},{5... | collective-permute-start | bytes 2359304 | tf_op jit(solution)/shard_map/ppermute | solution.py:456
  108.0 15.9 %collective-permute-start.19 = (bf16[4,32,768]{2,1,0:T(8,128)(2,1)S(1)}, bf16[4,32,768]{2,1,0:T(8,128)(2,1)S(1)}, u32[]{:S(2)}, u32[]{:S(2)}) collective-permute-start(bf16[4,32,768]{2,1,0:T(8,128)(2,1)S(1)} %get-tuple-element.48), channel_id=1, source_target_pairs={{0,8},{4,12},{8,0},{12,4},{16,24},{20,28},{24,16},{28,20},{1,9},{5... | collective-permute-start | bytes 589832 | tf_op jit(solution)/shard_map/ppermute | solution.py:461
  108.1 15.8 %collective-permute-start.20 = (bf16[4,32,768]{2,1,0:T(8,128)(2,1)S(1)}, bf16[4,32,768]{2,1,0:T(8,128)(2,1)S(1)}, u32[]{:S(2)}, u32[]{:S(2)}) collective-permute-start(bf16[4,32,768]{2,1,0:T(8,128)(2,1)S(1)} %get-tuple-element.49), channel_id=1, source_target_pairs={{0,16},{4,20},{8,24},{12,28},{16,0},{20,4},{24,8},{28,12},{1,17},{... | collective-permute-start | bytes 589832 | tf_op jit(solution)/shard_map/ppermute | solution.py:461
  108.7 15.2 %collective-permute-start.21 = (bf16[4,32,768]{2,1,0:T(8,128)(2,1)S(1)}, bf16[4,32,768]{2,1,0:T(8,128)(2,1)S(1)}, u32[]{:S(2)}, u32[]{:S(2)}) collective-permute-start(bf16[4,32,768]{2,1,0:T(8,128)(2,1)S(1)} %get-tuple-element.50), channel_id=1, source_target_pairs={{0,24},{4,28},{8,16},{12,20},{16,8},{20,12},{24,0},{28,4},{1,25},{... | collective-permute-start | bytes 589832 | tf_op jit(solution)/shard_map/ppermute | solution.py:461
  111.6 33.7 %collective-permute-start.28 = (bf16[8,1,64,256]{3,2,1,0:T(8,128)(2,1)S(1)}, bf16[8,1,64,256]{3,2,1,0:T(8,128)(2,1)S(1)}, u32[]{:S(2)}, u32[]{:S(2)}) collective-permute-start(bf16[8,1,64,256]{3,2,1,0:T(8,128)(2,1)S(1)} %get-tuple-element.56), channel_id=1, source_target_pairs={{0,1},{1,2},{2,3},{4,5},{5,6},{6,7},{8,9},{9,10},{10,11},{12,13},{... | collective-permute-start | bytes 786440 | tf_op jit(solution)/shard_map/ppermute | solution.py:366
  115.5 29.8 %collective-permute-start.29 = (bf16[8,1,64,256]{3,2,1,0:T(8,128)(2,1)S(1)}, bf16[8,1,64,256]{3,2,1,0:T(8,128)(2,1)}, u32[]{:S(2)}, u32[]{:S(2)}) collective-permute-start(bf16[8,1,64,256]{3,2,1,0:T(8,128)(2,1)S(1)} %get-tuple-element.57), channel_id=1, source_target_pairs={{1,0},{2,1},{3,2},{5,4},{6,5},{7,6},{9,8},{10,9},{11,10},{13,12},{... | collective-permute-start | bytes 786440 | tf_op jit(solution)/shard_map/ppermute | solution.py:366
  123.9 13.7 %copy-start.12 = (bf16[3,3,256,256]{3,2,1,0:T(8,128)(2,1)S(1)}, bf16[3,3,256,256]{3,2,1,0:T(8,128)(2,1)}, u32[]{:S(2)}) copy-start(bf16[3,3,256,256]{3,2,1,0:T(8,128)(2,1)} %w_ref.1) | copy-start | bytes 3538948
  124.0 5.2 %collective-permute-start.22 = (bf16[32,768]{1,0:T(8,128)(2,1)S(1)}, bf16[32,768]{1,0:T(8,128)(2,1)S(1)}, u32[]{:S(2)}, u32[]{:S(2)}) collective-permute-start(bf16[32,768]{1,0:T(8,128)(2,1)S(1)} %get-tuple-element.52), channel_id=1, source_target_pairs={{0,1},{1,0},{2,3},{3,2},{4,5},{5,4},{6,7},{7,6},{8,9},{9,8},{10,11... | collective-permute-start | bytes 147464 | tf_op jit(solution)/shard_map/ppermute | solution.py:474
  126.7 5.0 %collective-permute-start.23 = (bf16[32,768]{1,0:T(8,128)(2,1)S(1)}, bf16[32,768]{1,0:T(8,128)(2,1)S(1)}, u32[]{:S(2)}, u32[]{:S(2)}) collective-permute-start(bf16[32,768]{1,0:T(8,128)(2,1)S(1)} %get-tuple-element.53), channel_id=1, source_target_pairs={{0,2},{1,3},{2,0},{3,1},{4,6},{5,7},{6,4},{7,5},{8,10},{9,11},{10,... | collective-permute-start | bytes 147464 | tf_op jit(solution)/shard_map/ppermute | solution.py:474
  127.2 5.9 %collective-permute-start.24 = (bf16[32,768]{1,0:T(8,128)(2,1)S(1)}, bf16[32,768]{1,0:T(8,128)(2,1)S(1)}, u32[]{:S(2)}, u32[]{:S(2)}) collective-permute-start(bf16[32,768]{1,0:T(8,128)(2,1)S(1)} %get-tuple-element.54), channel_id=1, source_target_pairs={{0,3},{1,2},{2,1},{3,0},{4,7},{5,6},{6,5},{7,4},{8,11},{9,10},{10,... | collective-permute-start | bytes 147464 | tf_op jit(solution)/shard_map/ppermute | solution.py:474
  133.2 5.2 %collective-permute-start.25 = (bf16[32,768]{1,0:T(8,128)(2,1)S(1)}, bf16[32,768]{1,0:T(8,128)(2,1)S(1)}, u32[]{:S(2)}, u32[]{:S(2)}) collective-permute-start(bf16[32,768]{1,0:T(8,128)(2,1)S(1)} %line_sum.1.refs_0_), channel_id=1, source_target_pairs={{0,1},{1,0},{2,3},{3,2},{4,5},{5,4},{6,7},{7,6},{8,9},{9,8},{10,11... | collective-permute-start | bytes 147464 | tf_op jit(solution)/shard_map/ppermute | solution.py:478
  133.3 5.3 %collective-permute-start.26 = (bf16[32,768]{1,0:T(8,128)(2,1)S(1)}, bf16[32,768]{1,0:T(8,128)(2,1)S(1)}, u32[]{:S(2)}, u32[]{:S(2)}) collective-permute-start(bf16[32,768]{1,0:T(8,128)(2,1)S(1)} %line_sum.1.refs_0_), channel_id=1, source_target_pairs={{0,2},{1,3},{2,0},{3,1},{4,6},{5,7},{6,4},{7,5},{8,10},{9,11},{10,... | collective-permute-start | bytes 147464 | tf_op jit(solution)/shard_map/ppermute | solution.py:478
  135.8 5.9 %collective-permute-start.27 = (bf16[32,768]{1,0:T(8,128)(2,1)S(1)}, bf16[32,768]{1,0:T(8,128)(2,1)S(1)}, u32[]{:S(2)}, u32[]{:S(2)}) collective-permute-start(bf16[32,768]{1,0:T(8,128)(2,1)S(1)} %line_sum.1.refs_0_), channel_id=1, source_target_pairs={{0,3},{1,2},{2,1},{3,0},{4,7},{5,6},{6,5},{7,4},{8,11},{9,10},{10,... | collective-permute-start | bytes 147464 | tf_op jit(solution)/shard_map/ppermute | solution.py:478
  141.8 13.7 %collective-permute-start.30 = (bf16[4,32,768]{2,1,0:T(8,128)(2,1)S(1)}, bf16[4,32,768]{2,1,0:T(8,128)(2,1)S(1)}, u32[]{:S(2)}, u32[]{:S(2)}) collective-permute-start(bf16[4,32,768]{2,1,0:T(8,128)(2,1)S(1)} %line_place.1.refs_0_), channel_id=1, source_target_pairs={{0,8},{4,12},{8,0},{12,4},{16,24},{20,28},{24,16},{28,20},{1,9},{5... | collective-permute-start | bytes 589832 | tf_op jit(solution)/shard_map/ppermute | solution.py:482
  141.9 13.6 %collective-permute-start.31 = (bf16[4,32,768]{2,1,0:T(8,128)(2,1)S(1)}, bf16[4,32,768]{2,1,0:T(8,128)(2,1)S(1)}, u32[]{:S(2)}, u32[]{:S(2)}) collective-permute-start(bf16[4,32,768]{2,1,0:T(8,128)(2,1)S(1)} %line_place.1.refs_0_), channel_id=1, source_target_pairs={{0,16},{4,20},{8,24},{12,28},{16,0},{20,4},{24,8},{28,12},{1,17},{... | collective-permute-start | bytes 589832 | tf_op jit(solution)/shard_map/ppermute | solution.py:482
  142.4 13.1 %collective-permute-start.32 = (bf16[4,32,768]{2,1,0:T(8,128)(2,1)S(1)}, bf16[4,32,768]{2,1,0:T(8,128)(2,1)S(1)}, u32[]{:S(2)}, u32[]{:S(2)}) collective-permute-start(bf16[4,32,768]{2,1,0:T(8,128)(2,1)S(1)} %line_place.1.refs_0_), channel_id=1, source_target_pairs={{0,24},{4,28},{8,16},{12,20},{16,8},{20,12},{24,0},{28,4},{1,25},{... | collective-permute-start | bytes 589832 | tf_op jit(solution)/shard_map/ppermute | solution.py:482
  145.3 1.6 copy-start.20
  155.6 2.4 %collective-permute-start.33 = (bf16[4,4,32,768]{3,2,1,0:T(8,128)(2,1)S(1)}, bf16[4,4,32,768]{3,2,1,0:T(8,128)(2,1)S(1)}, u32[]{:S(2)}, u32[]{:S(2)}) collective-permute-start(bf16[4,4,32,768]{3,2,1,0:T(8,128)(2,1)S(1)} %plane_place.1.mine_ref), channel_id=1, source_target_pairs={{0,4},{4,0},{8,12},{12,8},{16,20},{20,16},{24,28},{28,24},{1,5},{5... | collective-permute-start | bytes 2359304 | tf_op jit(solution)/shard_map/ppermute | solution.py:495
